TPU v7x, 512 devices: a whole 4x4x16 slice. The times are simulated.
512 devices in a mesh: lon: 32 (over x_lo, z), lat: 8 (over y, core), mem: 2 (over x_hi).
Axes of the slice: x: 4 (x_hi: 2, x_lo: 2; x = x_hi * 2 + x_lo), y: 4, z: 16, core: 2. Of those that a mesh axis runs over, the one named last changes fastest.
Arguments:
- states: bfloat16 [2, 4, 48, 73728], P('mem', None, 'lat', 'lon'), may hold values from -6 to 6
- cotangent: bfloat16 [2, 4, 48, 73728], P('mem', None, 'lat', 'lon'), may hold values from -6 to 6
- region: int32 [48, 4], P('lat'), may hold values from 0 to 2
- pos_index: int32 [144, 144], replicated, may hold values from 0 to 3311
- w_qkv: bfloat16 [192, 576], replicated, may hold values from -0.4375 to 0.4375
- w_proj: bfloat16 [192, 192], replicated, may hold values from -0.4375 to 0.4375
- w_up: bfloat16 [192, 768], replicated, may hold values from -0.4375 to 0.4375
- w_down: bfloat16 [768, 192], replicated, may hold values from -0.21875 to 0.21875
- gains: float32 [2, 192], replicated, may hold values from 0.1 to 1.9
- earth_bias: float32 [8, 6, 3312], P('lat'), may hold values from -4 to 4
Outputs:
- grad_states: bfloat16 [2, 4, 48, 73728], P('mem', None, 'lat', 'lon')
- grad_qkv: float32 [192, 576], replicated
- grad_proj: float32 [192, 192], replicated
- grad_up: float32 [192, 768], replicated
- grad_down: float32 [768, 192], replicated
- grad_gains: float32 [2, 192], replicated
- grad_bias: float32 [8, 6, 3312], P('lat')
All inputs are finite; a program needn't handle non-finite values.
Results may differ from a plain program's by a relative error of at most 0.02.
Values may be sent and summed in bfloat16 or wider, within the bound.
No kernel may reach another device: no remote copies, remote signals or barrier semaphores. Data moves between devices by JAX's collectives and lax.ppermute only.
A program may use at most 64 MiB of HBM per device.

v0:
```python
import jax
import jax.numpy as jnp
from jax import lax
from jax.sharding import PartitionSpec as P

HEADS = 6
WIN_PL = 2
WIN_LAT = 6
WIN_LON = 12


EPS = 1e-05


def passed_along(block, axis, distance):
    devices = range(lax.axis_size(axis))
    route = [((i - distance) % len(devices), i) for i in devices]
    return lax.ppermute(block, axis, route)


def windows(block):
    levels, rows, cols, depth = block.shape
    shaped = block.reshape(
        levels // WIN_PL, WIN_PL, rows // WIN_LAT, WIN_LAT, cols // WIN_LON, WIN_LON, depth
    )
    shaped = shaped.transpose(0, 2, 4, 1, 3, 5, 6)
    return shaped.reshape(-1, WIN_PL * WIN_LAT * WIN_LON, depth)


def unwindows(tiles, levels, rows, cols):
    depth = tiles.shape[-1]
    shaped = tiles.reshape(
        levels // WIN_PL, rows // WIN_LAT, cols // WIN_LON, WIN_PL, WIN_LAT, WIN_LON, depth
    )
    shaped = shaped.transpose(0, 3, 1, 4, 2, 5, 6)
    return shaped.reshape(levels, rows, cols, depth)


def layer_norm(source, gain):
    centre = source - jnp.mean(source, axis=-1, keepdims=True)
    recip = lax.rsqrt(jnp.mean(centre * centre, axis=-1, keepdims=True) + EPS)
    normed = centre * recip
    return (normed, recip, normed * gain)


def norm_back(upper, normed, recip, gain):
    lowered = upper * gain
    return recip * (
        lowered
        - jnp.mean(lowered, axis=-1, keepdims=True)
        - normed * jnp.mean(lowered * normed, axis=-1, keepdims=True)
    )


def gelu_parts(upward):
    cumulative = 0.5 * (1.0 + lax.erf(upward * 0.7071067811865476))
    density = jnp.exp(-0.5 * upward * upward) * 0.3989422804014327
    return (upward * cumulative, cumulative + upward * density)


def product(form, left, right):
    return jnp.einsum(form, left, right, preferred_element_type=jnp.float32)


def matmul(left, right):
    return jnp.dot(left, right, preferred_element_type=jnp.float32)


def block_grads(states, cotan, labels, table, pos_index, w_qkv, w_proj, w_up, w_down, gains):
    levels, rows, cols, width = states.shape
    head_size = width // HEADS
    scale = head_size ** (-0.5)
    span = WIN_PL * WIN_LAT * WIN_LON
    flat_in = windows(states).reshape(-1, width)
    count = flat_in.shape[0]
    nwin = count // span
    groups = (levels // WIN_PL, rows // WIN_LAT, cols // WIN_LON)
    label_grid = jnp.broadcast_to(labels.T[:, :, None, None], (levels, rows, cols, 1))
    win_labels = windows(label_grid)[..., 0]
    same = win_labels[:, :, None] == win_labels[:, None, :]
    normed_one, recip_one, scaled_one = layer_norm(flat_in.astype(jnp.float32), gains[0])
    hidden_one = scaled_one.astype(jnp.bfloat16)
    triple = matmul(hidden_one, w_qkv).astype(jnp.bfloat16).reshape(nwin, span, 3, HEADS, head_size)
    query = triple[:, :, 0]
    keys = triple[:, :, 1]
    values_h = triple[:, :, 2]
    earth = jnp.take(table, pos_index, axis=2)
    scores = product("wqhd,wkhd->whqk", query, keys) * scale
    scores = (scores.reshape(groups + (HEADS, span, span)) + earth[None, :, None]).reshape(
        nwin, HEADS, span, span
    )
    expo = jnp.where(same[:, None], jnp.exp(scores), 0.0)
    probs = expo / jnp.sum(expo, axis=-1, keepdims=True)
    probs_low = probs.astype(jnp.bfloat16)
    attended = (
        product("whqk,wkhd->wqhd", probs_low, values_h).astype(jnp.bfloat16).reshape(count, width)
    )
    mixed = flat_in.astype(jnp.float32) + matmul(attended, w_proj)
    resid = mixed.astype(jnp.bfloat16)
    normed_two, recip_two, scaled_two = layer_norm(resid.astype(jnp.float32), gains[1])
    hidden_two = scaled_two.astype(jnp.bfloat16)
    upward = matmul(hidden_two, w_up)
    acted, slope = gelu_parts(upward)
    acted_low = acted.astype(jnp.bfloat16)
    grad_out = windows(cotan).reshape(count, width)
    grad_down = matmul(acted_low.T, grad_out)
    grad_act = (matmul(grad_out, w_down.T) * slope).astype(jnp.bfloat16)
    grad_up = matmul(hidden_two.T, grad_act)
    grad_hid_two = matmul(grad_act, w_up.T)
    gain_two = jnp.sum(grad_hid_two * normed_two, axis=0)
    grad_resid = (
        grad_out.astype(jnp.float32) + norm_back(grad_hid_two, normed_two, recip_two, gains[1])
    ).astype(jnp.bfloat16)
    grad_proj = matmul(attended.T, grad_resid)
    grad_att = (
        matmul(grad_resid, w_proj.T).astype(jnp.bfloat16).reshape(nwin, span, HEADS, head_size)
    )
    grad_prob = product("wqhd,wkhd->whqk", grad_att, values_h)
    grad_score = probs * (grad_prob - jnp.sum(probs * grad_prob, axis=-1, keepdims=True))
    per_type = jnp.sum(grad_score.reshape(groups + (HEADS, span, span)), axis=(0, 2))
    spread = per_type.reshape(groups[1] * HEADS, span * span).T
    grad_table = jax.ops.segment_sum(
        spread, pos_index.reshape(-1), num_segments=table.shape[2]
    ).T.reshape(groups[1], HEADS, table.shape[2])
    grad_low = (grad_score * scale).astype(jnp.bfloat16)
    grad_val = product("whqk,wqhd->wkhd", probs_low, grad_att).astype(jnp.bfloat16)
    grad_query = product("whqk,wkhd->wqhd", grad_low, keys).astype(jnp.bfloat16)
    grad_keys = product("whqk,wqhd->wkhd", grad_low, query).astype(jnp.bfloat16)
    grad_triple = jnp.stack([grad_query, grad_keys, grad_val], axis=2).reshape(count, 3 * width)
    grad_qkv = matmul(hidden_one.T, grad_triple)
    grad_hid_one = matmul(grad_triple, w_qkv.T)
    gain_one = jnp.sum(grad_hid_one * normed_one, axis=0)
    grad_in = (
        grad_resid.astype(jnp.float32) + norm_back(grad_hid_one, normed_one, recip_one, gains[0])
    ).astype(jnp.bfloat16)
    grad_block = unwindows(grad_in.reshape(nwin, span, width), levels, rows, cols)
    return (
        grad_block,
        (grad_qkv, grad_proj, grad_up, grad_down, jnp.stack([gain_one, gain_two])),
        grad_table,
    )


def body(states, cotangent, region, pos_index, w_qkv, w_proj, w_up, w_down, gains, earth_bias):
    width = w_proj.shape[0]
    members, levels, rows, merged = states.shape
    cols = merged // width
    half_lat = WIN_LAT // 2
    half_lon = WIN_LON // 2
    grid = jnp.roll(states.reshape(levels, rows, cols, width), -(WIN_PL // 2), axis=0)
    cotan = jnp.roll(cotangent.reshape(levels, rows, cols, width), -(WIN_PL // 2), axis=0)
    grid_rows, cotan_rows = passed_along((grid[:, :half_lat], cotan[:, :half_lat]), "lat", -1)
    grid = jnp.concatenate([grid[:, half_lat:], grid_rows], axis=1)
    cotan = jnp.concatenate([cotan[:, half_lat:], cotan_rows], axis=1)
    grid_cols, cotan_cols = passed_along((grid[:, :, :half_lon], cotan[:, :, :half_lon]), "lon", -1)
    grid = jnp.concatenate([grid[:, :, half_lon:], grid_cols], axis=2)
    cotan = jnp.concatenate([cotan[:, :, half_lon:], cotan_cols], axis=2)
    grad_block, grads, grad_table = block_grads(
        grid, cotan, region, earth_bias, pos_index, w_qkv, w_proj, w_up, w_down, gains
    )
    moved_cols = passed_along(grad_block[:, :, -half_lon:], "lon", 1)
    grad_block = jnp.concatenate([moved_cols, grad_block[:, :, :-half_lon]], axis=2)
    moved_rows = passed_along(grad_block[:, -half_lat:], "lat", 1)
    grad_block = jnp.concatenate([moved_rows, grad_block[:, :-half_lat]], axis=1)
    grad_block = jnp.roll(grad_block, WIN_PL // 2, axis=0)
    grad_states = grad_block.reshape(members, levels, rows, merged)
    summed = lax.psum((grads[0], grads[1], grads[2], grads[3], grads[4]), ("lon", "lat", "mem"))
    grad_bias = lax.psum(grad_table, ("lon", "mem"))
    factor = float(
        members
        * lax.axis_size("mem")
        * levels
        * rows
        * lax.axis_size("lat")
        * cols
        * lax.axis_size("lon")
    ) ** (-0.5)
    return (
        grad_states,
        summed[0] * factor,
        summed[1] * factor,
        summed[2] * factor,
        summed[3] * factor,
        summed[4] * factor,
        grad_bias,
    )


def solution(mesh):
    return jax.shard_map(
        body,
        mesh=mesh,
        in_specs=(
            P("mem", None, "lat", "lon"),
            P("mem", None, "lat", "lon"),
            P("lat", None),
            P(),
            P(),
            P(),
            P(),
            P(),
            P(),
            P("lat", None, None),
        ),
        out_specs=(P("mem", None, "lat", "lon"), P(), P(), P(), P(), P(), P("lat", None, None)),
        check_vma=False,
    )
```

profile of v0, /device:TPU:1, one launch (start us, length us, event | category | flops | bytes accessed | tf_op | source)
XLA Modules:
  0.0 996.9 jit_solution(458201664842764370)
XLA Ops:
  7.2 1.1 slice_reduce_fusion
  8.4 1.0 slice.95
  9.7 6.9 collective-permute-start.2
  16.6 1.0 slice_reduce_fusion.1
  17.6 1.0 slice.87
  20.2 38.7 %gather_fusion = f32[20736,6]{1,0:T(8,128)} fusion(f32[6,3312]{0,1:T(8,128)S(1)} %bitcast.73, s32[21504]{0:T(1024)S(1)} %pad_clamp_fusion), kind=kCustom, calls=%fused_computation | custom fusion | bytes 1078272 | tf_op jit(solution)/shard_map/jit(_take)/gather | solution.py:87
  58.8 11.6 %copy.81 = f32[144,144,6]{0,1,2:T(8,128)S(1)} copy(f32[144,144,6]{2,1,0:T(8,128)} %bitcast.74) | data formatting | bytes 995328 | tf_op jit(solution)/shard_map/jit(_take)/gather | solution.py:87
  70.5 1.0 select_bitcast_fusion
  72.3 9.1 collective-permute-start.3
  81.5 2.8 collective-permute-start.1
  85.0 1.9 collective-permute-done.1
  89.2 1.9 fusion.16
  93.0 1.2 fusion.19
  95.2 1.3 fusion.45
  96.7 0.9 fusion.55
  98.1 1.1 fusion.10
  99.2 1.7 fusion.23
  100.8 3.3 fusion.9
  104.1 3.3 fusion.8
  107.4 2.6 fusion.53
  112.0 1.2 pad_maximum_fusion
  114.6 1.1 fusion.54
  115.8 6.2 copy.93
  121.9 113.6 %scatter_custom_fusion = f32[3312,6]{1,0:T(8,128)} fusion(s32[20736]{0:T(1024)} %reshape.228, f32[20736,6]{1,0:T(8,128)} %copy.93, f32[]{:T(128)} %constant.14.clone.1), kind=kCustom, calls=%fused_computation.33 | custom fusion | flops 124416 | bytes 80000 | tf_op jit(solution)/shard_map/scatter-add | solution.py:122
  236.7 1.9 collective-permute-start.4
  238.6 104.2 %psum.46 = f32[2,192]{1,0:T(2,128)S(1)} all-reduce(f32[2,192]{1,0:T(2,128)S(1)} %pad_maximum_fusion.9), channel_id=1, replica_groups=mesh['lon'=32,'lat'=8,'mem'=2] {'lon','lat','mem'}, use_global_device_ids=true, to_apply=%region_16.17 | all-reduce | flops 384 | bytes 3072 | tf_op jit(solution)/shard_map/psum | solution.py:167
  343.8 154.9 %all-reduce.4.cloned.1.call-done = f32[1,6,3312]{1,2,0:T(8,128)} async-done(((f32[1,6,3312]{1,2,0:T(8,128)}), f32[1,6,3312]{1,2,0:T(8,128)}) %all-reduce.4.cloned.1.call-update) | async-done | bytes 79504 | tf_op jit(solution)/shard_map/psum | solution.py:168
  498.8 2.6 copy.94
  502.3 482.4 %all-reduce.6.cloned.1.call-done = (f32[192,576]{1,0:T(8,128)}, f32[192,192]{1,0:T(8,128)}, f32[192,768]{1,0:T(8,128)}, f32[768,192]{0,1:T(8,128)}) async-done(((f32[192,576]{1,0:T(8,128)}, f32[192,192]{1,0:T(8,128)}, f32[192,768]{1,0:T(8,128)}, f32[768,192]{0,1:T(8,128)}), (f32[192,576]{1,0:T(8,128)}, f32[192,192]{1,0:T(8,128)}, f32[192,768]{1,0:T(8,128)}, ...) | async-done | bytes 1769488 | tf_op jit(solution)/shard_map/psum | solution.py:167
  984.7 1.9 broadcast_multiply_fusion.2
  986.7 1.6 broadcast_multiply_fusion.3
  988.3 0.9 broadcast_multiply_fusion.1
  (120 shorter events, 16.3 us)
Async XLA Ops:
  7.2 85.4 %copy-start = (bf16[192,768]{1,0:T(8,128)(2,1)S(1)}, bf16[192,768]{1,0:T(8,128)(2,1)}, u32[]{:S(2)}) copy-start(bf16[192,768]{1,0:T(8,128)(2,1)} %param.16) | copy-start | bytes 884740
  7.2 11.7 %copy-start.3 = (s32[144,144]{1,0:T(8,128)S(1)}, s32[144,144]{1,0:T(8,128)}, u32[]{:S(2)}) copy-start(s32[144,144]{1,0:T(8,128)} %param.13) | copy-start | bytes 248836
  7.2 11.8 %copy-start.16 = (s32[6,4]{0,1:T(4,128)S(1)}, s32[6,4]{0,1:T(4,128)}, u32[]{:S(2)}) copy-start(s32[6,4]{0,1:T(4,128)} %param.12) | copy-start | bytes 292
  7.2 491.6 %all-reduce.4.cloned.1.call-start = ((), (), s32[]{:S(2)}) async-start(), calls=%async_computation | async-start | bytes 3391488 | tf_op jit(solution)/shard_map/psum | solution.py:168
  9.4 10.2 %copy-start.15 = (f32[1,6,3312]{2,0,1:T(1,128)S(1)}, f32[1,6,3312]{2,0,1:T(1,128)}, u32[]{:S(2)}) copy-start(f32[1,6,3312]{2,0,1:T(1,128)} %param.19) | copy-start | bytes 238468
  9.7 62.6 %collective-permute-start.2 = (bf16[4,3,12,192]{3,2,1,0:T(8,128)(2,1)S(1)}, bf16[4,3,12,192]{3,2,1,0:T(8,128)(2,1)S(1)}, u32[]{:S(2)}, u32[]{:S(2)}) collective-permute-start(bf16[4,3,12,192]{3,2,1,0:T(8,128)(2,1)S(1)} %get-tuple-element.53), channel_id=1, source_target_pairs={{2,0},{4,2},{6,4},{8,6},{10,8},{12,10},{14,12},{0,14},{3,1},{5,3},... | collective-permute-start | bytes 165896 | tf_op jit(solution)/shard_map/ppermute | solution.py:18
  18.9 62.5 %collective-permute-start = (bf16[4,3,12,192]{3,2,1,0:T(8,128)(2,1)S(1)}, bf16[4,3,12,192]{3,2,1,0:T(8,128)(2,1)S(1)}, u32[]{:S(2)}, u32[]{:S(2)}) collective-permute-start(bf16[4,3,12,192]{3,2,1,0:T(8,128)(2,1)S(1)} %get-tuple-element.57), channel_id=1, source_target_pairs={{2,0},{4,2},{6,4},{8,6},{10,8},{12,10},{14,12},{0,14},{3,1},{5,3},... | collective-permute-start | bytes 165896 | tf_op jit(solution)/shard_map/ppermute | solution.py:18
  70.4 1.0 copy-start.17
  71.5 15.6 %copy-start.9 = (bf16[192,576]{1,0:T(8,128)(2,1)S(1)}, bf16[192,576]{1,0:T(8,128)(2,1)}, u32[]{:S(2)}) copy-start(bf16[192,576]{1,0:T(8,128)(2,1)} %param.14) | copy-start | bytes 663556
  72.3 12.0 %collective-permute-start.3 = (bf16[4,6,6,192]{3,2,1,0:T(8,128)(2,1)S(1)}, bf16[4,6,6,192]{3,2,1,0:T(8,128)(2,1)S(1)}, u32[]{:S(2)}, u32[]{:S(2)}) collective-permute-start(bf16[4,6,6,192]{3,2,1,0:T(8,128)(2,1)S(1)} %get-tuple-element.51), channel_id=1, source_target_pairs={{16,0},{32,16},{48,32},{64,48},{80,64},{96,80},{112,96},{128,112},... | collective-permute-start | bytes 165896 | tf_op jit(solution)/shard_map/ppermute | solution.py:18
  81.5 5.4 collective-permute-start.1
  84.3 3.4 copy-start.1
  88.5 0.7 copy-start.13
  88.5 2.6 copy-start.11
  91.1 0.9 copy-start.8
  92.3 1.8 copy-start.18
  98.1 2.8 copy-start.14
  99.2 5.0 copy-start.12
  107.4 2.6 copy-start.2
  110.2 1.8 copy-start.4
  112.0 2.2 copy-start.10
  113.2 1.5 copy-start.7
  235.6 749.1 %all-reduce.6.cloned.1.call-start = ((), (), s32[]{:S(2)}) async-start(), calls=%async_computation.1 | async-start | bytes 3735552 | tf_op jit(solution)/shard_map/psum | solution.py:167
  236.7 106.1 %collective-permute-start.4 = (bf16[4,6,6,192]{3,2,1,0:T(8,128)(2,1)S(1)}, bf16[4,6,6,192]{3,2,1,0:T(8,128)(2,1)S(1)}, u32[]{:S(2)}, u32[]{:S(2)}) collective-permute-start(bf16[4,6,6,192]{3,2,1,0:T(8,128)(2,1)S(1)} %get-tuple-element.49), channel_id=1, source_target_pairs={{496,0},{0,16},{16,32},{32,48},{48,64},{64,80},{80,96},{96,112},{1... | collective-permute-start | bytes 165896 | tf_op jit(solution)/shard_map/ppermute | solution.py:18
  342.8 158.5 %collective-permute-start.5 = (bf16[4,3,12,192]{3,2,1,0:T(8,128)(2,1)S(1)}, bf16[4,3,12,192]{3,2,1,0:T(8,128)(2,1)S(1)}, u32[]{:S(2)}, u32[]{:S(2)}) collective-permute-start(bf16[4,3,12,192]{3,2,1,0:T(8,128)(2,1)S(1)} %fusion.37), channel_id=1, source_target_pairs={{14,0},{0,2},{2,4},{4,6},{6,8},{8,10},{10,12},{12,14},{15,1},{1,3}... | collective-permute-start | bytes 165896 | tf_op jit(solution)/shard_map/ppermute | solution.py:18
  984.7 3.6 copy-start.6
  984.7 4.4 copy-start.5
Sparse Core Ops, SparseCore 0:
  235.7 262.9 all-reduce.3
  505.1 479.5 all-reduce.5
where the time goes:
time: 998 us; the launch traced here: 997 us
  waiting for transfers between devices  640 us (64%)
  other arithmetic  126 us (13%)
  blocking collectives  104 us (10%)
  local copies, waits for them, and re-layouts  71.9 us (7%)
  starting transfers between devices  21.3 us (2%)
  matrix products  18.7 us (2%)
  between operations  14.7 us (1%)
    psum x1, waiting for transfers between devices, body(): lax.psum((grads[0], grads[1], grads[2], grads[3], grads[4]), ('lon', 'lat...  482 us
    psum x1, waiting for transfers between devices, body(): grad_bias = lax.psum(grad_table, ('lon', 'mem'))  155 us
    scatter-add x1, other arithmetic, block_grads(): jax.ops.segment_sum(spread, pos_index.reshape(-1), num_segments=table.sha...  114 us
    psum x1, blocking collectives, body(): lax.psum((grads[0], grads[1], grads[2], grads[3], grads[4]), ('lon', 'lat...  104 us
    gather x2, local copies, waits for them, and re-layouts, block_grads(): earth = jnp.take(table, pos_index, axis=2)  50.3 us
    ppermute x6, starting transfers between devices, passed_along(): return lax.ppermute(block, axis, route)  21.2 us
  transfers between devices with their start and end apart: 8, of which 3 were waited for; matrix products, arithmetic and copies ran while one was open for 6% of the time, Pallas kernels for 0%

commit v1 on v0

v1 whole, which is shorter than its diff:
```python
import jax
import jax.numpy as jnp
from jax import lax
from jax.experimental import pallas as pl
from jax.experimental.pallas import tpu as pltpu
from jax.sharding import Mesh
from jax.sharding import PartitionSpec as P

HEADS = 6
SIZE = 32
WIDTH = 192
WIN = 144
CELLS = 288
WIN_PL = 2
WIN_LAT = 6
WIN_LON = 12
BIAS_POS = 3312
CHUNKS = 26
LANES = 128
EPS = 1e-05
X, Y, Z = 4, 4, 16
XY = X * Y
HALF = 1792
PIECE = HALF // XY
BIAS_PIECE = HEADS * 32 // XY
ALL = ("x", "z", "y", "c", "m")
PLANE = ("x", "m", "y")
BF = jnp.bfloat16
F32 = jnp.float32


def nn(left, right):
    return lax.dot_general(left, right, (((1,), (0,)), ((), ())), preferred_element_type=F32)


def nt(left, right):
    return lax.dot_general(left, right, (((1,), (1,)), ((), ())), preferred_element_type=F32)


def tn(left, right):
    return lax.dot_general(left, right, (((0,), (0,)), ((), ())), preferred_element_type=F32)


def layer_norm(source, gain):
    centre = source - jnp.mean(source, axis=-1, keepdims=True)
    recip = lax.rsqrt(jnp.mean(centre * centre, axis=-1, keepdims=True) + EPS)
    normed = centre * recip
    return (normed, recip, normed * gain)


def norm_back(upper, normed, recip, gain):
    lowered = upper * gain
    return recip * (
        lowered
        - jnp.mean(lowered, axis=-1, keepdims=True)
        - normed * jnp.mean(lowered * normed, axis=-1, keepdims=True)
    )


def gelu_parts(upward):
    cumulative = 0.5 * (1.0 + lax.erf(upward * 0.7071067811865476))
    density = jnp.exp(-0.5 * upward * upward) * 0.3989422804014327
    return (upward * cumulative, cumulative + upward * density)


def bias_kernel(pos_ref, table_ref, earth_ref):
    def eight_rows(r, carry):
        rows = pl.ds(pl.multiple_of(r * 8, 8), 8)
        for start, width in ((0, LANES), (LANES, WIN - LANES)):
            place = pos_ref[rows, start : start + LANES]
            low = place & (LANES - 1)
            high = place >> 7
            found = [jnp.zeros((8, LANES), F32) for _ in range(HEADS)]
            for c in range(CHUNKS):
                here = high == c
                for h in range(HEADS):
                    at = h * CHUNKS + c
                    row = jnp.broadcast_to(table_ref[at : at + 1, :], (8, LANES))
                    taken = jnp.take_along_axis(row, low, axis=1, mode="promise_in_bounds")
                    found[h] = jnp.where(here, taken, found[h])
            for h in range(HEADS):
                earth_ref[h, rows, start : start + width] = found[h][:, :width]
        return carry

    lax.fori_loop(0, WIN // 8, eight_rows, 0)


def scatter_kernel(pos_ref, score_ref, table_ref, place_ref, rest_ref):
    which = lax.broadcasted_iota(jnp.int32, (LANES, LANES), 0)
    chunk = lax.broadcasted_iota(jnp.int32, (32, LANES), 0)
    tail = WIN - LANES

    def product(places, scores):
        left, right = [], []
        for n in range(8):
            place = places[n : n + 1]
            right.append(jnp.where(which == (place & (LANES - 1)), 1.0, 0.0).astype(BF))
            here = chunk == (place >> 7)
            parts = [jnp.where(here, score[n : n + 1], 0.0).astype(BF) for score in scores]
            left.append(jnp.concatenate(parts, axis=0))
        return nt(jnp.concatenate(left, axis=1), jnp.concatenate(right, axis=1))

    place_ref[...] = jnp.zeros_like(place_ref)
    rest_ref[...] = jnp.zeros_like(rest_ref)
    place_ref[:, :WIN] = pos_ref[:, LANES:].T
    for h in range(HEADS):
        rest_ref[h, :, :WIN] = score_ref[h, :, LANES:].T
    total = jnp.zeros((HEADS * 32, LANES), F32)
    for k in range(2):
        for at in range(0, tail, 8):
            lanes = slice(k * LANES, (k + 1) * LANES)
            total += product(
                place_ref[at : at + 8, lanes], [rest_ref[h, at : at + 8, lanes] for h in range(HEADS)]
            )
    table_ref[...] = total

    def eight_rows(r, carry):
        rows = pl.ds(pl.multiple_of(r * 8, 8), 8)
        table_ref[...] += product(
            pos_ref[rows, :LANES], [score_ref[h, rows, :LANES] for h in range(HEADS)]
        )
        return carry

    lax.fori_loop(0, WIN // 8, eight_rows, 0, unroll=2)


def block_kernel(
    region_ref, core_ref, x_ref, g_ref, earth_ref, qkv_ref, proj_ref, up_ref, down_ref, gains_ref,
    grad_ref, send_ref, keep_ref, score_ref, triple_ref, wide_ref, gain_ref,
):
    scale = SIZE ** (-0.5)
    x = x_ref[...].astype(F32)
    g_low = g_ref[...]
    gain_a, gain_b = gains_ref[0:1, :], gains_ref[1:2, :]
    normed_one, recip_one, scaled_one = layer_norm(x, gain_a)
    hidden_one = scaled_one.astype(BF)
    triple = nn(hidden_one, qkv_ref[...]).astype(BF)
    head_of = lax.broadcasted_iota(jnp.int32, (1, WIDTH), 1) // SIZE
    masks = [(head_of == h) for h in range(HEADS)]

    def stacked(part):
        return jnp.concatenate([jnp.where(m, part, jnp.zeros_like(part)) for m in masks], axis=0)

    def joined(full):
        full = full.reshape(HEADS, WIN, WIDTH)
        total = jnp.where(masks[0], full[0], 0.0)
        for h in range(1, HEADS):
            total = jnp.where(masks[h], full[h], total)
        return total

    kept = []
    earth = earth_ref[...]
    group_row = lax.broadcasted_iota(jnp.int32, (1, WIN), 1) // WIN_LON
    group_col = lax.broadcasted_iota(jnp.int32, (WIN, 1), 0) // WIN_LON
    attended = []
    for w in range(2):
        rows = slice(w * WIN, (w + 1) * WIN)
        part = triple[rows]
        query, keys, vals = part[:, :WIDTH], part[:, WIDTH : 2 * WIDTH], part[:, 2 * WIDTH :]
        label_row = jnp.zeros((1, WIN), jnp.int32)
        label_col = jnp.zeros((WIN, 1), jnp.int32)
        for group in range(WIN_PL * WIN_LAT):
            label = region_ref[group % WIN_LAT, w * WIN_PL + group // WIN_LAT]
            label_row = jnp.where(group_row == group, label, label_row)
            label_col = jnp.where(group_col == group, label, label_col)
        same = label_row == label_col
        q_stack = stacked(query)
        scores = nt(q_stack, keys).reshape(HEADS, WIN, WIN) * scale + earth
        expo = jnp.where(same[None], jnp.exp(scores), 0.0)
        probs = expo / jnp.sum(expo, axis=-1, keepdims=True)
        probs_low = probs.astype(BF).reshape(HEADS * WIN, WIN)
        attended.append(joined(nn(probs_low, vals)).astype(BF))
        kept.append((q_stack, keys, vals, probs, probs_low))
    attended = jnp.concatenate(attended, axis=0)

    resid = (x + nn(attended, proj_ref[...])).astype(BF)
    normed_two, recip_two, scaled_two = layer_norm(resid.astype(F32), gain_b)
    hidden_two = scaled_two.astype(BF)
    acted, slope = gelu_parts(nn(hidden_two, up_ref[...]))
    acted_low = acted.astype(BF)
    down = tn(g_low, acted_low)
    grad_act = (nn(g_low, down_ref[...]) * slope).astype(BF)
    up = tn(hidden_two, grad_act)
    grad_hid_two = nt(grad_act, up_ref[...])
    gain_ref[...] = jnp.zeros_like(gain_ref)
    gain = jnp.sum(grad_hid_two * normed_two, axis=0, keepdims=True)
    gain_ref[2:3, :] = gain[:, :LANES]
    gain_ref[3:4, : WIDTH - LANES] = gain[:, LANES:]
    grad_resid = (
        g_low.astype(F32) + norm_back(grad_hid_two, normed_two, recip_two, gain_b)
    ).astype(BF)
    wide_ref[:, 3 * WIDTH :] = tn(attended, grad_resid)
    grad_att = nt(grad_resid, proj_ref[...]).astype(BF)
    total = None
    for w in range(2):
        rows = slice(w * WIN, (w + 1) * WIN)
        q_stack, keys, vals, probs, probs_low = kept[w]
        a_stack = stacked(grad_att[rows])
        grad_prob = nt(a_stack, vals).reshape(HEADS, WIN, WIN)
        grad_score = probs * (grad_prob - jnp.sum(probs * grad_prob, axis=-1, keepdims=True))
        total = grad_score if total is None else total + grad_score
        grad_low = (grad_score * scale).astype(BF).reshape(HEADS * WIN, WIN)
        triple_ref[rows, :WIDTH] = joined(nn(grad_low, keys)).astype(BF)
        triple_ref[rows, WIDTH : 2 * WIDTH] = tn(grad_low, q_stack).astype(BF)
        triple_ref[rows, 2 * WIDTH :] = tn(probs_low, a_stack).astype(BF)
    score_ref[...] = total
    grad_triple = triple_ref[...]
    wide_ref[:, : 3 * WIDTH] = tn(hidden_one, grad_triple)
    grad_hid_one = nt(grad_triple, qkv_ref[...])
    gain = jnp.sum(grad_hid_one * normed_one, axis=0, keepdims=True)
    gain_ref[0:1, :] = gain[:, :LANES]
    gain_ref[1:2, : WIDTH - LANES] = gain[:, LANES:]
    grad_ref[...] = (
        grad_resid.astype(F32) + norm_back(grad_hid_one, normed_one, recip_one, gain_a)
    ).astype(BF)
    lines = {}
    for part, whole in enumerate((wide_ref[...], up, down)):
        for k in range(6):
            lines[part * 6 + k] = whole[:, k * LANES : (k + 1) * LANES].astype(BF)
    extra = [jnp.zeros((HALF - 9 * WIDTH, LANES), BF), gain_ref[...].astype(BF)]

    def put(ref, half):
        for k in range(9):
            ref[k * WIDTH : (k + 1) * WIDTH, :] = lines[half * 9 + k]
        ref[9 * WIDTH :, :] = extra[half]

    core = core_ref[0]
    for mine in range(2):

        @pl.when(core == mine)
        def _():
            put(keep_ref, mine)
            put(send_ref, 1 - mine)


def first_sum_kernel(keep_ref, came_ref, table_ref, out_ref, pad_ref):
    pad_ref[...] = jnp.zeros_like(pad_ref)
    for p in range(XY):
        rows = slice(p * PIECE, (p + 1) * PIECE)
        out_ref[p, :PIECE, :] = (keep_ref[rows, :].astype(F32) + came_ref[rows, :].astype(F32)).astype(BF)
        pad_ref[p, :BIAS_PIECE, :] = table_ref[p * BIAS_PIECE : (p + 1) * BIAS_PIECE, :]
        out_ref[p, PIECE:, :] = pad_ref[p].astype(BF)


def second_sum_kernel(came_ref, out_ref, terms_ref, table_ref, pad_ref):
    came = came_ref[...].astype(F32)
    terms_ref[...] = jnp.sum(came[:, :PIECE], axis=0)
    for y in range(Y):
        part = came[y, PIECE:]
        for x in range(1, X):
            part = part + came[x * Y + y, PIECE:]
        table_ref[y * BIAS_PIECE : (y + 1) * BIAS_PIECE, :] = part[:BIAS_PIECE]
    pad_ref[...] = jnp.zeros_like(pad_ref)
    few, less = PIECE // Z, Y * BIAS_PIECE // Z
    for z in range(Z):
        pad_ref[z, :few, :] = terms_ref[z * few : (z + 1) * few, :]
        pad_ref[z, 8 : 8 + less, :] = table_ref[z * less : (z + 1) * less, :]
    out_ref[...] = pad_ref[...].astype(BF)


def third_sum_kernel(came_ref, out_ref):
    total = jnp.sum(came_ref[...].astype(F32), axis=0).astype(BF)
    for z in range(Z):
        out_ref[z] = total


def fan_kernel(came_ref, out_ref, came_wide_ref, terms_ref, table_ref):
    came_wide_ref[...] = came_ref[...].astype(F32)
    table_ref[...] = jnp.zeros_like(table_ref)
    few, less = PIECE // Z, Y * BIAS_PIECE // Z
    for z in range(Z):
        terms_ref[z * few : (z + 1) * few, :] = came_wide_ref[z, :few, :]
        y, at = z * less // BIAS_PIECE, z * less % BIAS_PIECE
        table_ref[y, at : at + less, :] = came_wide_ref[z, 8 : 8 + less, :]
    terms = terms_ref[...].astype(BF)
    for p in range(XY):
        out_ref[p, :PIECE, :] = terms
        out_ref[p, PIECE:, :] = table_ref[p % Y].astype(BF)


def finish_kernel(
    factor, both_ref, mine_ref, qkv_ref, proj_ref, up_ref, down_ref, gains_ref, bias_ref, flat_ref, wide_ref,
):
    for half in range(2):
        for p in range(XY):
            flat_ref[half, p * PIECE : (p + 1) * PIECE, :] = both_ref[half, p, :PIECE, :]

    def block(k):
        rows = slice(k % 9 * WIDTH, (k % 9 + 1) * WIDTH)
        return flat_ref[k // 9, rows, :].astype(F32) * factor

    for k in range(6):
        lanes = slice(k * LANES, (k + 1) * LANES)
        wide_ref[:, lanes] = block(k)
        up_ref[:, lanes] = block(6 + k)
        down_ref[:, lanes] = block(12 + k)
    qkv_ref[...] = wide_ref[:, : 3 * WIDTH]
    proj_ref[...] = wide_ref[:, 3 * WIDTH :]
    gains = flat_ref[1, 9 * WIDTH :, :].astype(F32) * factor
    for n in range(2):
        gains_ref[n : n + 1, :LANES] = gains[2 * n : 2 * n + 1]
        gains_ref[n : n + 1, LANES:] = gains[2 * n + 1 : 2 * n + 2, : WIDTH - LANES]
    for p in range(XY):
        piece = mine_ref[p, PIECE:, :].astype(F32)
        for r in range(BIAS_PIECE):
            h, c = divmod(p * BIAS_PIECE + r, 32)
            width = min(LANES, BIAS_POS - c * LANES)
            if width > 0:
                bias_ref[h : h + 1, c * LANES : c * LANES + width] = piece[r : r + 1, :width]


VMEM = pl.BlockSpec(memory_space=pltpu.VMEM)
SMEM = pl.BlockSpec(memory_space=pltpu.SMEM)


def kernel(function, name, outs, scratch=(), scalars=0, flops=1_000_000, moved=1_000_000):
    shapes = tuple(jax.ShapeDtypeStruct(s, t) for s, t in outs)

    def call(*args):
        return pl.pallas_call(
            function,
            out_shape=shapes,
            in_specs=[SMEM] * scalars + [VMEM] * (len(args) - scalars),
            out_specs=(VMEM,) * len(shapes),
            scratch_shapes=[pltpu.VMEM(s, t) for s, t in scratch],
            compiler_params=pltpu.CompilerParams(vmem_limit_bytes=48 * 1024 * 1024),
            cost_estimate=pl.CostEstimate(flops=flops, bytes_accessed=moved, transcendentals=0),
            name=name,
        )(*args)

    return call


find_bias = kernel(bias_kernel, "find_bias", [((HEADS, WIN, WIN), F32)], flops=20_000_000)
spread_bias = kernel(
    scatter_kernel,
    "spread_bias",
    [((HEADS * 32, LANES), F32)],
    [((WIN - LANES, 2 * LANES), jnp.int32), ((HEADS, WIN - LANES, 2 * LANES), F32)],
    flops=1_000_000_000,
)
block_grads = kernel(
    block_kernel,
    "block_grads",
    [((CELLS, WIDTH), BF), ((HALF, LANES), BF), ((HALF, LANES), BF), ((HEADS, WIN, WIN), F32)],
    [((CELLS, 3 * WIDTH), BF), ((WIDTH, 4 * WIDTH), F32), ((HALF - 9 * WIDTH, LANES), F32)],
    scalars=2,
    flops=1_000_000_000,
    moved=4_000_000,
)
first_sum = kernel(first_sum_kernel, "first_sum", [((XY, LANES, LANES), BF)], [((XY, 16, LANES), F32)])
second_sum = kernel(
    second_sum_kernel,
    "second_sum",
    [((Z, 16, LANES), BF)],
    [((PIECE, LANES), F32), ((Y * BIAS_PIECE, LANES), F32), ((Z, 16, LANES), F32)],
)
third_sum = kernel(third_sum_kernel, "third_sum", [((Z, 16, LANES), BF)])
fan = kernel(
    fan_kernel,
    "fan",
    [((XY, LANES, LANES), BF)],
    [((Z, 16, LANES), F32), ((PIECE, LANES), F32), ((Y, 16, LANES), F32)],
)


def finish(factor, both, mine):
    return kernel(
        lambda *refs: finish_kernel(factor, *refs),
        "finish",
        [
            ((WIDTH, 3 * WIDTH), F32),
            ((WIDTH, WIDTH), F32),
            ((WIDTH, 4 * WIDTH), F32),
            ((WIDTH, 4 * WIDTH), F32),
            ((2, WIDTH), F32),
            ((HEADS, BIAS_POS), F32),
        ],
        [((2, HALF, LANES), BF), ((WIDTH, 4 * WIDTH), F32)],
    )(both, mine)


def routes(lon_step, lat_step):
    lon, lat, mem = 2 * Z, 2 * Y, 2
    return [
        ((a * lat + b) * mem + c, ((a + lon_step) % lon * lat + (b + lat_step) % lat) * mem + c)
        for a in range(lon)
        for b in range(lat)
        for c in range(mem)
    ]


def shifted(pair):
    half_rows, half_cols = pair.shape[2] // 2, pair.shape[3] // 2
    pair = jnp.roll(pair, -1, axis=1)
    own, east = pair[:, :, half_rows:, half_cols:], pair[:, :, half_rows:, :half_cols]
    south, corner = pair[:, :, :half_rows, half_cols:], pair[:, :, :half_rows, :half_cols]
    corner = lax.ppermute(corner, ALL, routes(-1, -1))
    east = lax.ppermute(east, ALL, routes(-1, 0))
    south = lax.ppermute(south, ALL, routes(0, -1))
    top = jnp.concatenate([own, east], axis=3)
    bottom = jnp.concatenate([south, corner], axis=3)
    return jnp.concatenate([top, bottom], axis=2)


def unshifted(grad):
    half_rows, half_cols = grad.shape[1] // 2, grad.shape[2] // 2
    grad = jnp.roll(grad, 1, axis=0)
    own, east = grad[:, :half_rows, :half_cols], grad[:, :half_rows, half_cols:]
    south, corner = grad[:, half_rows:, :half_cols], grad[:, half_rows:, half_cols:]
    corner = lax.ppermute(corner, ALL, routes(1, 1))
    east = lax.ppermute(east, ALL, routes(1, 0))
    south = lax.ppermute(south, ALL, routes(0, 1))
    top = jnp.concatenate([corner, south], axis=2)
    bottom = jnp.concatenate([east, own], axis=2)
    return jnp.concatenate([top, bottom], axis=1)


def body(states, cotangent, region, pos_index, w_qkv, w_proj, w_up, w_down, gains, earth_bias):
    levels, rows, merged = states.shape[1:]
    place = jnp.pad(pos_index, ((0, 0), (0, 2 * LANES - WIN)))
    table = jnp.pad(earth_bias[0], ((0, 0), (0, CHUNKS * LANES - BIAS_POS)))
    (earth,) = find_bias(place, table.reshape(HEADS * CHUNKS, LANES))
    pair = shifted(jnp.concatenate([states, cotangent], axis=0))
    cells = pair.reshape(2, CELLS, WIDTH)
    core = lax.axis_index("c").astype(jnp.int32).reshape(1)
    grad, send, keep, score = block_grads(
        region, core, cells[0], cells[1], earth, w_qkv, w_proj, w_up, w_down.T, gains
    )
    came = lax.ppermute(send, "c", [(0, 1), (1, 0)])
    grad_states = unshifted(grad.reshape(levels, rows, merged))[None]
    (spread,) = spread_bias(pos_index, score)
    (plane,) = first_sum(keep, came, spread)
    plane = lax.all_to_all(plane, PLANE, 0, 0)
    (line,) = second_sum(plane)
    line = lax.all_to_all(line, "z", 0, 0)
    (line,) = third_sum(line)
    line = lax.all_to_all(line, "z", 0, 0)
    (plane,) = fan(line)
    plane = lax.all_to_all(plane, PLANE, 0, 0)
    both = lax.all_gather(plane, "c")
    factor = float(CELLS * lax.axis_size(ALL)) ** (-0.5)
    grad_qkv, grad_proj, grad_up, grad_down, grad_gains, grad_bias = finish(factor, both, plane)
    return (grad_states, grad_qkv, grad_proj, grad_up, grad_down.T, grad_gains, grad_bias[None])


def solution(mesh):
    fine = Mesh(mesh.devices.reshape(2, Z, Y, 2, 2), ALL)
    lon, lat = ("x", "z"), ("y", "c")
    return jax.shard_map(
        body,
        mesh=fine,
        in_specs=(
            P("m", None, lat, lon),
            P("m", None, lat, lon),
            P(lat, None),
            P(),
            P(),
            P(),
            P(),
            P(),
            P(),
            P(lat, None, None),
        ),
        out_specs=(P("m", None, lat, lon), P(), P(), P(), P(), P(), P(lat, None, None)),
        check_vma=False,
    )
```

time: 998 us -> 137 us (0.14)
  waiting for transfers between devices: 640 us -> 13.5 us
  other arithmetic: 126 us -> 0.41 us
  local copies, waits for them, and re-layouts: 71.9 us -> 8.05 us
  blocking collectives: 104 us -> 45.1 us
  Pallas kernels: 0 us -> 19.9 us
  matrix products: 18.7 us -> 0 us
  starting transfers between devices: 21.3 us -> 35 us
    psum x2 -> x0, waiting for transfers between devices: 637 us -> none  [the longest x1 482 us: body(): lax.psum((grads[0], grads[1], grads[2], grads[3], grads[4]), ('lon', 'lat...]
    scatter-add x1 -> x0, other arithmetic: 114 us -> none  [block_grads(): jax.ops.segment_sum(spread, pos_index.reshape(-1), num_segments=table.sha...]
    psum x1 -> x0, blocking collectives: 104 us -> none  [body(): lax.psum((grads[0], grads[1], grads[2], grads[3], grads[4]), ('lon', 'lat...]
    gather x2 -> x0, local copies, waits for them, and re-layouts: 50.3 us -> none  [block_grads(): earth = jnp.take(table, pos_index, axis=2)]
    all_to_all x0 -> x3, blocking collectives: none -> 45.1 us  [the longest x2 30.7 us: body(): line = lax.all_to_all(line, 'z', 0, 0)]
    pallas_call x0 -> x8, Pallas kernels: none -> 19.9 us  [call(): pl.pallas_call(function, out_shape=shapes, in_specs=[SMEM] * scalars + [V...]
    dot_general x16 -> x0, matrix products: 16.8 us -> none  [the longest x5 9.52 us: product(): return jnp.einsum(form, left, right, preferred_element_type=jnp.float32)]
    ppermute x6 -> x7, starting transfers between devices: 21.2 us -> 31.2 us  [the longest x1 12.9 us: shifted(): east = lax.ppermute(east, ALL, routes(-1, 0))]
  transfers between devices with their start and end apart: 8 -> 9, of which waited for: 3 -> 2; matrix products, arithmetic and copies ran while one was open for 6% -> 1% of each run, Pallas kernels for 0% -> 8%
where the time goes in v1:
time: 137 us; the launch traced here: 136 us
  blocking collectives  45.1 us (33%)
  starting transfers between devices  35 us (26%)
  Pallas kernels  19.9 us (15%)
  between operations  14.4 us (11%)
  waiting for transfers between devices  13.5 us (10%)
  local copies, waits for them, and re-layouts  8.05 us (6%)
    all_to_all x2, blocking collectives, body(): line = lax.all_to_all(line, 'z', 0, 0)  30.7 us
    pallas_call x8, Pallas kernels, call(): pl.pallas_call(function, out_shape=shapes, in_specs=[SMEM] * scalars + [V...  19.9 us
    all_to_all x1, blocking collectives, body(): plane = lax.all_to_all(plane, PLANE, 0, 0)  14.4 us
    ppermute x1, starting transfers between devices, shifted(): east = lax.ppermute(east, ALL, routes(-1, 0))  12.9 us
    all_to_all x1, waiting for transfers between devices, body(): plane = lax.all_to_all(plane, PLANE, 0, 0)  8.56 us
    ppermute x1, starting transfers between devices, unshifted(): corner = lax.ppermute(corner, ALL, routes(1, 1))  7.3 us
    unnamed x30, local copies, waits for them, and re-layouts  6.91 us
    ppermute x1, waiting for transfers between devices, unshifted(): east = lax.ppermute(east, ALL, routes(1, 0))  4.89 us
  transfers between devices with their start and end apart: 9, of which 2 were waited for; matrix products, arithmetic and copies ran while one was open for 1% of the time, Pallas kernels for 8%

profile of v1, /device:TPU:1, one launch (start us, length us, event | category | flops | bytes accessed | tf_op | source)
XLA Modules:
  0.0 136.3 jit_solution(12975653795706140586)
XLA Ops:
  7.2 1.0 constant_dynamic-update-slice_fusion.1
  8.4 0.2 fusion.1
  8.7 12.9 %collective-permute-start = (bf16[2,4,3,1152]{3,1,2,0:T(4,128)(2,1)S(1)}, bf16[2,4,3,1152]{3,1,2,0:T(4,128)(2,1)S(1)}, u32[]{:S(2)}, u32[]{:S(2)}) collective-permute-start(bf16[2,4,3,1152]{3,1,2,0:T(4,128)(2,1)S(1)} %get-tuple-element.49), channel_id=1, source_target_pairs={{0,496},{1,497},{2,498},{3,499},{4,500},{5,501},{6,502},{7,503},{8... | collective-permute-start | bytes 165896 | tf_op jit(solution)/shard_map/ppermute | solution.py:399
  21.6 3.5 %collective-permute-start.2 = (bf16[2,4,3,1152]{3,1,2,0:T(4,128)(2,1)S(1)}, bf16[2,4,3,1152]{3,1,2,0:T(4,128)(2,1)S(1)}, u32[]{:S(2)}, u32[]{:S(2)}) collective-permute-start(bf16[2,4,3,1152]{3,1,2,0:T(4,128)(2,1)S(1)} %get-tuple-element.50), channel_id=1, source_target_pairs={{0,510},{1,511},{2,496},{3,497},{4,498},{5,499},{6,500},{7,501},{8... | collective-permute-start | bytes 165896 | tf_op jit(solution)/shard_map/ppermute | solution.py:398
  25.1 2.0 %collective-permute-start.1 = (bf16[2,4,3,1152]{3,1,2,0:T(4,128)(2,1)S(1)}, bf16[2,4,3,1152]{3,1,2,0:T(4,128)(2,1)S(1)}, u32[]{:S(2)}, u32[]{:S(2)}) collective-permute-start(bf16[2,4,3,1152]{3,1,2,0:T(4,128)(2,1)S(1)} %get-tuple-element.51), channel_id=1, source_target_pairs={{0,14},{1,15},{2,0},{3,1},{4,2},{5,3},{6,4},{7,5},{8,6},{9,7},{10,... | collective-permute-start | bytes 165896 | tf_op jit(solution)/shard_map/ppermute | solution.py:400
  27.1 0.7 copy-done.11
  27.9 0.9 copy-done.3
  28.8 7.3 %find_bias.1.earth_ref = f32[6,144,144]{2,1,0:T(8,128)S(1)} custom-call(s32[144,256]{1,0:T(8,128)S(1)} %pad.8.pos_ref, f32[156,128]{1,0:T(8,128)S(1)} %reshape.29.table_ref), custom_call_target="tpu_custom_call" | custom-call | flops 20000000 | bytes 1000000 | tf_op jit(solution)/shard_map/find_bias/pallas_call | solution.py:320
  36.4 0.2 squeeze.10.g_ref
  36.6 0.2 squeeze.9.x_ref
  36.8 0.4 copy-done.7
  37.2 0.1 copy-done.5
  37.3 0.2 copy-done.4
  37.7 6.1 %block_grads.1 = (bf16[288,192]{1,0:T(8,128)(2,1)S(1)}, bf16[1792,128]{1,0:T(8,128)(2,1)S(1)}, bf16[1792,128]{1,0:T(8,128)(2,1)S(1)}, f32[6,144,144]{2,1,0:T(8,128)S(1)}) custom-call(s32[6,4]{1,0:T(8,128)S(1)} %copy.30.region_ref, s32[1]{0:T(128)} %bitcast.core_ref, bf16[288,192]{1,0:T(8,128)(2,1)S(1)} %squeeze.9.x_ref, bf16[288,192]{1,0:T(8,128)(2,1)S(1)} %squeeze.10.g_ref, ...), custom_call_target="tpu_custom_call" | custom-call | flops 1000000000 | bytes 4000000 | tf_op jit(solution)/shard_map/block_grads/pallas_call | solution.py:320
  43.8 3.0 %collective-permute-start.6 = (bf16[1792,128]{1,0:T(8,128)(2,1)S(1)}, bf16[1792,128]{1,0:T(8,128)(2,1)S(1)}, u32[]{:S(2)}, u32[]{:S(2)}) collective-permute-start(bf16[1792,128]{1,0:T(8,128)(2,1)S(1)} %get-tuple-element.19), channel_id=1, source_target_pairs={{0,2},{2,0},{1,3},{3,1},{4,6},{6,4},{5,7},{7,5},{8,10},{10,8},{9,1... | collective-permute-start | bytes 1376264 | tf_op jit(solution)/shard_map/ppermute | solution.py:430
  46.8 4.0 %spread_bias.1.table_ref = f32[192,128]{1,0:T(8,128)S(1)} custom-call(s32[144,144]{1,0:T(8,128)S(1)} %copy-done.3, f32[6,144,144]{2,1,0:T(8,128)S(1)} %get-tuple-element.20.score_ref), custom_call_target="tpu_custom_call" | custom-call | flops 1000000000 | bytes 1000000 | tf_op jit(solution)/shard_map/spread_bias/pallas_call | solution.py:320
  51.0 14.4 %all_to_all.20.came_ref = bf16[16,128,128]{2,1,0:T(8,128)(2,1)S(1)} all-to-all(bf16[16,128,128]{2,1,0:T(8,128)(2,1)S(1)} %first_sum.1), channel_id=1, replica_groups=mesh['x'=2,'z'=16,'y'=4,'c'=2,'m'=2] {'x','m','y'}, dimensions={0} | all-to-all | bytes 1048576 | tf_op jit(solution)/shard_map/all_to_all | solution.py:434
  65.6 16.3 %all_to_all.21.came_ref = bf16[16,16,128]{2,1,0:T(8,128)(2,1)S(1)} all-to-all(bf16[16,16,128]{2,1,0:T(8,128)(2,1)S(1)} %second_sum.1), channel_id=1, replica_groups=mesh['x'=2,'z'=16,'y'=4,'c'=2,'m'=2] {'z'}, dimensions={0} | all-to-all | bytes 131072 | tf_op jit(solution)/shard_map/all_to_all | solution.py:436
  81.9 14.4 %all_to_all.22.came_ref = bf16[16,16,128]{2,1,0:T(8,128)(2,1)S(1)} all-to-all(bf16[16,16,128]{2,1,0:T(8,128)(2,1)S(1)} %third_sum.1), channel_id=1, replica_groups=mesh['x'=2,'z'=16,'y'=4,'c'=2,'m'=2] {'z'}, dimensions={0} | all-to-all | bytes 131072 | tf_op jit(solution)/shard_map/all_to_all | solution.py:438
  96.3 0.9 fan.1
  97.1 3.8 %all-to-all-start.3 = ((bf16[16,128,128]{2,1,0:T(8,128)(2,1)}), bf16[16,128,128]{2,1,0:T(8,128)(2,1)S(1)}, u32[]{:S(2)}, u32[]{:S(2)}) async-start(bf16[16,128,128]{2,1,0:T(8,128)(2,1)} %fan.1), calls=%async_computation.3 | async-start | bytes 1048576 | tf_op jit(solution)/shard_map/all_to_all | solution.py:440
  101.0 0.2 slice.65
  101.3 8.6 %all-to-all-done.3.refs_1_ = bf16[16,128,128]{2,1,0:T(8,128)(2,1)S(1)} async-done(((bf16[16,128,128]{2,1,0:T(8,128)(2,1)}), bf16[16,128,128]{2,1,0:T(8,128)(2,1)S(1)}, u32[]{:S(2)}, u32[]{:S(2)}) %all-to-all-start.3) | async-done | bytes 524320 | tf_op jit(solution)/shard_map/all_to_all | solution.py:440
  109.8 0.8 copy-done
  110.7 7.3 %collective-permute-start.3 = (bf16[4,3,1152]{2,1,0:T(4,128)(2,1)S(1)}, bf16[4,3,1152]{2,1,0:T(4,128)(2,1)S(1)}, u32[]{:S(2)}, u32[]{:S(2)}) collective-permute-start(bf16[4,3,1152]{2,1,0:T(4,128)(2,1)S(1)} %get-tuple-element.54), channel_id=1, source_target_pairs={{0,18},{1,19},{2,20},{3,21},{4,22},{5,23},{6,24},{7,25},{8,26},{9,... | collective-permute-start | bytes 82952 | tf_op jit(solution)/shard_map/ppermute | solution.py:411
  118.0 2.4 %collective-permute-start.5 = (bf16[4,3,1152]{2,1,0:T(4,128)(2,1)S(1)}, bf16[4,3,1152]{2,1,0:T(4,128)(2,1)S(1)}, u32[]{:S(2)}, u32[]{:S(2)}) collective-permute-start(bf16[4,3,1152]{2,1,0:T(4,128)(2,1)S(1)} %get-tuple-element.56), channel_id=1, source_target_pairs={{0,16},{1,17},{2,18},{3,19},{4,20},{5,21},{6,22},{7,23},{8,24},{9,... | collective-permute-start | bytes 82952 | tf_op jit(solution)/shard_map/ppermute | solution.py:412
  120.4 0.1 collective-permute-start.4
  120.5 4.9 %collective-permute-done.5 = bf16[4,3,1152]{2,1,0:T(4,128)(2,1)S(1)} collective-permute-done((bf16[4,3,1152]{2,1,0:T(4,128)(2,1)S(1)}, bf16[4,3,1152]{2,1,0:T(4,128)(2,1)S(1)}, u32[]{:S(2)}, u32[]{:S(2)}) %collective-permute-start.5) | collective-permute-done | bytes 27680 | tf_op jit(solution)/shard_map/ppermute | solution.py:412
  125.5 0.7 copy.31
  126.2 1.2 copy-done.2
  127.4 1.3 finish.1
  128.8 0.7 copy.32
  (48 shorter events, 1.3 us)
Async XLA Ops:
  7.2 1.0 copy-start.9
  8.4 19.4 %copy-start.10 = (f32[1,6,3312]{2,0,1:T(1,128)S(1)}, f32[1,6,3312]{2,0,1:T(1,128)}, u32[]{:S(2)}) copy-start(f32[1,6,3312]{2,0,1:T(1,128)} %param.19) | copy-start | bytes 238468
  8.7 27.4 %collective-permute-start = (bf16[2,4,3,1152]{3,1,2,0:T(4,128)(2,1)S(1)}, bf16[2,4,3,1152]{3,1,2,0:T(4,128)(2,1)S(1)}, u32[]{:S(2)}, u32[]{:S(2)}) collective-permute-start(bf16[2,4,3,1152]{3,1,2,0:T(4,128)(2,1)S(1)} %get-tuple-element.49), channel_id=1, source_target_pairs={{0,496},{1,497},{2,498},{3,499},{4,500},{5,501},{6,502},{7,503},{8... | collective-permute-start | bytes 165896 | tf_op jit(solution)/shard_map/ppermute | solution.py:399
  21.6 14.5 %collective-permute-start.2 = (bf16[2,4,3,1152]{3,1,2,0:T(4,128)(2,1)S(1)}, bf16[2,4,3,1152]{3,1,2,0:T(4,128)(2,1)S(1)}, u32[]{:S(2)}, u32[]{:S(2)}) collective-permute-start(bf16[2,4,3,1152]{3,1,2,0:T(4,128)(2,1)S(1)} %get-tuple-element.50), channel_id=1, source_target_pairs={{0,510},{1,511},{2,496},{3,497},{4,498},{5,499},{6,500},{7,501},{8... | collective-permute-start | bytes 165896 | tf_op jit(solution)/shard_map/ppermute | solution.py:398
  25.1 11.1 %collective-permute-start.1 = (bf16[2,4,3,1152]{3,1,2,0:T(4,128)(2,1)S(1)}, bf16[2,4,3,1152]{3,1,2,0:T(4,128)(2,1)S(1)}, u32[]{:S(2)}, u32[]{:S(2)}) collective-permute-start(bf16[2,4,3,1152]{3,1,2,0:T(4,128)(2,1)S(1)} %get-tuple-element.51), channel_id=1, source_target_pairs={{0,14},{1,15},{2,0},{3,1},{4,2},{5,3},{6,4},{7,5},{8,6},{9,7},{10,... | collective-permute-start | bytes 165896 | tf_op jit(solution)/shard_map/ppermute | solution.py:400
  27.1 0.7 copy-start.11
  27.9 0.9 copy-start.3
  36.3 0.9 copy-start.7
  36.4 1.0 copy-start.5
  36.6 1.0 copy-start.4
  36.6 1.1 copy-start.6
  36.8 0.8 copy-start.8
  43.8 7.1 %collective-permute-start.6 = (bf16[1792,128]{1,0:T(8,128)(2,1)S(1)}, bf16[1792,128]{1,0:T(8,128)(2,1)S(1)}, u32[]{:S(2)}, u32[]{:S(2)}) collective-permute-start(bf16[1792,128]{1,0:T(8,128)(2,1)S(1)} %get-tuple-element.19), channel_id=1, source_target_pairs={{0,2},{2,0},{1,3},{3,1},{4,6},{6,4},{5,7},{7,5},{8,10},{10,8},{9,1... | collective-permute-start | bytes 1376264 | tf_op jit(solution)/shard_map/ppermute | solution.py:430
  97.1 12.7 %all-to-all-start.3 = ((bf16[16,128,128]{2,1,0:T(8,128)(2,1)}), bf16[16,128,128]{2,1,0:T(8,128)(2,1)S(1)}, u32[]{:S(2)}, u32[]{:S(2)}) async-start(bf16[16,128,128]{2,1,0:T(8,128)(2,1)} %fan.1), calls=%async_computation.3 | async-start | bytes 1048576 | tf_op jit(solution)/shard_map/all_to_all | solution.py:440
  100.9 25.3 %all-gather.3.cloned.1.call-start = ((), (), s32[]{:S(2)}) async-start(), calls=%async_computation.4 | async-start | bytes 1572864 | tf_op jit(solution)/shard_map/all_gather | solution.py:441
  109.8 0.8 copy-start
  110.6 15.6 %copy-start.1 = (bf16[16,128,128]{2,1,0:T(8,128)(2,1)S(1)}, bf16[16,128,128]{2,1,0:T(8,128)(2,1)}, u32[]{:S(2)}) copy-start(bf16[16,128,128]{2,1,0:T(8,128)(2,1)} %copy-done) | copy-start | bytes 1572868
  110.7 9.8 %collective-permute-start.3 = (bf16[4,3,1152]{2,1,0:T(4,128)(2,1)S(1)}, bf16[4,3,1152]{2,1,0:T(4,128)(2,1)S(1)}, u32[]{:S(2)}, u32[]{:S(2)}) collective-permute-start(bf16[4,3,1152]{2,1,0:T(4,128)(2,1)S(1)} %get-tuple-element.54), channel_id=1, source_target_pairs={{0,18},{1,19},{2,20},{3,21},{4,22},{5,23},{6,24},{7,25},{8,26},{9,... | collective-permute-start | bytes 82952 | tf_op jit(solution)/shard_map/ppermute | solution.py:411
  118.0 7.4 %collective-permute-start.5 = (bf16[4,3,1152]{2,1,0:T(4,128)(2,1)S(1)}, bf16[4,3,1152]{2,1,0:T(4,128)(2,1)S(1)}, u32[]{:S(2)}, u32[]{:S(2)}) collective-permute-start(bf16[4,3,1152]{2,1,0:T(4,128)(2,1)S(1)} %get-tuple-element.56), channel_id=1, source_target_pairs={{0,16},{1,17},{2,18},{3,19},{4,20},{5,21},{6,22},{7,23},{8,24},{9,... | collective-permute-start | bytes 82952 | tf_op jit(solution)/shard_map/ppermute | solution.py:412
  120.4 5.0 %collective-permute-start.4 = (bf16[4,3,1152]{2,1,0:T(4,128)(2,1)S(1)}, bf16[4,3,1152]{2,1,0:T(4,128)(2,1)S(1)}, u32[]{:S(2)}, u32[]{:S(2)}) collective-permute-start(bf16[4,3,1152]{2,1,0:T(4,128)(2,1)S(1)} %get-tuple-element.57), channel_id=1, source_target_pairs={{0,2},{1,3},{2,4},{3,5},{4,6},{5,7},{6,8},{7,9},{8,10},{9,11},{10,... | collective-permute-start | bytes 82952 | tf_op jit(solution)/shard_map/ppermute | solution.py:413
  126.2 1.2 copy-start.2
Sparse Core Ops, SparseCore 0:
  110.8 13.6 all-gather.2

commit v2 on v1

--- a/solution.py
+++ b/solution.py
@@ -18,13 +18,15 @@
 CHUNKS = 26
 LANES = 128
 EPS = 1e-05
-X, Y, Z = 4, 4, 16
-XY = X * Y
+Y, Z, FAR = 4, 16, 8
+NEAR = 32
 HALF = 1792
-PIECE = HALF // XY
-BIAS_PIECE = HEADS * 32 // XY
-ALL = ("x", "z", "y", "c", "m")
-PLANE = ("x", "m", "y")
+PIECE = HALF // NEAR
+BIAS_PIECE = HEADS * 32 // NEAR
+LINE = PIECE + Y * BIAS_PIECE
+ALL = ("x", "far", "pair", "y", "c", "m")
+PLANE = ("x", "m", "y", "pair")
+SWAP = [(0, 1), (1, 0)]
 BF = jnp.bfloat16
 F32 = jnp.float32
 
@@ -63,26 +65,47 @@
     return (upward * cumulative, cumulative + upward * density)
 
 
-def bias_kernel(pos_ref, table_ref, earth_ref):
+def bias_kernel(pos_ref, table_ref, earth_ref, place_ref, rest_ref):
+    tail = WIN - LANES
+
+    def looked_up(place):
+        low = place & (LANES - 1)
+        high = place >> 7
+        found = [jnp.zeros((8, LANES), F32) for _ in range(HEADS)]
+        for c in range(CHUNKS):
+            here = high == c
+            for h in range(HEADS):
+                row = table_ref[h : h + 1, c * LANES : min((c + 1) * LANES, BIAS_POS)]
+                if row.shape[1] < LANES:
+                    row = jnp.concatenate([row, jnp.zeros((1, LANES - row.shape[1]), F32)], axis=1)
+                row = jnp.broadcast_to(row, (8, LANES))
+                taken = jnp.take_along_axis(row, low, axis=1, mode="promise_in_bounds")
+                found[h] = jnp.where(here, taken, found[h])
+        return found
+
     def eight_rows(r, carry):
         rows = pl.ds(pl.multiple_of(r * 8, 8), 8)
-        for start, width in ((0, LANES), (LANES, WIN - LANES)):
-            place = pos_ref[rows, start : start + LANES]
-            low = place & (LANES - 1)
-            high = place >> 7
-            found = [jnp.zeros((8, LANES), F32) for _ in range(HEADS)]
-            for c in range(CHUNKS):
-                here = high == c
-                for h in range(HEADS):
-                    at = h * CHUNKS + c
-                    row = jnp.broadcast_to(table_ref[at : at + 1, :], (8, LANES))
-                    taken = jnp.take_along_axis(row, low, axis=1, mode="promise_in_bounds")
-                    found[h] = jnp.where(here, taken, found[h])
+        found = looked_up(pos_ref[rows, :LANES])
+        for h in range(HEADS):
+            earth_ref[h, rows, :LANES] = found[h]
+        return carry
+
+    lax.fori_loop(0, WIN // 8, eight_rows, 0)
+    place_ref[...] = jnp.zeros_like(place_ref)
+    place_ref[:, :WIN] = pos_ref[:, LANES:].T
+
+    def eight_columns(r, carry):
+        rows = pl.ds(pl.multiple_of(r * 8, 8), 8)
+        for k in range(2):
+            lanes = slice(k * LANES, (k + 1) * LANES)
+            found = looked_up(place_ref[rows, lanes])
             for h in range(HEADS):
-                earth_ref[h, rows, start : start + width] = found[h][:, :width]
+                rest_ref[h, rows, lanes] = found[h]
         return carry
 
-    lax.fori_loop(0, WIN // 8, eight_rows, 0)
+    lax.fori_loop(0, tail // 8, eight_columns, 0)
+    for h in range(HEADS):
+        earth_ref[h, :, LANES:] = rest_ref[h, :, :WIN].T
 
 
 def scatter_kernel(pos_ref, score_ref, table_ref, place_ref, rest_ref):
@@ -233,61 +256,54 @@
             put(send_ref, 1 - mine)
 
 
-def first_sum_kernel(keep_ref, came_ref, table_ref, out_ref, pad_ref):
+def first_sum_kernel(keep_ref, came_ref, table_ref, out_ref, total_ref, pad_ref):
+    total_ref[...] = keep_ref[...].astype(F32) + came_ref[...].astype(F32)
     pad_ref[...] = jnp.zeros_like(pad_ref)
-    for p in range(XY):
+    for p in range(NEAR):
+        pad_ref[p, :PIECE, :] = total_ref[p * PIECE : (p + 1) * PIECE, :]
+        pad_ref[p, PIECE : PIECE + BIAS_PIECE, :] = table_ref[p * BIAS_PIECE : (p + 1) * BIAS_PIECE, :]
+    out_ref[...] = pad_ref[...].astype(BF)
+
+
+def second_sum_kernel(came_ref, *refs):
+    out_ref, line_ref = refs[-2:]
+    came = came_ref[...].astype(F32)
+    line_ref[:PIECE, :] = jnp.sum(came[:, :PIECE], axis=0)
+    table = came[:, PIECE:].reshape(NEAR // Y // 2, Y, 2, 8, LANES)
+    table = jnp.sum(jnp.sum(table, axis=2), axis=0)
+    for y in range(Y):
+        at = PIECE + y * BIAS_PIECE
+        line_ref[at : at + BIAS_PIECE, :] = table[y, :BIAS_PIECE]
+    line = line_ref[...].astype(BF)
+    for n in range(FAR):
+        out_ref[n] = line
+
+
+def fan_kernel(came_ref, out_ref, line_ref, pad_ref):
+    line_ref[...] = jnp.sum(came_ref[...].astype(F32), axis=0)
+    pad_ref[...] = jnp.zeros_like(pad_ref)
+    for y in range(Y):
+        at = PIECE + y * BIAS_PIECE
+        pad_ref[y, :PIECE, :] = line_ref[:PIECE, :]
+        pad_ref[y, PIECE : PIECE + BIAS_PIECE, :] = line_ref[at : at + BIAS_PIECE, :]
+    pieces = pad_ref[...].astype(BF)
+    for p in range(NEAR):
+        out_ref[p] = pieces[p // 2 % Y]
+
+
+def finish_kernel(
+    factor, core_ref, mine_ref, came_ref, qkv_ref, proj_ref, up_ref, down_ref, gains_ref, bias_ref, flat_ref, wide_ref,
+):
+    core = core_ref[0]
+    mine, came = mine_ref[...].astype(F32), came_ref[...].astype(F32)
+    for p in range(NEAR):
         rows = slice(p * PIECE, (p + 1) * PIECE)
-        out_ref[p, :PIECE, :] = (keep_ref[rows, :].astype(F32) + came_ref[rows, :].astype(F32)).astype(BF)
-        pad_ref[p, :BIAS_PIECE, :] = table_ref[p * BIAS_PIECE : (p + 1) * BIAS_PIECE, :]
-        out_ref[p, PIECE:, :] = pad_ref[p].astype(BF)
-
-
-def second_sum_kernel(came_ref, out_ref, terms_ref, table_ref, pad_ref):
-    came = came_ref[...].astype(F32)
-    terms_ref[...] = jnp.sum(came[:, :PIECE], axis=0)
-    for y in range(Y):
-        part = came[y, PIECE:]
-        for x in range(1, X):
-            part = part + came[x * Y + y, PIECE:]
-        table_ref[y * BIAS_PIECE : (y + 1) * BIAS_PIECE, :] = part[:BIAS_PIECE]
-    pad_ref[...] = jnp.zeros_like(pad_ref)
-    few, less = PIECE // Z, Y * BIAS_PIECE // Z
-    for z in range(Z):
-        pad_ref[z, :few, :] = terms_ref[z * few : (z + 1) * few, :]
-        pad_ref[z, 8 : 8 + less, :] = table_ref[z * less : (z + 1) * less, :]
-    out_ref[...] = pad_ref[...].astype(BF)
-
-
-def third_sum_kernel(came_ref, out_ref):
-    total = jnp.sum(came_ref[...].astype(F32), axis=0).astype(BF)
-    for z in range(Z):
-        out_ref[z] = total
-
-
-def fan_kernel(came_ref, out_ref, came_wide_ref, terms_ref, table_ref):
-    came_wide_ref[...] = came_ref[...].astype(F32)
-    table_ref[...] = jnp.zeros_like(table_ref)
-    few, less = PIECE // Z, Y * BIAS_PIECE // Z
-    for z in range(Z):
-        terms_ref[z * few : (z + 1) * few, :] = came_wide_ref[z, :few, :]
-        y, at = z * less // BIAS_PIECE, z * less % BIAS_PIECE
-        table_ref[y, at : at + less, :] = came_wide_ref[z, 8 : 8 + less, :]
-    terms = terms_ref[...].astype(BF)
-    for p in range(XY):
-        out_ref[p, :PIECE, :] = terms
-        out_ref[p, PIECE:, :] = table_ref[p % Y].astype(BF)
-
-
-def finish_kernel(
-    factor, both_ref, mine_ref, qkv_ref, proj_ref, up_ref, down_ref, gains_ref, bias_ref, flat_ref, wide_ref,
-):
-    for half in range(2):
-        for p in range(XY):
-            flat_ref[half, p * PIECE : (p + 1) * PIECE, :] = both_ref[half, p, :PIECE, :]
+        flat_ref[core, rows, :] = mine[p, :PIECE] * factor
+        flat_ref[1 - core, rows, :] = came[p, :PIECE] * factor
 
     def block(k):
         rows = slice(k % 9 * WIDTH, (k % 9 + 1) * WIDTH)
-        return flat_ref[k // 9, rows, :].astype(F32) * factor
+        return flat_ref[k // 9, rows, :]
 
     for k in range(6):
         lanes = slice(k * LANES, (k + 1) * LANES)
@@ -296,12 +312,12 @@
         down_ref[:, lanes] = block(12 + k)
     qkv_ref[...] = wide_ref[:, : 3 * WIDTH]
     proj_ref[...] = wide_ref[:, 3 * WIDTH :]
-    gains = flat_ref[1, 9 * WIDTH :, :].astype(F32) * factor
+    gains = flat_ref[1, 9 * WIDTH :, :]
     for n in range(2):
         gains_ref[n : n + 1, :LANES] = gains[2 * n : 2 * n + 1]
         gains_ref[n : n + 1, LANES:] = gains[2 * n + 1 : 2 * n + 2, : WIDTH - LANES]
-    for p in range(XY):
-        piece = mine_ref[p, PIECE:, :].astype(F32)
+    for p in range(NEAR):
+        piece = mine[p, PIECE:]
         for r in range(BIAS_PIECE):
             h, c = divmod(p * BIAS_PIECE + r, 32)
             width = min(LANES, BIAS_POS - c * LANES)
@@ -311,16 +327,17 @@
 
 VMEM = pl.BlockSpec(memory_space=pltpu.VMEM)
 SMEM = pl.BlockSpec(memory_space=pltpu.SMEM)
-
-
-def kernel(function, name, outs, scratch=(), scalars=0, flops=1_000_000, moved=1_000_000):
+ANY = pl.BlockSpec(memory_space=pl.ANY)
+
+
+def kernel(function, name, outs, scratch=(), scalars=0, later=0, flops=1_000_000, moved=1_000_000):
     shapes = tuple(jax.ShapeDtypeStruct(s, t) for s, t in outs)
 
     def call(*args):
         return pl.pallas_call(
             function,
             out_shape=shapes,
-            in_specs=[SMEM] * scalars + [VMEM] * (len(args) - scalars),
+            in_specs=[SMEM] * scalars + [VMEM] * (len(args) - scalars - later) + [ANY] * later,
             out_specs=(VMEM,) * len(shapes),
             scratch_shapes=[pltpu.VMEM(s, t) for s, t in scratch],
             compiler_params=pltpu.CompilerParams(vmem_limit_bytes=48 * 1024 * 1024),
@@ -331,12 +348,13 @@
     return call
 
 
-find_bias = kernel(bias_kernel, "find_bias", [((HEADS, WIN, WIN), F32)], flops=20_000_000)
+REST = [((WIN - LANES, 2 * LANES), jnp.int32), ((HEADS, WIN - LANES, 2 * LANES), F32)]
+find_bias = kernel(bias_kernel, "find_bias", [((HEADS, WIN, WIN), F32)], REST, flops=20_000_000)
 spread_bias = kernel(
     scatter_kernel,
     "spread_bias",
     [((HEADS * 32, LANES), F32)],
-    [((WIN - LANES, 2 * LANES), jnp.int32), ((HEADS, WIN - LANES, 2 * LANES), F32)],
+    REST,
     flops=1_000_000_000,
 )
 block_grads = kernel(
@@ -348,23 +366,18 @@
     flops=1_000_000_000,
     moved=4_000_000,
 )
-first_sum = kernel(first_sum_kernel, "first_sum", [((XY, LANES, LANES), BF)], [((XY, 16, LANES), F32)])
+first_sum = kernel(
+    first_sum_kernel, "first_sum", [((NEAR, 64, LANES), BF)], [((HALF, LANES), F32), ((NEAR, 64, LANES), F32)]
+)
 second_sum = kernel(
-    second_sum_kernel,
-    "second_sum",
-    [((Z, 16, LANES), BF)],
-    [((PIECE, LANES), F32), ((Y * BIAS_PIECE, LANES), F32), ((Z, 16, LANES), F32)],
+    second_sum_kernel, "second_sum", [((FAR, LINE, LANES), BF)], [((LINE, LANES), F32)], later=3
 )
-third_sum = kernel(third_sum_kernel, "third_sum", [((Z, 16, LANES), BF)])
 fan = kernel(
-    fan_kernel,
-    "fan",
-    [((XY, LANES, LANES), BF)],
-    [((Z, 16, LANES), F32), ((PIECE, LANES), F32), ((Y, 16, LANES), F32)],
+    fan_kernel, "fan", [((NEAR, 64, LANES), BF)], [((LINE, LANES), F32), ((Y, 64, LANES), F32)]
 )
 
 
-def finish(factor, both, mine):
+def finish(factor, core, mine, came):
     return kernel(
         lambda *refs: finish_kernel(factor, *refs),
         "finish",
@@ -376,8 +389,9 @@
             ((2, WIDTH), F32),
             ((HEADS, BIAS_POS), F32),
         ],
-        [((2, HALF, LANES), BF), ((WIDTH, 4 * WIDTH), F32)],
-    )(both, mine)
+        [((2, HALF, LANES), F32), ((WIDTH, 4 * WIDTH), F32)],
+        scalars=1,
+    )(core, mine, came)
 
 
 def routes(lon_step, lat_step):
@@ -403,50 +417,52 @@
     return jnp.concatenate([top, bottom], axis=2)
 
 
-def unshifted(grad):
+def sent_back(grad):
     half_rows, half_cols = grad.shape[1] // 2, grad.shape[2] // 2
-    grad = jnp.roll(grad, 1, axis=0)
-    own, east = grad[:, :half_rows, :half_cols], grad[:, :half_rows, half_cols:]
-    south, corner = grad[:, half_rows:, :half_cols], grad[:, half_rows:, half_cols:]
+    east, south = grad[:, :half_rows, half_cols:], grad[:, half_rows:, :half_cols]
+    corner = grad[:, half_rows:, half_cols:]
     corner = lax.ppermute(corner, ALL, routes(1, 1))
     east = lax.ppermute(east, ALL, routes(1, 0))
     south = lax.ppermute(south, ALL, routes(0, 1))
+    return corner, east, south
+
+
+def unshifted(grad, corner, east, south):
+    own = grad[:, : grad.shape[1] // 2, : grad.shape[2] // 2]
     top = jnp.concatenate([corner, south], axis=2)
     bottom = jnp.concatenate([east, own], axis=2)
-    return jnp.concatenate([top, bottom], axis=1)
+    return jnp.roll(jnp.concatenate([top, bottom], axis=1), 1, axis=0)
 
 
 def body(states, cotangent, region, pos_index, w_qkv, w_proj, w_up, w_down, gains, earth_bias):
     levels, rows, merged = states.shape[1:]
-    place = jnp.pad(pos_index, ((0, 0), (0, 2 * LANES - WIN)))
-    table = jnp.pad(earth_bias[0], ((0, 0), (0, CHUNKS * LANES - BIAS_POS)))
-    (earth,) = find_bias(place, table.reshape(HEADS * CHUNKS, LANES))
+    (earth,) = find_bias(pos_index, earth_bias[0])
     pair = shifted(jnp.concatenate([states, cotangent], axis=0))
     cells = pair.reshape(2, CELLS, WIDTH)
     core = lax.axis_index("c").astype(jnp.int32).reshape(1)
     grad, send, keep, score = block_grads(
         region, core, cells[0], cells[1], earth, w_qkv, w_proj, w_up, w_down.T, gains
     )
-    came = lax.ppermute(send, "c", [(0, 1), (1, 0)])
-    grad_states = unshifted(grad.reshape(levels, rows, merged))[None]
+    came = lax.ppermute(send, "c", SWAP)
+    grad = grad.reshape(levels, rows, merged)
+    back = sent_back(grad)
     (spread,) = spread_bias(pos_index, score)
     (plane,) = first_sum(keep, came, spread)
     plane = lax.all_to_all(plane, PLANE, 0, 0)
-    (line,) = second_sum(plane)
-    line = lax.all_to_all(line, "z", 0, 0)
-    (line,) = third_sum(line)
-    line = lax.all_to_all(line, "z", 0, 0)
+    (line,) = second_sum(plane, *back)
+    line = lax.all_to_all(line, "far", 0, 0)
     (plane,) = fan(line)
     plane = lax.all_to_all(plane, PLANE, 0, 0)
-    both = lax.all_gather(plane, "c")
+    came = lax.ppermute(plane, "c", SWAP)
     factor = float(CELLS * lax.axis_size(ALL)) ** (-0.5)
-    grad_qkv, grad_proj, grad_up, grad_down, grad_gains, grad_bias = finish(factor, both, plane)
+    grad_qkv, grad_proj, grad_up, grad_down, grad_gains, grad_bias = finish(factor, core, plane, came)
+    grad_states = unshifted(grad, *back)[None]
     return (grad_states, grad_qkv, grad_proj, grad_up, grad_down.T, grad_gains, grad_bias[None])
 
 
 def solution(mesh):
-    fine = Mesh(mesh.devices.reshape(2, Z, Y, 2, 2), ALL)
-    lon, lat = ("x", "z"), ("y", "c")
+    fine = Mesh(mesh.devices.reshape(2, FAR, 2, Y, 2, 2), ALL)
+    lon, lat = ("x", "far", "pair"), ("y", "c")
     return jax.shard_map(
         body,
         mesh=fine,

time: 137 us -> 104 us (0.76)
  between operations: 14.4 us -> 0.93 us
  blocking collectives: 45.1 us -> 35.2 us
  waiting for transfers between devices: 13.5 us -> 5.47 us
  starting transfers between devices: 35 us -> 39 us
  local copies, waits for them, and re-layouts: 8.05 us -> 4.35 us
  Pallas kernels: 19.9 us -> 18.2 us
    all_to_all x2 -> x1, blocking collectives: 30.7 us -> 17.9 us  [body(): line = lax.all_to_all(line, 'far', 0, 0)]
    all_to_all x1, waiting for transfers between devices: 8.56 us -> 0.11 us  [body(): plane = lax.all_to_all(plane, PLANE, 0, 0)]
    unnamed x30 -> x23, local copies, waits for them, and re-layouts: 6.91 us -> 3.33 us
    ppermute x4 -> x5, starting transfers between devices: 12.8 us -> 15.8 us  [the longest x1 5.74 us: body(): came = lax.ppermute(plane, 'c', SWAP)]
    all_to_all x1, blocking collectives: 14.4 us -> 17.3 us  [body(): plane = lax.all_to_all(plane, PLANE, 0, 0)]
    pallas_call x8 -> x7, Pallas kernels: 19.9 us -> 18.2 us  [call(): pl.pallas_call(function, out_shape=shapes, in_specs=[SMEM] * scalars + [V...]
    ppermute x4 -> x5, waiting for transfers between devices: 4.89 us -> 5.35 us  [the longest x1 3.93 us: sent_back(): east = lax.ppermute(east, ALL, routes(1, 0))]
  transfers between devices with their start and end apart: 9 -> 9, of which waited for: 2 -> 4; matrix products, arithmetic and copies ran while one was open for 1% -> 1% of each run, Pallas kernels for 8% -> 9%
where the time goes in v2:
time: 104 us
  starting transfers between devices  39 us (38%)
  blocking collectives  35.2 us (34%)
  Pallas kernels  18.2 us (18%)
  waiting for transfers between devices  5.47 us (5%)
  local copies, waits for them, and re-layouts  4.35 us (4%)
    pallas_call x7, Pallas kernels, call(): pl.pallas_call(function, out_shape=shapes, in_specs=[SMEM] * scalars + [V...  18.2 us
    all_to_all x1, blocking collectives, body(): line = lax.all_to_all(line, 'far', 0, 0)  17.9 us
    all_to_all x1, blocking collectives, body(): plane = lax.all_to_all(plane, PLANE, 0, 0)  17.3 us
    ppermute x1, starting transfers between devices, shifted(): east = lax.ppermute(east, ALL, routes(-1, 0))  13 us
    ppermute x1, starting transfers between devices, body(): came = lax.ppermute(plane, 'c', SWAP)  5.74 us
    all_to_all x1, starting transfers between devices, body(): plane = lax.all_to_all(plane, PLANE, 0, 0)  4.76 us
    ppermute x1, starting transfers between devices, sent_back(): corner = lax.ppermute(corner, ALL, routes(1, 1))  4.5 us
    ppermute x1, waiting for transfers between devices, sent_back(): east = lax.ppermute(east, ALL, routes(1, 0))  3.93 us
  transfers between devices with their start and end apart: 9, of which 4 were waited for; matrix products, arithmetic and copies ran while one was open for 1% of the time, Pallas kernels for 9%

profile of v2, /device:TPU:1, one launch (start us, length us, event | category | flops | bytes accessed | tf_op | source)
XLA Modules:
  0.0 103.6 jit_solution(12113335022808936886)
XLA Ops:
  0.6 1.0 constant_dynamic-update-slice_fusion.1
  1.8 0.1 slice.62
  1.9 0.2 fusion.5
  2.2 13.0 %collective-permute-start = (bf16[2,4,3,1152]{3,1,2,0:T(4,128)(2,1)S(1)}, bf16[2,4,3,1152]{3,1,2,0:T(4,128)(2,1)S(1)}, u32[]{:S(2)}, u32[]{:S(2)}) collective-permute-start(bf16[2,4,3,1152]{3,1,2,0:T(4,128)(2,1)S(1)} %get-tuple-element.42), channel_id=1, source_target_pairs={{0,496},{1,497},{2,498},{3,499},{4,500},{5,501},{6,502},{7,503},{8... | collective-permute-start | bytes 165896 | tf_op jit(solution)/shard_map/ppermute | solution.py:413
  15.2 3.5 %collective-permute-start.2 = (bf16[2,4,3,1152]{3,1,2,0:T(4,128)(2,1)S(1)}, bf16[2,4,3,1152]{3,1,2,0:T(4,128)(2,1)S(1)}, u32[]{:S(2)}, u32[]{:S(2)}) collective-permute-start(bf16[2,4,3,1152]{3,1,2,0:T(4,128)(2,1)S(1)} %get-tuple-element.43), channel_id=1, source_target_pairs={{0,510},{1,511},{2,496},{3,497},{4,498},{5,499},{6,500},{7,501},{8... | collective-permute-start | bytes 165896 | tf_op jit(solution)/shard_map/ppermute | solution.py:412
  18.7 2.0 %collective-permute-start.1 = (bf16[2,4,3,1152]{3,1,2,0:T(4,128)(2,1)S(1)}, bf16[2,4,3,1152]{3,1,2,0:T(4,128)(2,1)S(1)}, u32[]{:S(2)}, u32[]{:S(2)}) collective-permute-start(bf16[2,4,3,1152]{3,1,2,0:T(4,128)(2,1)S(1)} %get-tuple-element.44), channel_id=1, source_target_pairs={{0,14},{1,15},{2,0},{3,1},{4,2},{5,3},{6,4},{7,5},{8,6},{9,7},{10,... | collective-permute-start | bytes 165896 | tf_op jit(solution)/shard_map/ppermute | solution.py:414
  20.8 5.3 %find_bias.1.earth_ref = f32[6,144,144]{2,1,0:T(8,128)S(1)} custom-call(s32[144,144]{1,0:T(8,128)S(1)} %copy-done, f32[6,3312]{1,0:T(8,128)S(1)} %bitcast.9), custom_call_target="tpu_custom_call" | custom-call | flops 20000000 | bytes 1000000 | tf_op jit(solution)/shard_map/find_bias/pallas_call | solution.py:337
  26.4 0.2 squeeze.10.g_ref
  26.7 0.2 squeeze.9.x_ref
  26.9 0.4 copy-done.4
  27.3 0.1 copy-done.2
  27.4 0.2 copy-done.1
  27.7 6.1 %block_grads.1 = (bf16[288,192]{1,0:T(8,128)(2,1)S(1)}, bf16[1792,128]{1,0:T(8,128)(2,1)S(1)}, bf16[1792,128]{1,0:T(8,128)(2,1)S(1)}, f32[6,144,144]{2,1,0:T(8,128)S(1)}) custom-call(s32[6,4]{1,0:T(8,128)S(1)} %copy.24.region_ref, s32[1]{0:T(128)} %bitcast.core_ref.refs_0_, bf16[288,192]{1,0:T(8,128)(2,1)S(1)} %squeeze.9.x_ref, ...), custom_call_target="tpu_custom_call" | custom-call | flops 1000000000 | bytes 4000000 | tf_op jit(solution)/shard_map/block_grads/pallas_call | solution.py:337
  33.9 3.0 %collective-permute-start.6 = (bf16[1792,128]{1,0:T(8,128)(2,1)S(1)}, bf16[1792,128]{1,0:T(8,128)(2,1)S(1)}, u32[]{:S(2)}, u32[]{:S(2)}) collective-permute-start(bf16[1792,128]{1,0:T(8,128)(2,1)S(1)} %get-tuple-element.19), channel_id=1, source_target_pairs={{0,2},{2,0},{1,3},{3,1},{4,6},{6,4},{5,7},{7,5},{8,10},{10,8},{9,1... | collective-permute-start | bytes 1376264 | tf_op jit(solution)/shard_map/ppermute | solution.py:446
  36.9 4.0 %spread_bias.1.table_ref = f32[192,128]{1,0:T(8,128)S(1)} custom-call(s32[144,144]{1,0:T(8,128)S(1)} %copy-done, f32[6,144,144]{2,1,0:T(8,128)S(1)} %get-tuple-element.20.score_ref), custom_call_target="tpu_custom_call" | custom-call | flops 1000000000 | bytes 1000000 | tf_op jit(solution)/shard_map/spread_bias/pallas_call | solution.py:337
  40.9 1.0 %first_sum.1 = bf16[32,64,128]{2,1,0:T(8,128)(2,1)} custom-call(bf16[1792,128]{1,0:T(8,128)(2,1)S(1)} %get-tuple-element.18.keep_ref, bf16[1792,128]{1,0:T(8,128)(2,1)S(1)} %collective-permute-done.6.came_ref, f32[192,128]{1,0:T(8,128)S(1)} %spread_bias.1.table_ref), custom_call_target="tpu_custom_call" | custom-call | flops 1000000 | bytes 1000000 | tf_op jit(solution)/shard_map/first_sum/pallas_call | solution.py:337
  42.0 4.8 %all-to-all-start = ((bf16[32,64,128]{2,1,0:T(8,128)(2,1)}), bf16[32,64,128]{2,1,0:T(8,128)(2,1)S(1)}, u32[]{:S(2)}, u32[]{:S(2)}) async-start(bf16[32,64,128]{2,1,0:T(8,128)(2,1)} %first_sum.1), calls=%async_computation | async-start | bytes 1048576 | tf_op jit(solution)/shard_map/all_to_all | solution.py:451
  46.7 0.2 reshape.26
  47.0 4.5 %collective-permute-start.3 = (bf16[4,3,1152]{2,1,0:T(4,128)(2,1)S(1)}, bf16[4,3,1152]{2,1,0:T(4,128)(2,1)S(1)}, u32[]{:S(2)}, u32[]{:S(2)}) collective-permute-start(bf16[4,3,1152]{2,1,0:T(4,128)(2,1)S(1)} %get-tuple-element.47), channel_id=1, source_target_pairs={{0,18},{1,19},{2,20},{3,21},{4,22},{5,23},{6,24},{7,25},{8,26},{9,... | collective-permute-start | bytes 82952 | tf_op jit(solution)/shard_map/ppermute | solution.py:424
  51.5 1.9 %collective-permute-start.5 = (bf16[4,3,1152]{2,1,0:T(4,128)(2,1)S(1)}, bf16[4,3,1152]{2,1,0:T(4,128)(2,1)S(1)}, u32[]{:S(2)}, u32[]{:S(2)}) collective-permute-start(bf16[4,3,1152]{2,1,0:T(4,128)(2,1)S(1)} %get-tuple-element.49), channel_id=1, source_target_pairs={{0,16},{1,17},{2,18},{3,19},{4,20},{5,21},{6,22},{7,23},{8,24},{9,... | collective-permute-start | bytes 82952 | tf_op jit(solution)/shard_map/ppermute | solution.py:425
  53.4 0.6 collective-permute-start.4
  54.0 0.7 collective-permute-done.3.refs_0_
  54.7 3.9 %collective-permute-done.5.refs_1_ = bf16[4,3,1152]{2,1,0:T(4,128)(2,1)S(1)} collective-permute-done((bf16[4,3,1152]{2,1,0:T(4,128)(2,1)S(1)}, bf16[4,3,1152]{2,1,0:T(4,128)(2,1)S(1)}, u32[]{:S(2)}, u32[]{:S(2)}) %collective-permute-start.5) | collective-permute-done | bytes 27680 | tf_op jit(solution)/shard_map/ppermute | solution.py:425
  58.6 0.1 all-to-all-done.came_ref
  58.7 0.1 second_sum.1
  58.8 17.9 %all_to_all.15.came_ref = bf16[8,80,128]{2,1,0:T(8,128)(2,1)S(1)} all-to-all(bf16[8,80,128]{2,1,0:T(8,128)(2,1)S(1)} %second_sum.1), channel_id=1, replica_groups=mesh['x'=2,'far'=8,'pair'=2,'y'=4,'c'=2,'m'=2] {'far'}, dimensions={0} | all-to-all | bytes 327680 | tf_op jit(solution)/shard_map/all_to_all | solution.py:453
  76.8 17.3 %all_to_all.16.refs_1_ = bf16[32,64,128]{2,1,0:T(8,128)(2,1)S(1)} all-to-all(bf16[32,64,128]{2,1,0:T(8,128)(2,1)S(1)} %fan.1), channel_id=1, replica_groups=mesh['x'=2,'far'=8,'pair'=2,'y'=4,'c'=2,'m'=2] {'x','m','y','pair'}, dimensions={0} | all-to-all | bytes 1048576 | tf_op jit(solution)/shard_map/all_to_all | solution.py:455
  94.1 5.7 %collective-permute-start.7 = (bf16[32,64,128]{2,1,0:T(8,128)(2,1)S(1)}, bf16[32,64,128]{2,1,0:T(8,128)(2,1)S(1)}, u32[]{:S(2)}, u32[]{:S(2)}) collective-permute-start(bf16[32,64,128]{2,1,0:T(8,128)(2,1)S(1)} %all_to_all.16.refs_1_), channel_id=1, source_target_pairs={{0,2},{2,0},{1,3},{3,1},{4,6},{6,4},{5,7},{7,5},{8,10},{10,8},{9,1... | collective-permute-start | bytes 1572872 | tf_op jit(solution)/shard_map/ppermute | solution.py:456
  99.9 0.7 copy.25
  100.6 0.7 collective-permute-done.7.refs_2_
  101.4 1.5 %finish.1 = (f32[192,576]{1,0:T(8,128)}, f32[192,192]{1,0:T(8,128)}, f32[192,768]{1,0:T(8,128)}, f32[192,768]{1,0:T(8,128)}, f32[2,192]{1,0:T(2,128)}, /*index=5*/f32[6,3312]{1,0:T(8,128)S(1)}) custom-call(s32[1]{0:T(128)} %bitcast.core_ref.refs_0_, bf16[32,64,128]{2,1,0:T(8,128)(2,1)S(1)} %all_to_all.16.refs_1_, ...), custom_call_target="tpu_custom_call" | custom-call | flops 1000000 | bytes 1000000 | tf_op jit(solution)/shard_map/finish/pallas_call | solution.py:337
  102.9 0.7 copy.26
  (31 shorter events, 0.8 us)
Async XLA Ops:
  0.6 1.0 copy-start.6
  1.9 18.8 %copy-start.8 = (s32[6,4]{0,1:T(4,128)S(1)}, s32[6,4]{0,1:T(4,128)}, u32[]{:S(2)}) copy-start(s32[6,4]{0,1:T(4,128)} %param.12) | copy-start | bytes 292
  1.9 18.9 %copy-start.7 = (f32[1,6,3312]{2,0,1:T(1,128)S(1)}, f32[1,6,3312]{2,0,1:T(1,128)}, u32[]{:S(2)}) copy-start(f32[1,6,3312]{2,0,1:T(1,128)} %param.19) | copy-start | bytes 238468
  2.2 18.7 %copy-start = (s32[144,144]{1,0:T(8,128)S(1)}, s32[144,144]{1,0:T(8,128)}, u32[]{:S(2)}) copy-start(s32[144,144]{1,0:T(8,128)} %pos_ref.3) | copy-start | bytes 248836
  2.2 24.0 %collective-permute-start = (bf16[2,4,3,1152]{3,1,2,0:T(4,128)(2,1)S(1)}, bf16[2,4,3,1152]{3,1,2,0:T(4,128)(2,1)S(1)}, u32[]{:S(2)}, u32[]{:S(2)}) collective-permute-start(bf16[2,4,3,1152]{3,1,2,0:T(4,128)(2,1)S(1)} %get-tuple-element.42), channel_id=1, source_target_pairs={{0,496},{1,497},{2,498},{3,499},{4,500},{5,501},{6,502},{7,503},{8... | collective-permute-start | bytes 165896 | tf_op jit(solution)/shard_map/ppermute | solution.py:413
  15.2 11.0 %collective-permute-start.2 = (bf16[2,4,3,1152]{3,1,2,0:T(4,128)(2,1)S(1)}, bf16[2,4,3,1152]{3,1,2,0:T(4,128)(2,1)S(1)}, u32[]{:S(2)}, u32[]{:S(2)}) collective-permute-start(bf16[2,4,3,1152]{3,1,2,0:T(4,128)(2,1)S(1)} %get-tuple-element.43), channel_id=1, source_target_pairs={{0,510},{1,511},{2,496},{3,497},{4,498},{5,499},{6,500},{7,501},{8... | collective-permute-start | bytes 165896 | tf_op jit(solution)/shard_map/ppermute | solution.py:412
  18.7 7.5 %collective-permute-start.1 = (bf16[2,4,3,1152]{3,1,2,0:T(4,128)(2,1)S(1)}, bf16[2,4,3,1152]{3,1,2,0:T(4,128)(2,1)S(1)}, u32[]{:S(2)}, u32[]{:S(2)}) collective-permute-start(bf16[2,4,3,1152]{3,1,2,0:T(4,128)(2,1)S(1)} %get-tuple-element.44), channel_id=1, source_target_pairs={{0,14},{1,15},{2,0},{3,1},{4,2},{5,3},{6,4},{7,5},{8,6},{9,7},{10,... | collective-permute-start | bytes 165896 | tf_op jit(solution)/shard_map/ppermute | solution.py:414
  26.4 0.9 copy-start.4
  26.4 1.0 copy-start.2
  26.6 1.0 copy-start.1
  26.7 1.1 %copy-start.3 = (bf16[192,576]{1,0:T(8,128)(2,1)S(1)}, bf16[192,576]{1,0:T(8,128)(2,1)}, u32[]{:S(2)}) copy-start(bf16[192,576]{1,0:T(8,128)(2,1)} %qkv_ref.1) | copy-start | bytes 663556
  26.9 0.8 copy-start.5
  33.9 7.1 %collective-permute-start.6 = (bf16[1792,128]{1,0:T(8,128)(2,1)S(1)}, bf16[1792,128]{1,0:T(8,128)(2,1)S(1)}, u32[]{:S(2)}, u32[]{:S(2)}) collective-permute-start(bf16[1792,128]{1,0:T(8,128)(2,1)S(1)} %get-tuple-element.19), channel_id=1, source_target_pairs={{0,2},{2,0},{1,3},{3,1},{4,6},{6,4},{5,7},{7,5},{8,10},{10,8},{9,1... | collective-permute-start | bytes 1376264 | tf_op jit(solution)/shard_map/ppermute | solution.py:446
  42.0 16.7 %all-to-all-start = ((bf16[32,64,128]{2,1,0:T(8,128)(2,1)}), bf16[32,64,128]{2,1,0:T(8,128)(2,1)S(1)}, u32[]{:S(2)}, u32[]{:S(2)}) async-start(bf16[32,64,128]{2,1,0:T(8,128)(2,1)} %first_sum.1), calls=%async_computation | async-start | bytes 1048576 | tf_op jit(solution)/shard_map/all_to_all | solution.py:451
  47.0 7.7 %collective-permute-start.3 = (bf16[4,3,1152]{2,1,0:T(4,128)(2,1)S(1)}, bf16[4,3,1152]{2,1,0:T(4,128)(2,1)S(1)}, u32[]{:S(2)}, u32[]{:S(2)}) collective-permute-start(bf16[4,3,1152]{2,1,0:T(4,128)(2,1)S(1)} %get-tuple-element.47), channel_id=1, source_target_pairs={{0,18},{1,19},{2,20},{3,21},{4,22},{5,23},{6,24},{7,25},{8,26},{9,... | collective-permute-start | bytes 82952 | tf_op jit(solution)/shard_map/ppermute | solution.py:424
  51.5 7.1 %collective-permute-start.5 = (bf16[4,3,1152]{2,1,0:T(4,128)(2,1)S(1)}, bf16[4,3,1152]{2,1,0:T(4,128)(2,1)S(1)}, u32[]{:S(2)}, u32[]{:S(2)}) collective-permute-start(bf16[4,3,1152]{2,1,0:T(4,128)(2,1)S(1)} %get-tuple-element.49), channel_id=1, source_target_pairs={{0,16},{1,17},{2,18},{3,19},{4,20},{5,21},{6,22},{7,23},{8,24},{9,... | collective-permute-start | bytes 82952 | tf_op jit(solution)/shard_map/ppermute | solution.py:425
  53.4 5.2 %collective-permute-start.4 = (bf16[4,3,1152]{2,1,0:T(4,128)(2,1)S(1)}, bf16[4,3,1152]{2,1,0:T(4,128)(2,1)S(1)}, u32[]{:S(2)}, u32[]{:S(2)}) collective-permute-start(bf16[4,3,1152]{2,1,0:T(4,128)(2,1)S(1)} %get-tuple-element.50), channel_id=1, source_target_pairs={{0,2},{1,3},{2,4},{3,5},{4,6},{5,7},{6,8},{7,9},{8,10},{9,11},{10,... | collective-permute-start | bytes 82952 | tf_op jit(solution)/shard_map/ppermute | solution.py:426
  94.1 7.3 %collective-permute-start.7 = (bf16[32,64,128]{2,1,0:T(8,128)(2,1)S(1)}, bf16[32,64,128]{2,1,0:T(8,128)(2,1)S(1)}, u32[]{:S(2)}, u32[]{:S(2)}) collective-permute-start(bf16[32,64,128]{2,1,0:T(8,128)(2,1)S(1)} %all_to_all.16.refs_1_), channel_id=1, source_target_pairs={{0,2},{2,0},{1,3},{3,1},{4,6},{6,4},{5,7},{7,5},{8,10},{10,8},{9,1... | collective-permute-start | bytes 1572872 | tf_op jit(solution)/shard_map/ppermute | solution.py:456

commit v3 on v2

--- a/solution.py
+++ b/solution.py
@@ -65,23 +65,30 @@
     return (upward * cumulative, cumulative + upward * density)
 
 
-def bias_kernel(pos_ref, table_ref, earth_ref, place_ref, rest_ref):
+def bias_kernel(pos_ref, table_ref, *refs):
+    earth_ref, place_ref, rest_ref, pair_ref = refs[-4:]
     tail = WIN - LANES
+    pair_ref[...] = jnp.zeros_like(pair_ref)
+    for n in range(HEADS // 2):
+        first, second = [
+            jnp.floor(table_ref[h] * 8191.0 + 0.5).astype(jnp.int32) for h in (2 * n, 2 * n + 1)
+        ]
+        pair_ref[n : n + 1, :BIAS_POS] = (first << 16) + (second & 65535)
 
     def looked_up(place):
         low = place & (LANES - 1)
         high = place >> 7
-        found = [jnp.zeros((8, LANES), F32) for _ in range(HEADS)]
+        found = [jnp.zeros((8, LANES), jnp.int32) for _ in range(HEADS // 2)]
         for c in range(CHUNKS):
             here = high == c
-            for h in range(HEADS):
-                row = table_ref[h : h + 1, c * LANES : min((c + 1) * LANES, BIAS_POS)]
-                if row.shape[1] < LANES:
-                    row = jnp.concatenate([row, jnp.zeros((1, LANES - row.shape[1]), F32)], axis=1)
-                row = jnp.broadcast_to(row, (8, LANES))
+            for n in range(HEADS // 2):
+                row = jnp.broadcast_to(pair_ref[n : n + 1, c * LANES : (c + 1) * LANES], (8, LANES))
                 taken = jnp.take_along_axis(row, low, axis=1, mode="promise_in_bounds")
-                found[h] = jnp.where(here, taken, found[h])
-        return found
+                found[n] = jnp.where(here, taken, found[n])
+        parts = []
+        for both in found:
+            parts += [both >> 16, (both << 16) >> 16]
+        return [part.astype(F32) * (1.0 / 8191.0) for part in parts]
 
     def eight_rows(r, carry):
         rows = pl.ds(pl.multiple_of(r * 8, 8), 8)
@@ -90,36 +97,38 @@
             earth_ref[h, rows, :LANES] = found[h]
         return carry
 
-    lax.fori_loop(0, WIN // 8, eight_rows, 0)
+    lax.fori_loop(0, WIN // 8, eight_rows, 0, unroll=2)
     place_ref[...] = jnp.zeros_like(place_ref)
     place_ref[:, :WIN] = pos_ref[:, LANES:].T
-
-    def eight_columns(r, carry):
-        rows = pl.ds(pl.multiple_of(r * 8, 8), 8)
+    for at in range(0, tail, 8):
         for k in range(2):
             lanes = slice(k * LANES, (k + 1) * LANES)
-            found = looked_up(place_ref[rows, lanes])
+            found = looked_up(place_ref[at : at + 8, lanes])
             for h in range(HEADS):
-                rest_ref[h, rows, lanes] = found[h]
-        return carry
-
-    lax.fori_loop(0, tail // 8, eight_columns, 0)
+                rest_ref[h, at : at + 8, lanes] = found[h]
     for h in range(HEADS):
         earth_ref[h, :, LANES:] = rest_ref[h, :, :WIN].T
 
 
 def scatter_kernel(pos_ref, score_ref, table_ref, place_ref, rest_ref):
-    which = lax.broadcasted_iota(jnp.int32, (LANES, LANES), 0)
-    chunk = lax.broadcasted_iota(jnp.int32, (32, LANES), 0)
+    which = lax.broadcasted_iota(jnp.int32, (LANES, LANES), 0).astype(F32).astype(BF)
+    chunk = lax.broadcasted_iota(jnp.int32, (32, LANES), 0).astype(F32).astype(BF)
+    one, zero = jnp.ones((LANES, LANES), BF), jnp.zeros((LANES, LANES), BF)
+    none = jnp.zeros((32, LANES), BF)
     tail = WIN - LANES
 
+    def rows_of(row, count):
+        part = jnp.broadcast_to(row, (16, LANES)).astype(BF)
+        return jnp.concatenate([part] * (count // 16), axis=0)
+
     def product(places, scores):
+        low = (places & (LANES - 1)).astype(F32)
+        high = (places >> 7).astype(F32)
         left, right = [], []
-        for n in range(8):
-            place = places[n : n + 1]
-            right.append(jnp.where(which == (place & (LANES - 1)), 1.0, 0.0).astype(BF))
-            here = chunk == (place >> 7)
-            parts = [jnp.where(here, score[n : n + 1], 0.0).astype(BF) for score in scores]
+        for n in range(places.shape[0]):
+            right.append(jnp.where(which == rows_of(low[n : n + 1], LANES), one, zero))
+            here = chunk == rows_of(high[n : n + 1], 32)
+            parts = [jnp.where(here, rows_of(score[n : n + 1], 32), none) for score in scores]
             left.append(jnp.concatenate(parts, axis=0))
         return nt(jnp.concatenate(left, axis=1), jnp.concatenate(right, axis=1))
 
@@ -130,25 +139,18 @@
         rest_ref[h, :, :WIN] = score_ref[h, :, LANES:].T
     total = jnp.zeros((HEADS * 32, LANES), F32)
     for k in range(2):
-        for at in range(0, tail, 8):
+        for at in range(0, tail, min(tail,16)):
             lanes = slice(k * LANES, (k + 1) * LANES)
-            total += product(
-                place_ref[at : at + 8, lanes], [rest_ref[h, at : at + 8, lanes] for h in range(HEADS)]
-            )
+            rows = slice(at, at + min(tail,16))
+            total += product(place_ref[rows, lanes], [rest_ref[h, rows, lanes] for h in range(HEADS)])
+    for at in range(0, WIN, 16):
+        rows = slice(at, at + 16)
+        total += product(pos_ref[rows, :LANES], [score_ref[h, rows, :LANES] for h in range(HEADS)])
     table_ref[...] = total
 
-    def eight_rows(r, carry):
-        rows = pl.ds(pl.multiple_of(r * 8, 8), 8)
-        table_ref[...] += product(
-            pos_ref[rows, :LANES], [score_ref[h, rows, :LANES] for h in range(HEADS)]
-        )
-        return carry
-
-    lax.fori_loop(0, WIN // 8, eight_rows, 0, unroll=2)
-
 
 def block_kernel(
-    region_ref, core_ref, x_ref, g_ref, earth_ref, qkv_ref, proj_ref, up_ref, down_ref, gains_ref,
+    region_ref, core_ref, x_ref, g_ref, earth_ref, gains_ref, qkv_ref, proj_ref, up_ref, down_ref,
     grad_ref, send_ref, keep_ref, score_ref, triple_ref, wide_ref, gain_ref,
 ):
     scale = SIZE ** (-0.5)
@@ -265,8 +267,7 @@
     out_ref[...] = pad_ref[...].astype(BF)
 
 
-def second_sum_kernel(came_ref, *refs):
-    out_ref, line_ref = refs[-2:]
+def second_sum_kernel(came_ref, out_ref, line_ref):
     came = came_ref[...].astype(F32)
     line_ref[:PIECE, :] = jnp.sum(came[:, :PIECE], axis=0)
     table = came[:, PIECE:].reshape(NEAR // Y // 2, Y, 2, 8, LANES)
@@ -279,7 +280,8 @@
         out_ref[n] = line
 
 
-def fan_kernel(came_ref, out_ref, line_ref, pad_ref):
+def fan_kernel(came_ref, *refs):
+    out_ref, line_ref, pad_ref = refs[-3:]
     line_ref[...] = jnp.sum(came_ref[...].astype(F32), axis=0)
     pad_ref[...] = jnp.zeros_like(pad_ref)
     for y in range(Y):
@@ -292,7 +294,8 @@
 
 
 def finish_kernel(
-    factor, core_ref, mine_ref, came_ref, qkv_ref, proj_ref, up_ref, down_ref, gains_ref, bias_ref, flat_ref, wide_ref,
+    factor, core_ref, mine_ref, came_ref, qkv_out, proj_out, up_out, down_out, gains_ref, bias_ref,
+    flat_ref, wide_ref, qkv_ref, proj_ref, up_ref, down_ref, done,
 ):
     core = core_ref[0]
     mine, came = mine_ref[...].astype(F32), came_ref[...].astype(F32)
@@ -305,13 +308,23 @@
         rows = slice(k % 9 * WIDTH, (k % 9 + 1) * WIDTH)
         return flat_ref[k // 9, rows, :]
 
+    def leave(n, ref, out):
+        copy = pltpu.make_async_copy(ref, out, done.at[n])
+        copy.start()
+        return copy
+
     for k in range(6):
-        lanes = slice(k * LANES, (k + 1) * LANES)
-        wide_ref[:, lanes] = block(k)
-        up_ref[:, lanes] = block(6 + k)
-        down_ref[:, lanes] = block(12 + k)
+        up_ref[:, k * LANES : (k + 1) * LANES] = block(6 + k)
+    copies = [leave(0, up_ref, up_out)]
+    for k in range(6):
+        down_ref[:, k * LANES : (k + 1) * LANES] = block(12 + k)
+    copies.append(leave(1, down_ref, down_out))
+    for k in range(6):
+        wide_ref[:, k * LANES : (k + 1) * LANES] = block(k)
     qkv_ref[...] = wide_ref[:, : 3 * WIDTH]
+    copies.append(leave(2, qkv_ref, qkv_out))
     proj_ref[...] = wide_ref[:, 3 * WIDTH :]
+    copies.append(leave(3, proj_ref, proj_out))
     gains = flat_ref[1, 9 * WIDTH :, :]
     for n in range(2):
         gains_ref[n : n + 1, :LANES] = gains[2 * n : 2 * n + 1]
@@ -322,7 +335,9 @@
             h, c = divmod(p * BIAS_PIECE + r, 32)
             width = min(LANES, BIAS_POS - c * LANES)
             if width > 0:
-                bias_ref[h : h + 1, c * LANES : c * LANES + width] = piece[r : r + 1, :width]
+                bias_ref[h, :, c * LANES : c * LANES + width] = piece[r : r + 1, :width]
+    for copy in copies:
+        copy.wait()
 
 
 VMEM = pl.BlockSpec(memory_space=pltpu.VMEM)
@@ -330,7 +345,7 @@
 ANY = pl.BlockSpec(memory_space=pl.ANY)
 
 
-def kernel(function, name, outs, scratch=(), scalars=0, later=0, flops=1_000_000, moved=1_000_000):
+def kernel(function, name, outs, scratch=(), copies=0, scalars=0, later=0, outside=0, flops=1_000_000, moved=1_000_000):
     shapes = tuple(jax.ShapeDtypeStruct(s, t) for s, t in outs)
 
     def call(*args):
@@ -338,8 +353,8 @@
             function,
             out_shape=shapes,
             in_specs=[SMEM] * scalars + [VMEM] * (len(args) - scalars - later) + [ANY] * later,
-            out_specs=(VMEM,) * len(shapes),
-            scratch_shapes=[pltpu.VMEM(s, t) for s, t in scratch],
+            out_specs=(ANY,) * outside + (VMEM,) * (len(shapes) - outside),
+            scratch_shapes=[pltpu.VMEM(s, t) for s, t in scratch] + [pltpu.SemaphoreType.DMA((copies,))] * (copies > 0),
             compiler_params=pltpu.CompilerParams(vmem_limit_bytes=48 * 1024 * 1024),
             cost_estimate=pl.CostEstimate(flops=flops, bytes_accessed=moved, transcendentals=0),
             name=name,
@@ -349,7 +364,7 @@
 
 
 REST = [((WIN - LANES, 2 * LANES), jnp.int32), ((HEADS, WIN - LANES, 2 * LANES), F32)]
-find_bias = kernel(bias_kernel, "find_bias", [((HEADS, WIN, WIN), F32)], REST, flops=20_000_000)
+find_bias = kernel(bias_kernel, "find_bias", [((HEADS, WIN, WIN), F32)], REST + [((8, CHUNKS * LANES), jnp.int32)], later=5, flops=20_000_000)
 spread_bias = kernel(
     scatter_kernel,
     "spread_bias",
@@ -370,10 +385,10 @@
     first_sum_kernel, "first_sum", [((NEAR, 64, LANES), BF)], [((HALF, LANES), F32), ((NEAR, 64, LANES), F32)]
 )
 second_sum = kernel(
-    second_sum_kernel, "second_sum", [((FAR, LINE, LANES), BF)], [((LINE, LANES), F32)], later=3
+    second_sum_kernel, "second_sum", [((FAR, LINE, LANES), BF)], [((LINE, LANES), F32)]
 )
 fan = kernel(
-    fan_kernel, "fan", [((NEAR, 64, LANES), BF)], [((LINE, LANES), F32), ((Y, 64, LANES), F32)]
+    fan_kernel, "fan", [((NEAR, 64, LANES), BF)], [((LINE, LANES), F32), ((Y, 64, LANES), F32)], later=3
 )
 
 
@@ -387,10 +402,13 @@
             ((WIDTH, 4 * WIDTH), F32),
             ((WIDTH, 4 * WIDTH), F32),
             ((2, WIDTH), F32),
-            ((HEADS, BIAS_POS), F32),
+            ((HEADS, 1, BIAS_POS), F32),
         ],
-        [((2, HALF, LANES), F32), ((WIDTH, 4 * WIDTH), F32)],
+        [((2, HALF, LANES), F32), ((WIDTH, 4 * WIDTH), F32)]
+        + [((WIDTH, 3 * WIDTH), F32), ((WIDTH, WIDTH), F32), ((WIDTH, 4 * WIDTH), F32), ((WIDTH, 4 * WIDTH), F32)],
+        copies=4,
         scalars=1,
+        outside=4,
     )(core, mine, came)
 
 
@@ -436,12 +454,13 @@
 
 def body(states, cotangent, region, pos_index, w_qkv, w_proj, w_up, w_down, gains, earth_bias):
     levels, rows, merged = states.shape[1:]
-    (earth,) = find_bias(pos_index, earth_bias[0])
+    weights = (gains, w_qkv, w_proj, w_up, w_down.T)
+    (earth,) = find_bias(pos_index, earth_bias.transpose(1, 0, 2), *weights)
     pair = shifted(jnp.concatenate([states, cotangent], axis=0))
     cells = pair.reshape(2, CELLS, WIDTH)
     core = lax.axis_index("c").astype(jnp.int32).reshape(1)
     grad, send, keep, score = block_grads(
-        region, core, cells[0], cells[1], earth, w_qkv, w_proj, w_up, w_down.T, gains
+        region, core, cells[0], cells[1], earth, *weights
     )
     came = lax.ppermute(send, "c", SWAP)
     grad = grad.reshape(levels, rows, merged)
@@ -449,15 +468,15 @@
     (spread,) = spread_bias(pos_index, score)
     (plane,) = first_sum(keep, came, spread)
     plane = lax.all_to_all(plane, PLANE, 0, 0)
-    (line,) = second_sum(plane, *back)
+    (line,) = second_sum(plane)
     line = lax.all_to_all(line, "far", 0, 0)
-    (plane,) = fan(line)
+    (plane,) = fan(line, *back)
     plane = lax.all_to_all(plane, PLANE, 0, 0)
     came = lax.ppermute(plane, "c", SWAP)
     factor = float(CELLS * lax.axis_size(ALL)) ** (-0.5)
     grad_qkv, grad_proj, grad_up, grad_down, grad_gains, grad_bias = finish(factor, core, plane, came)
     grad_states = unshifted(grad, *back)[None]
-    return (grad_states, grad_qkv, grad_proj, grad_up, grad_down.T, grad_gains, grad_bias[None])
+    return (grad_states, grad_qkv, grad_proj, grad_up, grad_down.T, grad_gains, grad_bias.transpose(1, 0, 2))
 
 
 def solution(mesh):

time: 104 us -> 97.9 us (0.941)
  blocking collectives: 35.2 us -> 29.3 us
  Pallas kernels: 18.2 us -> 14.7 us
  starting transfers between devices: 39 us -> 42 us
    all_to_all x1 -> x0, blocking collectives: 17.9 us -> none  [body(): line = lax.all_to_all(line, 'far', 0, 0)]
    all_to_all x1 -> x2, blocking collectives: 17.3 us -> 29.3 us  [body(): plane = lax.all_to_all(plane, PLANE, 0, 0)]
    pallas_call x7, Pallas kernels: 18.2 us -> 14.7 us  [call(): pl.pallas_call(function, out_shape=shapes, in_specs=[SMEM] * scalars + [V...]
    ppermute x1, waiting for transfers between devices: 3.93 us -> 1.04 us  [sent_back(): east = lax.ppermute(east, ALL, routes(1, 0))]
    ppermute x1, starting transfers between devices: 1.92 us -> 4.52 us  [sent_back(): east = lax.ppermute(east, ALL, routes(1, 0))]
    all_to_all x1, waiting for transfers between devices: 0.11 us -> 2.29 us  [body(): line = lax.all_to_all(line, 'far', 0, 0)]
    ppermute x1, starting transfers between devices: 5.74 us -> 7.27 us  [body(): came = lax.ppermute(plane, 'c', SWAP)]
    ppermute x1, waiting for transfers between devices: 0.67 us -> 1.84 us  [sent_back(): corner = lax.ppermute(corner, ALL, routes(1, 1))]
  transfers between devices with their start and end apart: 9 -> 9, of which waited for: 4 -> 4; matrix products, arithmetic and copies ran while one was open for 1% -> 1% of each run, Pallas kernels for 9% -> 5%
where the time goes in v3:
time: 97.9 us; the launch traced here: 97.4 us
  starting transfers between devices  42 us (43%)
  blocking collectives  29.3 us (30%)
  Pallas kernels  14.7 us (15%)
  waiting for transfers between devices  5.92 us (6%)
  local copies, waits for them, and re-layouts  4.13 us (4%)
    all_to_all x2, blocking collectives, body(): plane = lax.all_to_all(plane, PLANE, 0, 0)  29.3 us
    pallas_call x7, Pallas kernels, call(): pl.pallas_call(function, out_shape=shapes, in_specs=[SMEM] * scalars + [V...  14.7 us
    ppermute x1, starting transfers between devices, shifted(): east = lax.ppermute(east, ALL, routes(-1, 0))  12.9 us
    ppermute x1, starting transfers between devices, body(): came = lax.ppermute(plane, 'c', SWAP)  7.27 us
    ppermute x1, starting transfers between devices, sent_back(): east = lax.ppermute(east, ALL, routes(1, 0))  4.52 us
    all_to_all x1, starting transfers between devices, body(): line = lax.all_to_all(line, 'far', 0, 0)  4.51 us
    ppermute x1, starting transfers between devices, sent_back(): corner = lax.ppermute(corner, ALL, routes(1, 1))  4.28 us
    ppermute x1, starting transfers between devices, shifted(): corner = lax.ppermute(corner, ALL, routes(-1, -1))  3.48 us
  transfers between devices with their start and end apart: 9, of which 4 were waited for; matrix products, arithmetic and copies ran while one was open for 1% of the time, Pallas kernels for 5%

profile of v3, /device:TPU:1, one launch (start us, length us, event | category | flops | bytes accessed | tf_op | source)
XLA Modules:
  0.0 97.4 jit_solution(13178140231464788496)
XLA Ops:
  0.6 1.0 constant_dynamic-update-slice_fusion.1
  1.8 0.1 slice.62
  2.0 0.2 fusion.5
  2.2 12.9 %collective-permute-start = (bf16[2,4,3,1152]{3,1,2,0:T(4,128)(2,1)S(1)}, bf16[2,4,3,1152]{3,1,2,0:T(4,128)(2,1)S(1)}, u32[]{:S(2)}, u32[]{:S(2)}) collective-permute-start(bf16[2,4,3,1152]{3,1,2,0:T(4,128)(2,1)S(1)} %get-tuple-element.42), channel_id=1, source_target_pairs={{0,496},{1,497},{2,498},{3,499},{4,500},{5,501},{6,502},{7,503},{8... | collective-permute-start | bytes 165896 | tf_op jit(solution)/shard_map/ppermute | solution.py:431
  15.1 3.5 %collective-permute-start.2 = (bf16[2,4,3,1152]{3,1,2,0:T(4,128)(2,1)S(1)}, bf16[2,4,3,1152]{3,1,2,0:T(4,128)(2,1)S(1)}, u32[]{:S(2)}, u32[]{:S(2)}) collective-permute-start(bf16[2,4,3,1152]{3,1,2,0:T(4,128)(2,1)S(1)} %get-tuple-element.43), channel_id=1, source_target_pairs={{0,510},{1,511},{2,496},{3,497},{4,498},{5,499},{6,500},{7,501},{8... | collective-permute-start | bytes 165896 | tf_op jit(solution)/shard_map/ppermute | solution.py:430
  18.6 2.0 %collective-permute-start.1 = (bf16[2,4,3,1152]{3,1,2,0:T(4,128)(2,1)S(1)}, bf16[2,4,3,1152]{3,1,2,0:T(4,128)(2,1)S(1)}, u32[]{:S(2)}, u32[]{:S(2)}) collective-permute-start(bf16[2,4,3,1152]{3,1,2,0:T(4,128)(2,1)S(1)} %get-tuple-element.44), channel_id=1, source_target_pairs={{0,14},{1,15},{2,0},{3,1},{4,2},{5,3},{6,4},{7,5},{8,6},{9,7},{10,... | collective-permute-start | bytes 165896 | tf_op jit(solution)/shard_map/ppermute | solution.py:432
  20.6 0.7 copy-done.8
  21.3 0.1 copy.23.region_ref
  21.4 0.6 copy-done.6
  22.1 2.9 %find_bias.1.earth_ref = f32[6,144,144]{2,1,0:T(8,128)S(1)} custom-call(s32[144,144]{1,0:T(8,128)S(1)} %copy-done.3, f32[6,1,3312]{2,1,0:T(1,128)S(1)} %bitcast.9, f32[2,192]{1,0:T(2,128)S(1)} %copy-done.6, bf16[192,576]{1,0:T(8,128)(2,1)S(1)} %copy-done.2, bf16[192,192]{1,0:T(8,128)(2,1)S(1)} %copy-done.4, bf16[192,768]{1,0:T(8,128)(2,1)S(1)} %copy-done, ...), custom_call_target="tpu_custom_call" | custom-call | flops 20000000 | bytes 1000000 | tf_op jit(solution)/shard_map/find_bias/pallas_call | solution.py:352
  25.0 0.1 maximum_maximum_fusion
  25.1 0.1 fusion.7
  25.2 0.2 squeeze.7.g_ref
  25.4 0.2 squeeze.6.x_ref
  25.6 6.1 %block_grads.1 = (bf16[288,192]{1,0:T(8,128)(2,1)S(1)}, bf16[1792,128]{1,0:T(8,128)(2,1)S(1)}, bf16[1792,128]{1,0:T(8,128)(2,1)S(1)}, f32[6,144,144]{2,1,0:T(8,128)S(1)}) custom-call(s32[6,4]{1,0:T(8,128)S(1)} %copy.23.region_ref, s32[1]{0:T(128)} %bitcast.core_ref.refs_0_, bf16[288,192]{1,0:T(8,128)(2,1)S(1)} %squeeze.6.x_ref, ...), custom_call_target="tpu_custom_call" | custom-call | flops 1000000000 | bytes 4000000 | tf_op jit(solution)/shard_map/block_grads/pallas_call | solution.py:352
  31.8 3.0 %collective-permute-start.6 = (bf16[1792,128]{1,0:T(8,128)(2,1)S(1)}, bf16[1792,128]{1,0:T(8,128)(2,1)S(1)}, u32[]{:S(2)}, u32[]{:S(2)}) collective-permute-start(bf16[1792,128]{1,0:T(8,128)(2,1)S(1)} %get-tuple-element.19), channel_id=1, source_target_pairs={{0,2},{2,0},{1,3},{3,1},{4,6},{6,4},{5,7},{7,5},{8,10},{10,8},{9,1... | collective-permute-start | bytes 1376264 | tf_op jit(solution)/shard_map/ppermute | solution.py:465
  34.8 2.4 %spread_bias.1.table_ref = f32[192,128]{1,0:T(8,128)S(1)} custom-call(s32[144,144]{1,0:T(8,128)S(1)} %copy-done.3, f32[6,144,144]{2,1,0:T(8,128)S(1)} %get-tuple-element.20.score_ref), custom_call_target="tpu_custom_call" | custom-call | flops 1000000000 | bytes 1000000 | tf_op jit(solution)/shard_map/spread_bias/pallas_call | solution.py:352
  37.3 0.2 first_sum.1
  37.5 16.4 %all_to_all.15.came_ref = bf16[32,64,128]{2,1,0:T(8,128)(2,1)S(1)} all-to-all(bf16[32,64,128]{2,1,0:T(8,128)(2,1)S(1)} %first_sum.1), channel_id=1, replica_groups=mesh['x'=2,'far'=8,'pair'=2,'y'=4,'c'=2,'m'=2] {'x','m','y','pair'}, dimensions={0} | all-to-all | bytes 1048576 | tf_op jit(solution)/shard_map/all_to_all | solution.py:470
  54.0 0.8 second_sum.1
  54.7 4.5 %all-to-all-start.1 = ((bf16[8,80,128]{2,1,0:T(8,128)(2,1)}), bf16[8,80,128]{2,1,0:T(8,128)(2,1)S(1)}, u32[]{:S(2)}, u32[]{:S(2)}) async-start(bf16[8,80,128]{2,1,0:T(8,128)(2,1)} %second_sum.1), calls=%async_computation.1 | async-start | bytes 327680 | tf_op jit(solution)/shard_map/all_to_all | solution.py:472
  59.2 0.2 reshape.26
  59.5 4.3 %collective-permute-start.3 = (bf16[4,3,1152]{2,1,0:T(4,128)(2,1)S(1)}, bf16[4,3,1152]{2,1,0:T(4,128)(2,1)S(1)}, u32[]{:S(2)}, u32[]{:S(2)}) collective-permute-start(bf16[4,3,1152]{2,1,0:T(4,128)(2,1)S(1)} %get-tuple-element.47), channel_id=1, source_target_pairs={{0,18},{1,19},{2,20},{3,21},{4,22},{5,23},{6,24},{7,25},{8,26},{9,... | collective-permute-start | bytes 82952 | tf_op jit(solution)/shard_map/ppermute | solution.py:442
  63.8 4.5 %collective-permute-start.5 = (bf16[4,3,1152]{2,1,0:T(4,128)(2,1)S(1)}, bf16[4,3,1152]{2,1,0:T(4,128)(2,1)S(1)}, u32[]{:S(2)}, u32[]{:S(2)}) collective-permute-start(bf16[4,3,1152]{2,1,0:T(4,128)(2,1)S(1)} %get-tuple-element.49), channel_id=1, source_target_pairs={{0,16},{1,17},{2,18},{3,19},{4,20},{5,21},{6,22},{7,23},{8,24},{9,... | collective-permute-start | bytes 82952 | tf_op jit(solution)/shard_map/ppermute | solution.py:443
  68.3 1.8 %collective-permute-done.3.refs_0_ = bf16[4,3,1152]{2,1,0:T(4,128)(2,1)S(1)} collective-permute-done((bf16[4,3,1152]{2,1,0:T(4,128)(2,1)S(1)}, bf16[4,3,1152]{2,1,0:T(4,128)(2,1)S(1)}, u32[]{:S(2)}, u32[]{:S(2)}) %collective-permute-start.3) | collective-permute-done | bytes 27680 | tf_op jit(solution)/shard_map/ppermute | solution.py:442
  70.2 1.0 %collective-permute-done.5.refs_1_ = bf16[4,3,1152]{2,1,0:T(4,128)(2,1)S(1)} collective-permute-done((bf16[4,3,1152]{2,1,0:T(4,128)(2,1)S(1)}, bf16[4,3,1152]{2,1,0:T(4,128)(2,1)S(1)}, u32[]{:S(2)}, u32[]{:S(2)}) %collective-permute-start.5) | collective-permute-done | bytes 27680 | tf_op jit(solution)/shard_map/ppermute | solution.py:443
  71.2 2.3 %all-to-all-done.1.came_ref = bf16[8,80,128]{2,1,0:T(8,128)(2,1)S(1)} async-done(((bf16[8,80,128]{2,1,0:T(8,128)(2,1)}), bf16[8,80,128]{2,1,0:T(8,128)(2,1)S(1)}, u32[]{:S(2)}, u32[]{:S(2)}) %all-to-all-start.1) | async-done | bytes 163872 | tf_op jit(solution)/shard_map/all_to_all | solution.py:472
  73.6 12.8 %all_to_all.16.refs_1_ = bf16[32,64,128]{2,1,0:T(8,128)(2,1)S(1)} all-to-all(bf16[32,64,128]{2,1,0:T(8,128)(2,1)S(1)} %fan.1), channel_id=1, replica_groups=mesh['x'=2,'far'=8,'pair'=2,'y'=4,'c'=2,'m'=2] {'x','m','y','pair'}, dimensions={0} | all-to-all | bytes 1048576 | tf_op jit(solution)/shard_map/all_to_all | solution.py:474
  86.4 7.3 %collective-permute-start.7 = (bf16[32,64,128]{2,1,0:T(8,128)(2,1)S(1)}, bf16[32,64,128]{2,1,0:T(8,128)(2,1)S(1)}, u32[]{:S(2)}, u32[]{:S(2)}) collective-permute-start(bf16[32,64,128]{2,1,0:T(8,128)(2,1)S(1)} %all_to_all.16.refs_1_), channel_id=1, source_target_pairs={{0,2},{2,0},{1,3},{3,1},{4,6},{6,4},{5,7},{7,5},{8,10},{10,8},{9,1... | collective-permute-start | bytes 1572872 | tf_op jit(solution)/shard_map/ppermute | solution.py:475
  93.8 0.7 copy.24
  94.5 0.7 collective-permute-done.7.refs_2_
  95.2 2.2 %finish.1 = (f32[192,576]{1,0:T(8,128)}, f32[192,192]{1,0:T(8,128)}, f32[192,768]{1,0:T(8,128)}, f32[192,768]{1,0:T(8,128)}, f32[2,192]{1,0:T(2,128)}, /*index=5*/f32[6,1,3312]{2,1,0:T(1,128)}) custom-call(s32[1]{0:T(128)} %bitcast.core_ref.refs_0_, bf16[32,64,128]{2,1,0:T(8,128)(2,1)S(1)} %all_to_all.16.refs_1_, ...), custom_call_target="tpu_custom_call" | custom-call | flops 1000000 | bytes 1000000 | tf_op jit(solution)/shard_map/finish/pallas_call | solution.py:352
  (29 shorter events, 0.4 us)
Async XLA Ops:
  0.6 1.0 %copy-start.7 = (bf16[1,4,6,2304]{3,1,2,0:T(4,128)(2,1)S(1)}, bf16[1,4,6,2304]{3,1,2,0:T(4,128)(2,1)}, u32[]{:S(2)}) copy-start(bf16[1,4,6,2304]{3,1,2,0:T(4,128)(2,1)} %param.11) | copy-start | bytes 331780
  1.7 19.7 %copy-start.4 = (bf16[192,192]{1,0:T(8,128)(2,1)S(1)}, bf16[192,192]{1,0:T(8,128)(2,1)}, u32[]{:S(2)}) copy-start(bf16[192,192]{1,0:T(8,128)(2,1)} %proj_ref.1) | copy-start | bytes 221188
  1.7 19.7 %copy-start.5 = (f32[1,6,3312]{2,0,1:T(1,128)S(1)}, f32[1,6,3312]{2,0,1:T(1,128)}, u32[]{:S(2)}) copy-start(f32[1,6,3312]{2,0,1:T(1,128)} %param.19) | copy-start | bytes 238468
  1.8 19.6 %copy-start.1 = (bf16[768,192]{0,1:T(8,128)(2,1)S(1)}, bf16[768,192]{0,1:T(8,128)(2,1)}, u32[]{:S(2)}) copy-start(bf16[768,192]{0,1:T(8,128)(2,1)} %param.17) | copy-start | bytes 884740
  1.8 19.6 %copy-start.3 = (s32[144,144]{1,0:T(8,128)S(1)}, s32[144,144]{1,0:T(8,128)}, u32[]{:S(2)}) copy-start(s32[144,144]{1,0:T(8,128)} %pos_ref.3) | copy-start | bytes 248836
  1.9 19.5 %copy-start = (bf16[192,768]{1,0:T(8,128)(2,1)S(1)}, bf16[192,768]{1,0:T(8,128)(2,1)}, u32[]{:S(2)}) copy-start(bf16[192,768]{1,0:T(8,128)(2,1)} %up_ref.1) | copy-start | bytes 884740
  2.0 19.5 %copy-start.2 = (bf16[192,576]{1,0:T(8,128)(2,1)S(1)}, bf16[192,576]{1,0:T(8,128)(2,1)}, u32[]{:S(2)}) copy-start(bf16[192,576]{1,0:T(8,128)(2,1)} %qkv_ref.1) | copy-start | bytes 663556
  2.2 22.7 %collective-permute-start = (bf16[2,4,3,1152]{3,1,2,0:T(4,128)(2,1)S(1)}, bf16[2,4,3,1152]{3,1,2,0:T(4,128)(2,1)S(1)}, u32[]{:S(2)}, u32[]{:S(2)}) collective-permute-start(bf16[2,4,3,1152]{3,1,2,0:T(4,128)(2,1)S(1)} %get-tuple-element.42), channel_id=1, source_target_pairs={{0,496},{1,497},{2,498},{3,499},{4,500},{5,501},{6,502},{7,503},{8... | collective-permute-start | bytes 165896 | tf_op jit(solution)/shard_map/ppermute | solution.py:431
  15.1 9.8 %collective-permute-start.2 = (bf16[2,4,3,1152]{3,1,2,0:T(4,128)(2,1)S(1)}, bf16[2,4,3,1152]{3,1,2,0:T(4,128)(2,1)S(1)}, u32[]{:S(2)}, u32[]{:S(2)}) collective-permute-start(bf16[2,4,3,1152]{3,1,2,0:T(4,128)(2,1)S(1)} %get-tuple-element.43), channel_id=1, source_target_pairs={{0,510},{1,511},{2,496},{3,497},{4,498},{5,499},{6,500},{7,501},{8... | collective-permute-start | bytes 165896 | tf_op jit(solution)/shard_map/ppermute | solution.py:430
  18.6 6.4 %collective-permute-start.1 = (bf16[2,4,3,1152]{3,1,2,0:T(4,128)(2,1)S(1)}, bf16[2,4,3,1152]{3,1,2,0:T(4,128)(2,1)S(1)}, u32[]{:S(2)}, u32[]{:S(2)}) collective-permute-start(bf16[2,4,3,1152]{3,1,2,0:T(4,128)(2,1)S(1)} %get-tuple-element.44), channel_id=1, source_target_pairs={{0,14},{1,15},{2,0},{3,1},{4,2},{5,3},{6,4},{7,5},{8,6},{9,7},{10,... | collective-permute-start | bytes 165896 | tf_op jit(solution)/shard_map/ppermute | solution.py:432
  20.6 0.7 copy-start.8
  21.4 0.7 copy-start.6
  31.8 5.5 %collective-permute-start.6 = (bf16[1792,128]{1,0:T(8,128)(2,1)S(1)}, bf16[1792,128]{1,0:T(8,128)(2,1)S(1)}, u32[]{:S(2)}, u32[]{:S(2)}) collective-permute-start(bf16[1792,128]{1,0:T(8,128)(2,1)S(1)} %get-tuple-element.19), channel_id=1, source_target_pairs={{0,2},{2,0},{1,3},{3,1},{4,6},{6,4},{5,7},{7,5},{8,10},{10,8},{9,1... | collective-permute-start | bytes 1376264 | tf_op jit(solution)/shard_map/ppermute | solution.py:465
  54.7 18.8 %all-to-all-start.1 = ((bf16[8,80,128]{2,1,0:T(8,128)(2,1)}), bf16[8,80,128]{2,1,0:T(8,128)(2,1)S(1)}, u32[]{:S(2)}, u32[]{:S(2)}) async-start(bf16[8,80,128]{2,1,0:T(8,128)(2,1)} %second_sum.1), calls=%async_computation.1 | async-start | bytes 327680 | tf_op jit(solution)/shard_map/all_to_all | solution.py:472
  59.5 10.7 %collective-permute-start.3 = (bf16[4,3,1152]{2,1,0:T(4,128)(2,1)S(1)}, bf16[4,3,1152]{2,1,0:T(4,128)(2,1)S(1)}, u32[]{:S(2)}, u32[]{:S(2)}) collective-permute-start(bf16[4,3,1152]{2,1,0:T(4,128)(2,1)S(1)} %get-tuple-element.47), channel_id=1, source_target_pairs={{0,18},{1,19},{2,20},{3,21},{4,22},{5,23},{6,24},{7,25},{8,26},{9,... | collective-permute-start | bytes 82952 | tf_op jit(solution)/shard_map/ppermute | solution.py:442
  63.8 7.4 %collective-permute-start.5 = (bf16[4,3,1152]{2,1,0:T(4,128)(2,1)S(1)}, bf16[4,3,1152]{2,1,0:T(4,128)(2,1)S(1)}, u32[]{:S(2)}, u32[]{:S(2)}) collective-permute-start(bf16[4,3,1152]{2,1,0:T(4,128)(2,1)S(1)} %get-tuple-element.49), channel_id=1, source_target_pairs={{0,16},{1,17},{2,18},{3,19},{4,20},{5,21},{6,22},{7,23},{8,24},{9,... | collective-permute-start | bytes 82952 | tf_op jit(solution)/shard_map/ppermute | solution.py:443
  68.3 2.9 %collective-permute-start.4 = (bf16[4,3,1152]{2,1,0:T(4,128)(2,1)S(1)}, bf16[4,3,1152]{2,1,0:T(4,128)(2,1)S(1)}, u32[]{:S(2)}, u32[]{:S(2)}) collective-permute-start(bf16[4,3,1152]{2,1,0:T(4,128)(2,1)S(1)} %get-tuple-element.50), channel_id=1, source_target_pairs={{0,2},{1,3},{2,4},{3,5},{4,6},{5,7},{6,8},{7,9},{8,10},{9,11},{10,... | collective-permute-start | bytes 82952 | tf_op jit(solution)/shard_map/ppermute | solution.py:444
  86.4 8.8 %collective-permute-start.7 = (bf16[32,64,128]{2,1,0:T(8,128)(2,1)S(1)}, bf16[32,64,128]{2,1,0:T(8,128)(2,1)S(1)}, u32[]{:S(2)}, u32[]{:S(2)}) collective-permute-start(bf16[32,64,128]{2,1,0:T(8,128)(2,1)S(1)} %all_to_all.16.refs_1_), channel_id=1, source_target_pairs={{0,2},{2,0},{1,3},{3,1},{4,6},{6,4},{5,7},{7,5},{8,10},{10,8},{9,1... | collective-permute-start | bytes 1572872 | tf_op jit(solution)/shard_map/ppermute | solution.py:475

commit v4 on v3

--- a/solution.py
+++ b/solution.py
@@ -65,8 +65,14 @@
     return (upward * cumulative, cumulative + upward * density)
 
 
-def bias_kernel(pos_ref, table_ref, *refs):
-    earth_ref, place_ref, rest_ref, pair_ref = refs[-4:]
+def bias_kernel(pos_ref, table_ref, gains_far, region_far, *refs):
+    earth_ref, gains_ref, region_ref, place_ref, rest_ref, pair_ref, arrived = refs[-7:]
+    fetched = [
+        pltpu.make_async_copy(far, near, arrived.at[n])
+        for n, (far, near) in enumerate(((gains_far, gains_ref), (region_far, region_ref)))
+    ]
+    for copy in fetched:
+        copy.start()
     tail = WIN - LANES
     pair_ref[...] = jnp.zeros_like(pair_ref)
     for n in range(HEADS // 2):
@@ -108,6 +114,8 @@
                 rest_ref[h, at : at + 8, lanes] = found[h]
     for h in range(HEADS):
         earth_ref[h, :, LANES:] = rest_ref[h, :, :WIN].T
+    for copy in fetched:
+        copy.wait()
 
 
 def scatter_kernel(pos_ref, score_ref, table_ref, place_ref, rest_ref):
@@ -185,7 +193,7 @@
         label_row = jnp.zeros((1, WIN), jnp.int32)
         label_col = jnp.zeros((WIN, 1), jnp.int32)
         for group in range(WIN_PL * WIN_LAT):
-            label = region_ref[group % WIN_LAT, w * WIN_PL + group // WIN_LAT]
+            label = region_ref[w * WIN_PL + group // WIN_LAT, group % WIN_LAT]
             label_row = jnp.where(group_row == group, label, label_row)
             label_col = jnp.where(group_col == group, label, label_col)
         same = label_row == label_col
@@ -294,8 +302,8 @@
 
 
 def finish_kernel(
-    factor, core_ref, mine_ref, came_ref, qkv_out, proj_out, up_out, down_out, gains_ref, bias_ref,
-    flat_ref, wide_ref, qkv_ref, proj_ref, up_ref, down_ref, done,
+    factor, core_ref, mine_ref, came_ref, qkv_ref, proj_ref, up_ref, down_ref, gains_ref, bias_ref,
+    flat_ref, wide_ref,
 ):
     core = core_ref[0]
     mine, came = mine_ref[...].astype(F32), came_ref[...].astype(F32)
@@ -308,23 +316,13 @@
         rows = slice(k % 9 * WIDTH, (k % 9 + 1) * WIDTH)
         return flat_ref[k // 9, rows, :]
 
-    def leave(n, ref, out):
-        copy = pltpu.make_async_copy(ref, out, done.at[n])
-        copy.start()
-        return copy
-
     for k in range(6):
-        up_ref[:, k * LANES : (k + 1) * LANES] = block(6 + k)
-    copies = [leave(0, up_ref, up_out)]
-    for k in range(6):
-        down_ref[:, k * LANES : (k + 1) * LANES] = block(12 + k)
-    copies.append(leave(1, down_ref, down_out))
-    for k in range(6):
-        wide_ref[:, k * LANES : (k + 1) * LANES] = block(k)
+        lanes = slice(k * LANES, (k + 1) * LANES)
+        wide_ref[:, lanes] = block(k)
+        up_ref[:, lanes] = block(6 + k)
+        down_ref[:, lanes] = block(12 + k)
     qkv_ref[...] = wide_ref[:, : 3 * WIDTH]
-    copies.append(leave(2, qkv_ref, qkv_out))
     proj_ref[...] = wide_ref[:, 3 * WIDTH :]
-    copies.append(leave(3, proj_ref, proj_out))
     gains = flat_ref[1, 9 * WIDTH :, :]
     for n in range(2):
         gains_ref[n : n + 1, :LANES] = gains[2 * n : 2 * n + 1]
@@ -336,8 +334,6 @@
             width = min(LANES, BIAS_POS - c * LANES)
             if width > 0:
                 bias_ref[h, :, c * LANES : c * LANES + width] = piece[r : r + 1, :width]
-    for copy in copies:
-        copy.wait()
 
 
 VMEM = pl.BlockSpec(memory_space=pltpu.VMEM)
@@ -345,7 +341,7 @@
 ANY = pl.BlockSpec(memory_space=pl.ANY)
 
 
-def kernel(function, name, outs, scratch=(), copies=0, scalars=0, later=0, outside=0, flops=1_000_000, moved=1_000_000):
+def kernel(function, name, outs, scratch=(), scalars=0, later=0, copies=0, flops=1_000_000, moved=1_000_000):
     shapes = tuple(jax.ShapeDtypeStruct(s, t) for s, t in outs)
 
     def call(*args):
@@ -353,7 +349,7 @@
             function,
             out_shape=shapes,
             in_specs=[SMEM] * scalars + [VMEM] * (len(args) - scalars - later) + [ANY] * later,
-            out_specs=(ANY,) * outside + (VMEM,) * (len(shapes) - outside),
+            out_specs=(VMEM,) * len(shapes),
             scratch_shapes=[pltpu.VMEM(s, t) for s, t in scratch] + [pltpu.SemaphoreType.DMA((copies,))] * (copies > 0),
             compiler_params=pltpu.CompilerParams(vmem_limit_bytes=48 * 1024 * 1024),
             cost_estimate=pl.CostEstimate(flops=flops, bytes_accessed=moved, transcendentals=0),
@@ -364,7 +360,15 @@
 
 
 REST = [((WIN - LANES, 2 * LANES), jnp.int32), ((HEADS, WIN - LANES, 2 * LANES), F32)]
-find_bias = kernel(bias_kernel, "find_bias", [((HEADS, WIN, WIN), F32)], REST + [((8, CHUNKS * LANES), jnp.int32)], later=5, flops=20_000_000)
+find_bias = kernel(
+    bias_kernel,
+    "find_bias",
+    [((HEADS, WIN, WIN), F32), ((2, WIDTH), F32), ((4, WIN_LAT), jnp.int32)],
+    REST + [((8, CHUNKS * LANES), jnp.int32)],
+    copies=2,
+    later=6,
+    flops=20_000_000,
+)
 spread_bias = kernel(
     scatter_kernel,
     "spread_bias",
@@ -404,11 +408,8 @@
             ((2, WIDTH), F32),
             ((HEADS, 1, BIAS_POS), F32),
         ],
-        [((2, HALF, LANES), F32), ((WIDTH, 4 * WIDTH), F32)]
-        + [((WIDTH, 3 * WIDTH), F32), ((WIDTH, WIDTH), F32), ((WIDTH, 4 * WIDTH), F32), ((WIDTH, 4 * WIDTH), F32)],
-        copies=4,
+        [((2, HALF, LANES), F32), ((WIDTH, 4 * WIDTH), F32)],
         scalars=1,
-        outside=4,
     )(core, mine, came)
 
 
@@ -454,13 +455,14 @@
 
 def body(states, cotangent, region, pos_index, w_qkv, w_proj, w_up, w_down, gains, earth_bias):
     levels, rows, merged = states.shape[1:]
-    weights = (gains, w_qkv, w_proj, w_up, w_down.T)
-    (earth,) = find_bias(pos_index, earth_bias.transpose(1, 0, 2), *weights)
+    weights = (w_qkv, w_proj, w_up, w_down.T)
+    far = [pltpu.with_memory_space_constraint(array, pltpu.HBM) for array in (gains, region.T)]
+    earth, gains, region = find_bias(pos_index, earth_bias.transpose(1, 0, 2), *far, *weights)
     pair = shifted(jnp.concatenate([states, cotangent], axis=0))
     cells = pair.reshape(2, CELLS, WIDTH)
     core = lax.axis_index("c").astype(jnp.int32).reshape(1)
     grad, send, keep, score = block_grads(
-        region, core, cells[0], cells[1], earth, *weights
+        region, core, cells[0], cells[1], earth, gains, *weights
     )
     came = lax.ppermute(send, "c", SWAP)
     grad = grad.reshape(levels, rows, merged)

time: 97.9 us -> 97.2 us (level)
  local copies, waits for them, and re-layouts: 4.13 us -> 2.72 us
    unnamed x21 -> x16, local copies, waits for them, and re-layouts: 3.11 us -> 1.7 us
  transfers between devices with their start and end apart: 9 -> 9, of which waited for: 4 -> 4; matrix products, arithmetic and copies ran while one was open for 1% -> 1% of each run, Pallas kernels for 5% -> 6%
where the time goes in v4:
time: 97.2 us; the launch traced here: 96.7 us
  starting transfers between devices  42.9 us (44%)
  blocking collectives  29.8 us (31%)
  Pallas kernels  14.1 us (15%)
  waiting for transfers between devices  5.92 us (6%)
  local copies, waits for them, and re-layouts  2.72 us (3%)
    all_to_all x2, blocking collectives, body(): plane = lax.all_to_all(plane, PLANE, 0, 0)  29.8 us
    pallas_call x7, Pallas kernels, call(): pl.pallas_call(function, out_shape=shapes, in_specs=[SMEM] * scalars + [V...  14.1 us
    ppermute x1, starting transfers between devices, shifted(): east = lax.ppermute(east, ALL, routes(-1, 0))  12.9 us
    ppermute x1, starting transfers between devices, body(): came = lax.ppermute(plane, 'c', SWAP)  7.27 us
    all_to_all x1, starting transfers between devices, body(): line = lax.all_to_all(line, 'far', 0, 0)  5.4 us
    ppermute x1, starting transfers between devices, sent_back(): east = lax.ppermute(east, ALL, routes(1, 0))  4.52 us
    ppermute x1, starting transfers between devices, sent_back(): corner = lax.ppermute(corner, ALL, routes(1, 1))  4.28 us
    ppermute x1, starting transfers between devices, shifted(): corner = lax.ppermute(corner, ALL, routes(-1, -1))  3.48 us
  transfers between devices with their start and end apart: 9, of which 4 were waited for; matrix products, arithmetic and copies ran while one was open for 1% of the time, Pallas kernels for 6%

profile of v4, /device:TPU:1, one launch (start us, length us, event | category | flops | bytes accessed | tf_op | source)
XLA Modules:
  0.0 96.7 jit_solution(8072988632422328908)
XLA Ops:
  0.6 1.0 %constant_dynamic-update-slice_fusion.1 = bf16[2,4,6,2304]{3,1,2,0:T(4,128)(2,1)S(1)} fusion(bf16[1,4,6,2304]{3,1,2,0:T(4,128)(2,1)} %param.10), kind=kLoop, calls=%fused_computation.20 | loop fusion | bytes 221184
  1.7 0.1 slice.63
  1.8 0.1 slice.62
  2.0 0.2 fusion.5
  2.2 12.9 %collective-permute-start = (bf16[2,4,3,1152]{3,1,2,0:T(4,128)(2,1)S(1)}, bf16[2,4,3,1152]{3,1,2,0:T(4,128)(2,1)S(1)}, u32[]{:S(2)}, u32[]{:S(2)}) collective-permute-start(bf16[2,4,3,1152]{3,1,2,0:T(4,128)(2,1)S(1)} %get-tuple-element.48), channel_id=1, source_target_pairs={{0,496},{1,497},{2,498},{3,499},{4,500},{5,501},{6,502},{7,503},{8... | collective-permute-start | bytes 165896 | tf_op jit(solution)/shard_map/ppermute | solution.py:432
  15.1 3.5 %collective-permute-start.2 = (bf16[2,4,3,1152]{3,1,2,0:T(4,128)(2,1)S(1)}, bf16[2,4,3,1152]{3,1,2,0:T(4,128)(2,1)S(1)}, u32[]{:S(2)}, u32[]{:S(2)}) collective-permute-start(bf16[2,4,3,1152]{3,1,2,0:T(4,128)(2,1)S(1)} %get-tuple-element.49), channel_id=1, source_target_pairs={{0,510},{1,511},{2,496},{3,497},{4,498},{5,499},{6,500},{7,501},{8... | collective-permute-start | bytes 165896 | tf_op jit(solution)/shard_map/ppermute | solution.py:431
  18.6 2.0 %collective-permute-start.1 = (bf16[2,4,3,1152]{3,1,2,0:T(4,128)(2,1)S(1)}, bf16[2,4,3,1152]{3,1,2,0:T(4,128)(2,1)S(1)}, u32[]{:S(2)}, u32[]{:S(2)}) collective-permute-start(bf16[2,4,3,1152]{3,1,2,0:T(4,128)(2,1)S(1)} %get-tuple-element.50), channel_id=1, source_target_pairs={{0,14},{1,15},{2,0},{3,1},{4,2},{5,3},{6,4},{7,5},{8,6},{9,7},{10,... | collective-permute-start | bytes 165896 | tf_op jit(solution)/shard_map/ppermute | solution.py:433
  20.6 2.9 %find_bias.1 = (f32[6,144,144]{2,1,0:T(8,128)S(1)}, f32[2,192]{1,0:T(2,128)S(1)}, s32[4,6]{1,0:T(4,128)S(1)}) custom-call(s32[144,144]{1,0:T(8,128)S(1)} %copy-done.3, f32[6,1,3312]{2,1,0:T(1,128)S(1)} %bitcast.10, f32[2,192]{1,0:T(2,128)} %gains_far.1, s32[4,6]{1,0:T(4,128)} %bitcast.11, bf16[192,576]{1,0:T(8,128)(2,1)S(1)} %copy-done.2, ...), custom_call_target="tpu_custom_call" | custom-call | flops 20000000 | bytes 1000000 | tf_op jit(solution)/shard_map/find_bias/pallas_call | solution.py:348
  23.6 0.1 maximum_maximum_fusion
  23.7 0.1 fusion.7
  23.8 0.2 squeeze.7.g_ref
  24.0 0.2 squeeze.6.x_ref
  24.2 6.1 %block_grads.1 = (bf16[288,192]{1,0:T(8,128)(2,1)S(1)}, bf16[1792,128]{1,0:T(8,128)(2,1)S(1)}, bf16[1792,128]{1,0:T(8,128)(2,1)S(1)}, f32[6,144,144]{2,1,0:T(8,128)S(1)}) custom-call(s32[4,6]{1,0:T(4,128)S(1)} %get-tuple-element.20.region_ref, s32[1]{0:T(128)} %bitcast.3.core_ref.refs_0_, bf16[288,192]{1,0:T(8,128)(2,1)S(1)} %squeeze.6.x_ref, ...), custom_call_target="tpu_custom_call" | custom-call | flops 1000000000 | bytes 4000000 | tf_op jit(solution)/shard_map/block_grads/pallas_call | solution.py:348
  30.3 3.0 %collective-permute-start.6 = (bf16[1792,128]{1,0:T(8,128)(2,1)S(1)}, bf16[1792,128]{1,0:T(8,128)(2,1)S(1)}, u32[]{:S(2)}, u32[]{:S(2)}) collective-permute-start(bf16[1792,128]{1,0:T(8,128)(2,1)S(1)} %get-tuple-element.25), channel_id=1, source_target_pairs={{0,2},{2,0},{1,3},{3,1},{4,6},{6,4},{5,7},{7,5},{8,10},{10,8},{9,1... | collective-permute-start | bytes 1376264 | tf_op jit(solution)/shard_map/ppermute | solution.py:467
  33.4 2.4 %spread_bias.1.table_ref = f32[192,128]{1,0:T(8,128)S(1)} custom-call(s32[144,144]{1,0:T(8,128)S(1)} %copy-done.3, f32[6,144,144]{2,1,0:T(8,128)S(1)} %get-tuple-element.26.score_ref), custom_call_target="tpu_custom_call" | custom-call | flops 1000000000 | bytes 1000000 | tf_op jit(solution)/shard_map/spread_bias/pallas_call | solution.py:348
  35.8 0.2 first_sum.1
  36.1 16.9 %all_to_all.15.came_ref = bf16[32,64,128]{2,1,0:T(8,128)(2,1)S(1)} all-to-all(bf16[32,64,128]{2,1,0:T(8,128)(2,1)S(1)} %first_sum.1), channel_id=1, replica_groups=mesh['x'=2,'far'=8,'pair'=2,'y'=4,'c'=2,'m'=2] {'x','m','y','pair'}, dimensions={0} | all-to-all | bytes 1048576 | tf_op jit(solution)/shard_map/all_to_all | solution.py:472
  53.0 0.8 second_sum.1
  53.8 5.4 %all-to-all-start.1 = ((bf16[8,80,128]{2,1,0:T(8,128)(2,1)}), bf16[8,80,128]{2,1,0:T(8,128)(2,1)S(1)}, u32[]{:S(2)}, u32[]{:S(2)}) async-start(bf16[8,80,128]{2,1,0:T(8,128)(2,1)} %second_sum.1), calls=%async_computation.1 | async-start | bytes 327680 | tf_op jit(solution)/shard_map/all_to_all | solution.py:474
  59.2 0.2 reshape.26
  59.5 4.3 %collective-permute-start.3 = (bf16[4,3,1152]{2,1,0:T(4,128)(2,1)S(1)}, bf16[4,3,1152]{2,1,0:T(4,128)(2,1)S(1)}, u32[]{:S(2)}, u32[]{:S(2)}) collective-permute-start(bf16[4,3,1152]{2,1,0:T(4,128)(2,1)S(1)} %get-tuple-element.53), channel_id=1, source_target_pairs={{0,18},{1,19},{2,20},{3,21},{4,22},{5,23},{6,24},{7,25},{8,26},{9,... | collective-permute-start | bytes 82952 | tf_op jit(solution)/shard_map/ppermute | solution.py:443
  63.7 4.5 %collective-permute-start.5 = (bf16[4,3,1152]{2,1,0:T(4,128)(2,1)S(1)}, bf16[4,3,1152]{2,1,0:T(4,128)(2,1)S(1)}, u32[]{:S(2)}, u32[]{:S(2)}) collective-permute-start(bf16[4,3,1152]{2,1,0:T(4,128)(2,1)S(1)} %get-tuple-element.55), channel_id=1, source_target_pairs={{0,16},{1,17},{2,18},{3,19},{4,20},{5,21},{6,22},{7,23},{8,24},{9,... | collective-permute-start | bytes 82952 | tf_op jit(solution)/shard_map/ppermute | solution.py:444
  68.3 1.8 %collective-permute-done.3.refs_0_ = bf16[4,3,1152]{2,1,0:T(4,128)(2,1)S(1)} collective-permute-done((bf16[4,3,1152]{2,1,0:T(4,128)(2,1)S(1)}, bf16[4,3,1152]{2,1,0:T(4,128)(2,1)S(1)}, u32[]{:S(2)}, u32[]{:S(2)}) %collective-permute-start.3) | collective-permute-done | bytes 27680 | tf_op jit(solution)/shard_map/ppermute | solution.py:443
  70.1 1.0 %collective-permute-done.5.refs_1_ = bf16[4,3,1152]{2,1,0:T(4,128)(2,1)S(1)} collective-permute-done((bf16[4,3,1152]{2,1,0:T(4,128)(2,1)S(1)}, bf16[4,3,1152]{2,1,0:T(4,128)(2,1)S(1)}, u32[]{:S(2)}, u32[]{:S(2)}) %collective-permute-start.5) | collective-permute-done | bytes 27680 | tf_op jit(solution)/shard_map/ppermute | solution.py:444
  71.2 2.3 %all-to-all-done.1.came_ref = bf16[8,80,128]{2,1,0:T(8,128)(2,1)S(1)} async-done(((bf16[8,80,128]{2,1,0:T(8,128)(2,1)}), bf16[8,80,128]{2,1,0:T(8,128)(2,1)S(1)}, u32[]{:S(2)}, u32[]{:S(2)}) %all-to-all-start.1) | async-done | bytes 163872 | tf_op jit(solution)/shard_map/all_to_all | solution.py:474
  73.5 0.1 fan.1
  73.6 12.8 %all_to_all.16.refs_1_ = bf16[32,64,128]{2,1,0:T(8,128)(2,1)S(1)} all-to-all(bf16[32,64,128]{2,1,0:T(8,128)(2,1)S(1)} %fan.1), channel_id=1, replica_groups=mesh['x'=2,'far'=8,'pair'=2,'y'=4,'c'=2,'m'=2] {'x','m','y','pair'}, dimensions={0} | all-to-all | bytes 1048576 | tf_op jit(solution)/shard_map/all_to_all | solution.py:476
  86.4 7.3 %collective-permute-start.7 = (bf16[32,64,128]{2,1,0:T(8,128)(2,1)S(1)}, bf16[32,64,128]{2,1,0:T(8,128)(2,1)S(1)}, u32[]{:S(2)}, u32[]{:S(2)}) collective-permute-start(bf16[32,64,128]{2,1,0:T(8,128)(2,1)S(1)} %all_to_all.16.refs_1_), channel_id=1, source_target_pairs={{0,2},{2,0},{1,3},{3,1},{4,6},{6,4},{5,7},{7,5},{8,10},{10,8},{9,1... | collective-permute-start | bytes 1572872 | tf_op jit(solution)/shard_map/ppermute | solution.py:477
  93.7 0.1 fusion.2
  93.7 0.7 copy.22
  94.4 0.7 collective-permute-done.7.refs_2_
  95.2 1.6 %finish.1 = (f32[192,576]{1,0:T(8,128)}, f32[192,192]{1,0:T(8,128)}, f32[192,768]{1,0:T(8,128)}, f32[192,768]{1,0:T(8,128)}, f32[2,192]{1,0:T(2,128)}, /*index=5*/f32[6,1,3312]{2,1,0:T(1,128)}) custom-call(s32[1]{0:T(128)} %bitcast.3.core_ref.refs_0_, bf16[32,64,128]{2,1,0:T(8,128)(2,1)S(1)} %all_to_all.16.refs_1_, ...), custom_call_target="tpu_custom_call" | custom-call | flops 1000000 | bytes 1000000 | tf_op jit(solution)/shard_map/finish/pallas_call | solution.py:348
  (24 shorter events, 0.2 us)
Async XLA Ops:
  0.6 1.0 %copy-start.6 = (bf16[1,4,6,2304]{3,1,2,0:T(4,128)(2,1)S(1)}, bf16[1,4,6,2304]{3,1,2,0:T(4,128)(2,1)}, u32[]{:S(2)}) copy-start(bf16[1,4,6,2304]{3,1,2,0:T(4,128)(2,1)} %param.11) | copy-start | bytes 331780
  1.7 18.9 %copy-start.4 = (bf16[192,192]{1,0:T(8,128)(2,1)S(1)}, bf16[192,192]{1,0:T(8,128)(2,1)}, u32[]{:S(2)}) copy-start(bf16[192,192]{1,0:T(8,128)(2,1)} %proj_ref.1) | copy-start | bytes 221188
  1.7 18.9 %copy-start.5 = (f32[1,6,3312]{2,0,1:T(1,128)S(1)}, f32[1,6,3312]{2,0,1:T(1,128)}, u32[]{:S(2)}) copy-start(f32[1,6,3312]{2,0,1:T(1,128)} %param.19) | copy-start | bytes 238468
  1.8 18.8 %copy-start.1 = (bf16[768,192]{0,1:T(8,128)(2,1)S(1)}, bf16[768,192]{0,1:T(8,128)(2,1)}, u32[]{:S(2)}) copy-start(bf16[768,192]{0,1:T(8,128)(2,1)} %param.17) | copy-start | bytes 884740
  1.8 18.8 %copy-start.3 = (s32[144,144]{1,0:T(8,128)S(1)}, s32[144,144]{1,0:T(8,128)}, u32[]{:S(2)}) copy-start(s32[144,144]{1,0:T(8,128)} %pos_ref.3) | copy-start | bytes 248836
  1.9 18.7 %copy-start = (bf16[192,768]{1,0:T(8,128)(2,1)S(1)}, bf16[192,768]{1,0:T(8,128)(2,1)}, u32[]{:S(2)}) copy-start(bf16[192,768]{1,0:T(8,128)(2,1)} %up_ref.1) | copy-start | bytes 884740
  2.0 18.7 %copy-start.2 = (bf16[192,576]{1,0:T(8,128)(2,1)S(1)}, bf16[192,576]{1,0:T(8,128)(2,1)}, u32[]{:S(2)}) copy-start(bf16[192,576]{1,0:T(8,128)(2,1)} %qkv_ref.1) | copy-start | bytes 663556
  2.2 21.3 %collective-permute-start = (bf16[2,4,3,1152]{3,1,2,0:T(4,128)(2,1)S(1)}, bf16[2,4,3,1152]{3,1,2,0:T(4,128)(2,1)S(1)}, u32[]{:S(2)}, u32[]{:S(2)}) collective-permute-start(bf16[2,4,3,1152]{3,1,2,0:T(4,128)(2,1)S(1)} %get-tuple-element.48), channel_id=1, source_target_pairs={{0,496},{1,497},{2,498},{3,499},{4,500},{5,501},{6,502},{7,503},{8... | collective-permute-start | bytes 165896 | tf_op jit(solution)/shard_map/ppermute | solution.py:432
  15.1 8.5 %collective-permute-start.2 = (bf16[2,4,3,1152]{3,1,2,0:T(4,128)(2,1)S(1)}, bf16[2,4,3,1152]{3,1,2,0:T(4,128)(2,1)S(1)}, u32[]{:S(2)}, u32[]{:S(2)}) collective-permute-start(bf16[2,4,3,1152]{3,1,2,0:T(4,128)(2,1)S(1)} %get-tuple-element.49), channel_id=1, source_target_pairs={{0,510},{1,511},{2,496},{3,497},{4,498},{5,499},{6,500},{7,501},{8... | collective-permute-start | bytes 165896 | tf_op jit(solution)/shard_map/ppermute | solution.py:431
  18.6 5.0 %collective-permute-start.1 = (bf16[2,4,3,1152]{3,1,2,0:T(4,128)(2,1)S(1)}, bf16[2,4,3,1152]{3,1,2,0:T(4,128)(2,1)S(1)}, u32[]{:S(2)}, u32[]{:S(2)}) collective-permute-start(bf16[2,4,3,1152]{3,1,2,0:T(4,128)(2,1)S(1)} %get-tuple-element.50), channel_id=1, source_target_pairs={{0,14},{1,15},{2,0},{3,1},{4,2},{5,3},{6,4},{7,5},{8,6},{9,7},{10,... | collective-permute-start | bytes 165896 | tf_op jit(solution)/shard_map/ppermute | solution.py:433
  30.3 5.5 %collective-permute-start.6 = (bf16[1792,128]{1,0:T(8,128)(2,1)S(1)}, bf16[1792,128]{1,0:T(8,128)(2,1)S(1)}, u32[]{:S(2)}, u32[]{:S(2)}) collective-permute-start(bf16[1792,128]{1,0:T(8,128)(2,1)S(1)} %get-tuple-element.25), channel_id=1, source_target_pairs={{0,2},{2,0},{1,3},{3,1},{4,6},{6,4},{5,7},{7,5},{8,10},{10,8},{9,1... | collective-permute-start | bytes 1376264 | tf_op jit(solution)/shard_map/ppermute | solution.py:467
  53.8 19.7 %all-to-all-start.1 = ((bf16[8,80,128]{2,1,0:T(8,128)(2,1)}), bf16[8,80,128]{2,1,0:T(8,128)(2,1)S(1)}, u32[]{:S(2)}, u32[]{:S(2)}) async-start(bf16[8,80,128]{2,1,0:T(8,128)(2,1)} %second_sum.1), calls=%async_computation.1 | async-start | bytes 327680 | tf_op jit(solution)/shard_map/all_to_all | solution.py:474
  59.5 10.7 %collective-permute-start.3 = (bf16[4,3,1152]{2,1,0:T(4,128)(2,1)S(1)}, bf16[4,3,1152]{2,1,0:T(4,128)(2,1)S(1)}, u32[]{:S(2)}, u32[]{:S(2)}) collective-permute-start(bf16[4,3,1152]{2,1,0:T(4,128)(2,1)S(1)} %get-tuple-element.53), channel_id=1, source_target_pairs={{0,18},{1,19},{2,20},{3,21},{4,22},{5,23},{6,24},{7,25},{8,26},{9,... | collective-permute-start | bytes 82952 | tf_op jit(solution)/shard_map/ppermute | solution.py:443
  63.7 7.4 %collective-permute-start.5 = (bf16[4,3,1152]{2,1,0:T(4,128)(2,1)S(1)}, bf16[4,3,1152]{2,1,0:T(4,128)(2,1)S(1)}, u32[]{:S(2)}, u32[]{:S(2)}) collective-permute-start(bf16[4,3,1152]{2,1,0:T(4,128)(2,1)S(1)} %get-tuple-element.55), channel_id=1, source_target_pairs={{0,16},{1,17},{2,18},{3,19},{4,20},{5,21},{6,22},{7,23},{8,24},{9,... | collective-permute-start | bytes 82952 | tf_op jit(solution)/shard_map/ppermute | solution.py:444
  68.3 2.9 %collective-permute-start.4 = (bf16[4,3,1152]{2,1,0:T(4,128)(2,1)S(1)}, bf16[4,3,1152]{2,1,0:T(4,128)(2,1)S(1)}, u32[]{:S(2)}, u32[]{:S(2)}) collective-permute-start(bf16[4,3,1152]{2,1,0:T(4,128)(2,1)S(1)} %get-tuple-element.56), channel_id=1, source_target_pairs={{0,2},{1,3},{2,4},{3,5},{4,6},{5,7},{6,8},{7,9},{8,10},{9,11},{10,... | collective-permute-start | bytes 82952 | tf_op jit(solution)/shard_map/ppermute | solution.py:445
  86.4 8.8 %collective-permute-start.7 = (bf16[32,64,128]{2,1,0:T(8,128)(2,1)S(1)}, bf16[32,64,128]{2,1,0:T(8,128)(2,1)S(1)}, u32[]{:S(2)}, u32[]{:S(2)}) collective-permute-start(bf16[32,64,128]{2,1,0:T(8,128)(2,1)S(1)} %all_to_all.16.refs_1_), channel_id=1, source_target_pairs={{0,2},{2,0},{1,3},{3,1},{4,6},{6,4},{5,7},{7,5},{8,10},{10,8},{9,1... | collective-permute-start | bytes 1572872 | tf_op jit(solution)/shard_map/ppermute | solution.py:477

commit v5 on v4

--- a/solution.py
+++ b/solution.py
@@ -103,7 +103,7 @@
             earth_ref[h, rows, :LANES] = found[h]
         return carry
 
-    lax.fori_loop(0, WIN // 8, eight_rows, 0, unroll=2)
+    lax.fori_loop(0, WIN // 8, eight_rows, 0, unroll=18)
     place_ref[...] = jnp.zeros_like(place_ref)
     place_ref[:, :WIN] = pos_ref[:, LANES:].T
     for at in range(0, tail, 8):
@@ -302,28 +302,35 @@
 
 
 def finish_kernel(
-    factor, core_ref, mine_ref, came_ref, qkv_ref, proj_ref, up_ref, down_ref, gains_ref, bias_ref,
-    flat_ref, wide_ref,
+    factor, core_ref, mine_ref, came_ref, qkv_ref, proj_ref, up_ref, down_ref, gains_ref, bias_ref
 ):
-    core = core_ref[0]
     mine, came = mine_ref[...].astype(F32), came_ref[...].astype(F32)
-    for p in range(NEAR):
-        rows = slice(p * PIECE, (p + 1) * PIECE)
-        flat_ref[core, rows, :] = mine[p, :PIECE] * factor
-        flat_ref[1 - core, rows, :] = came[p, :PIECE] * factor
-
-    def block(k):
-        rows = slice(k % 9 * WIDTH, (k % 9 + 1) * WIDTH)
-        return flat_ref[k // 9, rows, :]
-
-    for k in range(6):
-        lanes = slice(k * LANES, (k + 1) * LANES)
-        wide_ref[:, lanes] = block(k)
-        up_ref[:, lanes] = block(6 + k)
-        down_ref[:, lanes] = block(12 + k)
-    qkv_ref[...] = wide_ref[:, : 3 * WIDTH]
-    proj_ref[...] = wide_ref[:, 3 * WIDTH :]
-    gains = flat_ref[1, 9 * WIDTH :, :]
+    first = (jnp.zeros((1, 1, 1), jnp.int32) + core_ref[0]) == 0
+    halves = [jnp.where(first, mine, came) * factor, jnp.where(first, came, mine) * factor]
+
+    def put(block, rows, lines):
+        if block >= 6:
+            ref, at = (up_ref, down_ref)[block // 12], block % 6 * LANES
+            ref[rows, at : at + LANES] = lines
+        elif block < 4:
+            qkv_ref[rows, block * LANES : (block + 1) * LANES] = lines
+        elif block == 4:
+            qkv_ref[rows, 4 * LANES :] = lines[:, : LANES // 2]
+            proj_ref[rows, : LANES // 2] = lines[:, LANES // 2 :]
+        else:
+            proj_ref[rows, LANES // 2 :] = lines
+
+    for half in range(2):
+        for p in range(NEAR):
+            lines = halves[half][p, :PIECE]
+            at = 0
+            while at < PIECE and p * PIECE + at < 9 * WIDTH:
+                block, row = divmod(p * PIECE + at, WIDTH)
+                count = min(PIECE - at, WIDTH - row)
+                put(half * 9 + block, slice(row, row + count), lines[at : at + count])
+                at += count
+    p, at = divmod(9 * WIDTH, PIECE)
+    gains = halves[1][p, at : at + 8]
     for n in range(2):
         gains_ref[n : n + 1, :LANES] = gains[2 * n : 2 * n + 1]
         gains_ref[n : n + 1, LANES:] = gains[2 * n + 1 : 2 * n + 2, : WIDTH - LANES]
@@ -408,7 +415,6 @@
             ((2, WIDTH), F32),
             ((HEADS, 1, BIAS_POS), F32),
         ],
-        [((2, HALF, LANES), F32), ((WIDTH, 4 * WIDTH), F32)],
         scalars=1,
     )(core, mine, came)
 

time: 97.2 us -> 97.1 us (level)
  transfers between devices with their start and end apart: 9 -> 9, of which waited for: 4 -> 4; matrix products, arithmetic and copies ran while one was open for 1% -> 1% of each run, Pallas kernels for 6% -> 5%
where the time goes in v5:
time: 97.1 us; the launch traced here: 96.6 us
  starting transfers between devices  42.9 us (44%)
  blocking collectives  30.5 us (31%)
  Pallas kernels  13.2 us (14%)
  waiting for transfers between devices  5.92 us (6%)
  local copies, waits for them, and re-layouts  2.72 us (3%)
    all_to_all x2, blocking collectives, body(): plane = lax.all_to_all(plane, PLANE, 0, 0)  30.5 us
    pallas_call x7, Pallas kernels, call(): pl.pallas_call(function, out_shape=shapes, in_specs=[SMEM] * scalars + [V...  13.2 us
    ppermute x1, starting transfers between devices, shifted(): east = lax.ppermute(east, ALL, routes(-1, 0))  12.9 us
    ppermute x1, starting transfers between devices, body(): came = lax.ppermute(plane, 'c', SWAP)  7.27 us
    all_to_all x1, starting transfers between devices, body(): line = lax.all_to_all(line, 'far', 0, 0)  5.4 us
    ppermute x1, starting transfers between devices, sent_back(): east = lax.ppermute(east, ALL, routes(1, 0))  4.52 us
    ppermute x1, starting transfers between devices, sent_back(): corner = lax.ppermute(corner, ALL, routes(1, 1))  4.28 us
    ppermute x1, starting transfers between devices, shifted(): corner = lax.ppermute(corner, ALL, routes(-1, -1))  3.48 us
  transfers between devices with their start and end apart: 9, of which 4 were waited for; matrix products, arithmetic and copies ran while one was open for 1% of the time, Pallas kernels for 5%

profile of v5, /device:TPU:1, one launch (start us, length us, event | category | flops | bytes accessed | tf_op | source)
XLA Modules:
  0.0 96.6 jit_solution(6789558916220449533)
XLA Ops:
  0.6 1.0 %constant_dynamic-update-slice_fusion.1 = bf16[2,4,6,2304]{3,1,2,0:T(4,128)(2,1)S(1)} fusion(bf16[1,4,6,2304]{3,1,2,0:T(4,128)(2,1)} %param.10), kind=kLoop, calls=%fused_computation.20 | loop fusion | bytes 221184
  1.7 0.1 slice.63
  1.8 0.1 slice.62
  2.0 0.2 fusion.5
  2.2 12.9 %collective-permute-start = (bf16[2,4,3,1152]{3,1,2,0:T(4,128)(2,1)S(1)}, bf16[2,4,3,1152]{3,1,2,0:T(4,128)(2,1)S(1)}, u32[]{:S(2)}, u32[]{:S(2)}) collective-permute-start(bf16[2,4,3,1152]{3,1,2,0:T(4,128)(2,1)S(1)} %get-tuple-element.48), channel_id=1, source_target_pairs={{0,496},{1,497},{2,498},{3,499},{4,500},{5,501},{6,502},{7,503},{8... | collective-permute-start | bytes 165896 | tf_op jit(solution)/shard_map/ppermute | solution.py:438
  15.1 3.5 %collective-permute-start.2 = (bf16[2,4,3,1152]{3,1,2,0:T(4,128)(2,1)S(1)}, bf16[2,4,3,1152]{3,1,2,0:T(4,128)(2,1)S(1)}, u32[]{:S(2)}, u32[]{:S(2)}) collective-permute-start(bf16[2,4,3,1152]{3,1,2,0:T(4,128)(2,1)S(1)} %get-tuple-element.49), channel_id=1, source_target_pairs={{0,510},{1,511},{2,496},{3,497},{4,498},{5,499},{6,500},{7,501},{8... | collective-permute-start | bytes 165896 | tf_op jit(solution)/shard_map/ppermute | solution.py:437
  18.6 2.0 %collective-permute-start.1 = (bf16[2,4,3,1152]{3,1,2,0:T(4,128)(2,1)S(1)}, bf16[2,4,3,1152]{3,1,2,0:T(4,128)(2,1)S(1)}, u32[]{:S(2)}, u32[]{:S(2)}) collective-permute-start(bf16[2,4,3,1152]{3,1,2,0:T(4,128)(2,1)S(1)} %get-tuple-element.50), channel_id=1, source_target_pairs={{0,14},{1,15},{2,0},{3,1},{4,2},{5,3},{6,4},{7,5},{8,6},{9,7},{10,... | collective-permute-start | bytes 165896 | tf_op jit(solution)/shard_map/ppermute | solution.py:439
  20.6 2.2 %find_bias.1 = (f32[6,144,144]{2,1,0:T(8,128)S(1)}, f32[2,192]{1,0:T(2,128)S(1)}, s32[4,6]{1,0:T(4,128)S(1)}) custom-call(s32[144,144]{1,0:T(8,128)S(1)} %copy-done.3, f32[6,1,3312]{2,1,0:T(1,128)S(1)} %bitcast.10, f32[2,192]{1,0:T(2,128)} %gains_far.1, s32[4,6]{1,0:T(4,128)} %bitcast.11, bf16[192,576]{1,0:T(8,128)(2,1)S(1)} %copy-done.2, ...), custom_call_target="tpu_custom_call" | custom-call | flops 20000000 | bytes 1000000 | tf_op jit(solution)/shard_map/find_bias/pallas_call | solution.py:355
  22.8 0.1 maximum_maximum_fusion
  22.9 0.1 fusion.7
  23.1 0.2 squeeze.7.g_ref
  23.3 0.2 squeeze.6.x_ref
  23.5 6.1 %block_grads.1 = (bf16[288,192]{1,0:T(8,128)(2,1)S(1)}, bf16[1792,128]{1,0:T(8,128)(2,1)S(1)}, bf16[1792,128]{1,0:T(8,128)(2,1)S(1)}, f32[6,144,144]{2,1,0:T(8,128)S(1)}) custom-call(s32[4,6]{1,0:T(4,128)S(1)} %get-tuple-element.20.region_ref, s32[1]{0:T(128)} %bitcast.3.core_ref.refs_0_, bf16[288,192]{1,0:T(8,128)(2,1)S(1)} %squeeze.6.x_ref, ...), custom_call_target="tpu_custom_call" | custom-call | flops 1000000000 | bytes 4000000 | tf_op jit(solution)/shard_map/block_grads/pallas_call | solution.py:355
  29.6 3.0 %collective-permute-start.6 = (bf16[1792,128]{1,0:T(8,128)(2,1)S(1)}, bf16[1792,128]{1,0:T(8,128)(2,1)S(1)}, u32[]{:S(2)}, u32[]{:S(2)}) collective-permute-start(bf16[1792,128]{1,0:T(8,128)(2,1)S(1)} %get-tuple-element.25), channel_id=1, source_target_pairs={{0,2},{2,0},{1,3},{3,1},{4,6},{6,4},{5,7},{7,5},{8,10},{10,8},{9,1... | collective-permute-start | bytes 1376264 | tf_op jit(solution)/shard_map/ppermute | solution.py:473
  32.6 2.4 %spread_bias.1.table_ref = f32[192,128]{1,0:T(8,128)S(1)} custom-call(s32[144,144]{1,0:T(8,128)S(1)} %copy-done.3, f32[6,144,144]{2,1,0:T(8,128)S(1)} %get-tuple-element.26.score_ref), custom_call_target="tpu_custom_call" | custom-call | flops 1000000000 | bytes 1000000 | tf_op jit(solution)/shard_map/spread_bias/pallas_call | solution.py:355
  35.1 0.2 first_sum.1
  35.4 17.7 %all_to_all.15.came_ref = bf16[32,64,128]{2,1,0:T(8,128)(2,1)S(1)} all-to-all(bf16[32,64,128]{2,1,0:T(8,128)(2,1)S(1)} %first_sum.1), channel_id=1, replica_groups=mesh['x'=2,'far'=8,'pair'=2,'y'=4,'c'=2,'m'=2] {'x','m','y','pair'}, dimensions={0} | all-to-all | bytes 1048576 | tf_op jit(solution)/shard_map/all_to_all | solution.py:478
  53.0 0.8 second_sum.1
  53.8 5.4 %all-to-all-start.1 = ((bf16[8,80,128]{2,1,0:T(8,128)(2,1)}), bf16[8,80,128]{2,1,0:T(8,128)(2,1)S(1)}, u32[]{:S(2)}, u32[]{:S(2)}) async-start(bf16[8,80,128]{2,1,0:T(8,128)(2,1)} %second_sum.1), calls=%async_computation.1 | async-start | bytes 327680 | tf_op jit(solution)/shard_map/all_to_all | solution.py:480
  59.2 0.2 reshape.26
  59.5 4.3 %collective-permute-start.3 = (bf16[4,3,1152]{2,1,0:T(4,128)(2,1)S(1)}, bf16[4,3,1152]{2,1,0:T(4,128)(2,1)S(1)}, u32[]{:S(2)}, u32[]{:S(2)}) collective-permute-start(bf16[4,3,1152]{2,1,0:T(4,128)(2,1)S(1)} %get-tuple-element.53), channel_id=1, source_target_pairs={{0,18},{1,19},{2,20},{3,21},{4,22},{5,23},{6,24},{7,25},{8,26},{9,... | collective-permute-start | bytes 82952 | tf_op jit(solution)/shard_map/ppermute | solution.py:449
  63.7 4.5 %collective-permute-start.5 = (bf16[4,3,1152]{2,1,0:T(4,128)(2,1)S(1)}, bf16[4,3,1152]{2,1,0:T(4,128)(2,1)S(1)}, u32[]{:S(2)}, u32[]{:S(2)}) collective-permute-start(bf16[4,3,1152]{2,1,0:T(4,128)(2,1)S(1)} %get-tuple-element.55), channel_id=1, source_target_pairs={{0,16},{1,17},{2,18},{3,19},{4,20},{5,21},{6,22},{7,23},{8,24},{9,... | collective-permute-start | bytes 82952 | tf_op jit(solution)/shard_map/ppermute | solution.py:450
  68.3 1.8 %collective-permute-done.3.refs_0_ = bf16[4,3,1152]{2,1,0:T(4,128)(2,1)S(1)} collective-permute-done((bf16[4,3,1152]{2,1,0:T(4,128)(2,1)S(1)}, bf16[4,3,1152]{2,1,0:T(4,128)(2,1)S(1)}, u32[]{:S(2)}, u32[]{:S(2)}) %collective-permute-start.3) | collective-permute-done | bytes 27680 | tf_op jit(solution)/shard_map/ppermute | solution.py:449
  70.1 1.0 %collective-permute-done.5.refs_1_ = bf16[4,3,1152]{2,1,0:T(4,128)(2,1)S(1)} collective-permute-done((bf16[4,3,1152]{2,1,0:T(4,128)(2,1)S(1)}, bf16[4,3,1152]{2,1,0:T(4,128)(2,1)S(1)}, u32[]{:S(2)}, u32[]{:S(2)}) %collective-permute-start.5) | collective-permute-done | bytes 27680 | tf_op jit(solution)/shard_map/ppermute | solution.py:450
  71.2 2.3 %all-to-all-done.1.came_ref = bf16[8,80,128]{2,1,0:T(8,128)(2,1)S(1)} async-done(((bf16[8,80,128]{2,1,0:T(8,128)(2,1)}), bf16[8,80,128]{2,1,0:T(8,128)(2,1)S(1)}, u32[]{:S(2)}, u32[]{:S(2)}) %all-to-all-start.1) | async-done | bytes 163872 | tf_op jit(solution)/shard_map/all_to_all | solution.py:480
  73.5 0.1 fan.1
  73.6 12.8 %all_to_all.16.refs_1_ = bf16[32,64,128]{2,1,0:T(8,128)(2,1)S(1)} all-to-all(bf16[32,64,128]{2,1,0:T(8,128)(2,1)S(1)} %fan.1), channel_id=1, replica_groups=mesh['x'=2,'far'=8,'pair'=2,'y'=4,'c'=2,'m'=2] {'x','m','y','pair'}, dimensions={0} | all-to-all | bytes 1048576 | tf_op jit(solution)/shard_map/all_to_all | solution.py:482
  86.4 7.3 %collective-permute-start.7 = (bf16[32,64,128]{2,1,0:T(8,128)(2,1)S(1)}, bf16[32,64,128]{2,1,0:T(8,128)(2,1)S(1)}, u32[]{:S(2)}, u32[]{:S(2)}) collective-permute-start(bf16[32,64,128]{2,1,0:T(8,128)(2,1)S(1)} %all_to_all.16.refs_1_), channel_id=1, source_target_pairs={{0,2},{2,0},{1,3},{3,1},{4,6},{6,4},{5,7},{7,5},{8,10},{10,8},{9,1... | collective-permute-start | bytes 1572872 | tf_op jit(solution)/shard_map/ppermute | solution.py:483
  93.7 0.1 fusion.2
  93.7 0.7 copy.22
  94.4 0.7 collective-permute-done.7.refs_2_
  95.2 1.5 %finish.1 = (f32[192,576]{1,0:T(8,128)}, f32[192,192]{1,0:T(8,128)}, f32[192,768]{1,0:T(8,128)}, f32[192,768]{1,0:T(8,128)}, f32[2,192]{1,0:T(2,128)}, /*index=5*/f32[6,1,3312]{2,1,0:T(1,128)}) custom-call(s32[1]{0:T(128)} %bitcast.3.core_ref.refs_0_, bf16[32,64,128]{2,1,0:T(8,128)(2,1)S(1)} %all_to_all.16.refs_1_, ...), custom_call_target="tpu_custom_call" | custom-call | flops 1000000 | bytes 1000000 | tf_op jit(solution)/shard_map/finish/pallas_call | solution.py:355
  (24 shorter events, 0.2 us)
Async XLA Ops:
  0.6 1.0 %copy-start.6 = (bf16[1,4,6,2304]{3,1,2,0:T(4,128)(2,1)S(1)}, bf16[1,4,6,2304]{3,1,2,0:T(4,128)(2,1)}, u32[]{:S(2)}) copy-start(bf16[1,4,6,2304]{3,1,2,0:T(4,128)(2,1)} %param.11) | copy-start | bytes 331780
  1.7 18.9 %copy-start.4 = (bf16[192,192]{1,0:T(8,128)(2,1)S(1)}, bf16[192,192]{1,0:T(8,128)(2,1)}, u32[]{:S(2)}) copy-start(bf16[192,192]{1,0:T(8,128)(2,1)} %proj_ref.1) | copy-start | bytes 221188
  1.7 18.9 %copy-start.5 = (f32[1,6,3312]{2,0,1:T(1,128)S(1)}, f32[1,6,3312]{2,0,1:T(1,128)}, u32[]{:S(2)}) copy-start(f32[1,6,3312]{2,0,1:T(1,128)} %param.19) | copy-start | bytes 238468
  1.8 18.8 %copy-start.1 = (bf16[768,192]{0,1:T(8,128)(2,1)S(1)}, bf16[768,192]{0,1:T(8,128)(2,1)}, u32[]{:S(2)}) copy-start(bf16[768,192]{0,1:T(8,128)(2,1)} %param.17) | copy-start | bytes 884740
  1.8 18.8 %copy-start.3 = (s32[144,144]{1,0:T(8,128)S(1)}, s32[144,144]{1,0:T(8,128)}, u32[]{:S(2)}) copy-start(s32[144,144]{1,0:T(8,128)} %pos_ref.3) | copy-start | bytes 248836
  1.9 18.7 %copy-start = (bf16[192,768]{1,0:T(8,128)(2,1)S(1)}, bf16[192,768]{1,0:T(8,128)(2,1)}, u32[]{:S(2)}) copy-start(bf16[192,768]{1,0:T(8,128)(2,1)} %up_ref.1) | copy-start | bytes 884740
  2.0 18.7 %copy-start.2 = (bf16[192,576]{1,0:T(8,128)(2,1)S(1)}, bf16[192,576]{1,0:T(8,128)(2,1)}, u32[]{:S(2)}) copy-start(bf16[192,576]{1,0:T(8,128)(2,1)} %qkv_ref.1) | copy-start | bytes 663556
  2.2 20.6 %collective-permute-start = (bf16[2,4,3,1152]{3,1,2,0:T(4,128)(2,1)S(1)}, bf16[2,4,3,1152]{3,1,2,0:T(4,128)(2,1)S(1)}, u32[]{:S(2)}, u32[]{:S(2)}) collective-permute-start(bf16[2,4,3,1152]{3,1,2,0:T(4,128)(2,1)S(1)} %get-tuple-element.48), channel_id=1, source_target_pairs={{0,496},{1,497},{2,498},{3,499},{4,500},{5,501},{6,502},{7,503},{8... | collective-permute-start | bytes 165896 | tf_op jit(solution)/shard_map/ppermute | solution.py:438
  15.1 7.7 %collective-permute-start.2 = (bf16[2,4,3,1152]{3,1,2,0:T(4,128)(2,1)S(1)}, bf16[2,4,3,1152]{3,1,2,0:T(4,128)(2,1)S(1)}, u32[]{:S(2)}, u32[]{:S(2)}) collective-permute-start(bf16[2,4,3,1152]{3,1,2,0:T(4,128)(2,1)S(1)} %get-tuple-element.49), channel_id=1, source_target_pairs={{0,510},{1,511},{2,496},{3,497},{4,498},{5,499},{6,500},{7,501},{8... | collective-permute-start | bytes 165896 | tf_op jit(solution)/shard_map/ppermute | solution.py:437
  18.6 4.2 %collective-permute-start.1 = (bf16[2,4,3,1152]{3,1,2,0:T(4,128)(2,1)S(1)}, bf16[2,4,3,1152]{3,1,2,0:T(4,128)(2,1)S(1)}, u32[]{:S(2)}, u32[]{:S(2)}) collective-permute-start(bf16[2,4,3,1152]{3,1,2,0:T(4,128)(2,1)S(1)} %get-tuple-element.50), channel_id=1, source_target_pairs={{0,14},{1,15},{2,0},{3,1},{4,2},{5,3},{6,4},{7,5},{8,6},{9,7},{10,... | collective-permute-start | bytes 165896 | tf_op jit(solution)/shard_map/ppermute | solution.py:439
  29.6 5.5 %collective-permute-start.6 = (bf16[1792,128]{1,0:T(8,128)(2,1)S(1)}, bf16[1792,128]{1,0:T(8,128)(2,1)S(1)}, u32[]{:S(2)}, u32[]{:S(2)}) collective-permute-start(bf16[1792,128]{1,0:T(8,128)(2,1)S(1)} %get-tuple-element.25), channel_id=1, source_target_pairs={{0,2},{2,0},{1,3},{3,1},{4,6},{6,4},{5,7},{7,5},{8,10},{10,8},{9,1... | collective-permute-start | bytes 1376264 | tf_op jit(solution)/shard_map/ppermute | solution.py:473
  53.8 19.7 %all-to-all-start.1 = ((bf16[8,80,128]{2,1,0:T(8,128)(2,1)}), bf16[8,80,128]{2,1,0:T(8,128)(2,1)S(1)}, u32[]{:S(2)}, u32[]{:S(2)}) async-start(bf16[8,80,128]{2,1,0:T(8,128)(2,1)} %second_sum.1), calls=%async_computation.1 | async-start | bytes 327680 | tf_op jit(solution)/shard_map/all_to_all | solution.py:480
  59.5 10.7 %collective-permute-start.3 = (bf16[4,3,1152]{2,1,0:T(4,128)(2,1)S(1)}, bf16[4,3,1152]{2,1,0:T(4,128)(2,1)S(1)}, u32[]{:S(2)}, u32[]{:S(2)}) collective-permute-start(bf16[4,3,1152]{2,1,0:T(4,128)(2,1)S(1)} %get-tuple-element.53), channel_id=1, source_target_pairs={{0,18},{1,19},{2,20},{3,21},{4,22},{5,23},{6,24},{7,25},{8,26},{9,... | collective-permute-start | bytes 82952 | tf_op jit(solution)/shard_map/ppermute | solution.py:449
  63.7 7.4 %collective-permute-start.5 = (bf16[4,3,1152]{2,1,0:T(4,128)(2,1)S(1)}, bf16[4,3,1152]{2,1,0:T(4,128)(2,1)S(1)}, u32[]{:S(2)}, u32[]{:S(2)}) collective-permute-start(bf16[4,3,1152]{2,1,0:T(4,128)(2,1)S(1)} %get-tuple-element.55), channel_id=1, source_target_pairs={{0,16},{1,17},{2,18},{3,19},{4,20},{5,21},{6,22},{7,23},{8,24},{9,... | collective-permute-start | bytes 82952 | tf_op jit(solution)/shard_map/ppermute | solution.py:450
  68.3 2.9 %collective-permute-start.4 = (bf16[4,3,1152]{2,1,0:T(4,128)(2,1)S(1)}, bf16[4,3,1152]{2,1,0:T(4,128)(2,1)S(1)}, u32[]{:S(2)}, u32[]{:S(2)}) collective-permute-start(bf16[4,3,1152]{2,1,0:T(4,128)(2,1)S(1)} %get-tuple-element.56), channel_id=1, source_target_pairs={{0,2},{1,3},{2,4},{3,5},{4,6},{5,7},{6,8},{7,9},{8,10},{9,11},{10,... | collective-permute-start | bytes 82952 | tf_op jit(solution)/shard_map/ppermute | solution.py:451
  86.4 8.8 %collective-permute-start.7 = (bf16[32,64,128]{2,1,0:T(8,128)(2,1)S(1)}, bf16[32,64,128]{2,1,0:T(8,128)(2,1)S(1)}, u32[]{:S(2)}, u32[]{:S(2)}) collective-permute-start(bf16[32,64,128]{2,1,0:T(8,128)(2,1)S(1)} %all_to_all.16.refs_1_), channel_id=1, source_target_pairs={{0,2},{2,0},{1,3},{3,1},{4,6},{6,4},{5,7},{7,5},{8,10},{10,8},{9,1... | collective-permute-start | bytes 1572872 | tf_op jit(solution)/shard_map/ppermute | solution.py:483

commit v6 on v5

--- a/solution.py
+++ b/solution.py
@@ -65,12 +65,9 @@
     return (upward * cumulative, cumulative + upward * density)
 
 
-def bias_kernel(pos_ref, table_ref, gains_far, region_far, *refs):
-    earth_ref, gains_ref, region_ref, place_ref, rest_ref, pair_ref, arrived = refs[-7:]
-    fetched = [
-        pltpu.make_async_copy(far, near, arrived.at[n])
-        for n, (far, near) in enumerate(((gains_far, gains_ref), (region_far, region_ref)))
-    ]
+def bias_kernel(pos_ref, table_ref, *refs):
+    (earth_ref, *near), (place_ref, rest_ref, pair_ref, arrived) = refs[6:13], refs[13:]
+    fetched = [pltpu.make_async_copy(refs[n], near[n], arrived.at[n]) for n in range(6)]
     for copy in fetched:
         copy.start()
     tail = WIN - LANES
@@ -158,12 +155,16 @@
 
 
 def block_kernel(
-    region_ref, core_ref, x_ref, g_ref, earth_ref, gains_ref, qkv_ref, proj_ref, up_ref, down_ref,
+    region_ref, core_ref, cells_ref, earth_ref, gains_ref, qkv_ref, proj_ref, up_ref, down_ref,
     grad_ref, send_ref, keep_ref, score_ref, triple_ref, wide_ref, gain_ref,
 ):
     scale = SIZE ** (-0.5)
-    x = x_ref[...].astype(F32)
-    g_low = g_ref[...]
+    level = CELLS // 4
+    x, g = [
+        jnp.concatenate([part[level:], part[:level]], axis=0)
+        for part in (cells_ref[0].astype(F32), cells_ref[1].astype(F32))
+    ]
+    g_low = g.astype(BF)
     gain_a, gain_b = gains_ref[0:1, :], gains_ref[1:2, :]
     normed_one, recip_one, scaled_one = layer_norm(x, gain_a)
     hidden_one = scaled_one.astype(BF)
@@ -220,7 +221,7 @@
     gain_ref[2:3, :] = gain[:, :LANES]
     gain_ref[3:4, : WIDTH - LANES] = gain[:, LANES:]
     grad_resid = (
-        g_low.astype(F32) + norm_back(grad_hid_two, normed_two, recip_two, gain_b)
+        g + norm_back(grad_hid_two, normed_two, recip_two, gain_b)
     ).astype(BF)
     wide_ref[:, 3 * WIDTH :] = tn(attended, grad_resid)
     grad_att = nt(grad_resid, proj_ref[...]).astype(BF)
@@ -243,9 +244,8 @@
     gain = jnp.sum(grad_hid_one * normed_one, axis=0, keepdims=True)
     gain_ref[0:1, :] = gain[:, :LANES]
     gain_ref[1:2, : WIDTH - LANES] = gain[:, LANES:]
-    grad_ref[...] = (
-        grad_resid.astype(F32) + norm_back(grad_hid_one, normed_one, recip_one, gain_a)
-    ).astype(BF)
+    grad = grad_resid.astype(F32) + norm_back(grad_hid_one, normed_one, recip_one, gain_a)
+    grad_ref[...] = jnp.concatenate([grad[-level:], grad[:-level]], axis=0).astype(BF)
     lines = {}
     for part, whole in enumerate((wide_ref[...], up, down)):
         for k in range(6):
@@ -370,9 +370,10 @@
 find_bias = kernel(
     bias_kernel,
     "find_bias",
-    [((HEADS, WIN, WIN), F32), ((2, WIDTH), F32), ((4, WIN_LAT), jnp.int32)],
+    [((HEADS, WIN, WIN), F32), ((2, WIDTH), F32), ((4, WIN_LAT), jnp.int32)]
+    + [((WIDTH, 3 * WIDTH), BF), ((WIDTH, WIDTH), BF), ((WIDTH, 4 * WIDTH), BF), ((WIDTH, 4 * WIDTH), BF)],
     REST + [((8, CHUNKS * LANES), jnp.int32)],
-    copies=2,
+    copies=6,
     later=6,
     flops=20_000_000,
 )
@@ -431,7 +432,6 @@
 
 def shifted(pair):
     half_rows, half_cols = pair.shape[2] // 2, pair.shape[3] // 2
-    pair = jnp.roll(pair, -1, axis=1)
     own, east = pair[:, :, half_rows:, half_cols:], pair[:, :, half_rows:, :half_cols]
     south, corner = pair[:, :, :half_rows, half_cols:], pair[:, :, :half_rows, :half_cols]
     corner = lax.ppermute(corner, ALL, routes(-1, -1))
@@ -456,19 +456,19 @@
     own = grad[:, : grad.shape[1] // 2, : grad.shape[2] // 2]
     top = jnp.concatenate([corner, south], axis=2)
     bottom = jnp.concatenate([east, own], axis=2)
-    return jnp.roll(jnp.concatenate([top, bottom], axis=1), 1, axis=0)
+    return jnp.concatenate([top, bottom], axis=1)
 
 
 def body(states, cotangent, region, pos_index, w_qkv, w_proj, w_up, w_down, gains, earth_bias):
     levels, rows, merged = states.shape[1:]
-    weights = (w_qkv, w_proj, w_up, w_down.T)
-    far = [pltpu.with_memory_space_constraint(array, pltpu.HBM) for array in (gains, region.T)]
-    earth, gains, region = find_bias(pos_index, earth_bias.transpose(1, 0, 2), *far, *weights)
+    far = (gains, region.T, w_qkv, w_proj, w_up, w_down.T)
+    far = [pltpu.with_memory_space_constraint(array, pltpu.HBM) for array in far]
+    earth, gains, region, *weights = find_bias(pos_index, earth_bias.transpose(1, 0, 2), *far)
     pair = shifted(jnp.concatenate([states, cotangent], axis=0))
     cells = pair.reshape(2, CELLS, WIDTH)
     core = lax.axis_index("c").astype(jnp.int32).reshape(1)
     grad, send, keep, score = block_grads(
-        region, core, cells[0], cells[1], earth, gains, *weights
+        region, core, cells, earth, gains, *weights
     )
     came = lax.ppermute(send, "c", SWAP)
     grad = grad.reshape(levels, rows, merged)

time: 97.1 us -> 97 us (level)
    ppermute x1, starting transfers between devices: 12.9 us -> 2.62 us  [shifted(): east = lax.ppermute(east, ALL, routes(-1, 0))]
    ppermute x1, starting transfers between devices: 3.48 us -> 13.4 us  [shifted(): corner = lax.ppermute(corner, ALL, routes(-1, -1))]
    all_to_all x1, starting transfers between devices: 5.4 us -> 6.44 us  [body(): line = lax.all_to_all(line, 'far', 0, 0)]
where the time goes in v6:
time: 97 us; the launch traced here: 96.5 us
  starting transfers between devices  43.6 us (45%)
  blocking collectives  30.2 us (31%)
  Pallas kernels  13.7 us (14%)
  waiting for transfers between devices  5.47 us (6%)
  local copies, waits for them, and re-layouts  2.48 us (3%)
    all_to_all x2, blocking collectives, body(): plane = lax.all_to_all(plane, PLANE, 0, 0)  30.2 us
    pallas_call x7, Pallas kernels, call(): pl.pallas_call(function, out_shape=shapes, in_specs=[SMEM] * scalars + [V...  13.7 us
    ppermute x1, starting transfers between devices, shifted(): corner = lax.ppermute(corner, ALL, routes(-1, -1))  13.4 us
    ppermute x1, starting transfers between devices, body(): came = lax.ppermute(plane, 'c', SWAP)  7.12 us
    all_to_all x1, starting transfers between devices, body(): line = lax.all_to_all(line, 'far', 0, 0)  6.44 us
    ppermute x1, starting transfers between devices, sent_back(): east = lax.ppermute(east, ALL, routes(1, 0))  4.52 us
    ppermute x1, starting transfers between devices, sent_back(): corner = lax.ppermute(corner, ALL, routes(1, 1))  3.73 us
    ppermute x1, starting transfers between devices, body(): came = lax.ppermute(send, 'c', SWAP)  3.46 us
  transfers between devices with their start and end apart: 9, of which 4 were waited for; matrix products, arithmetic and copies ran while one was open for 1% of the time, Pallas kernels for 5%

profile of v6, /device:TPU:1, one launch (start us, length us, event | category | flops | bytes accessed | tf_op | source)
XLA Modules:
  0.0 96.5 jit_solution(6100333785373082135)
XLA Ops:
  0.6 1.0 %constant_dynamic-update-slice_fusion.1 = bf16[2,4,6,2304]{3,1,2,0:T(4,128)(2,1)S(1)} fusion(bf16[1,4,6,2304]{3,1,2,0:T(4,128)(2,1)} %param.10), kind=kLoop, calls=%fused_computation.3 | loop fusion | bytes 221184
  1.6 0.1 constant_dynamic-update-slice_fusion
  1.7 0.0 copy-start
  1.7 0.1 fusion
  1.8 13.4 %collective-permute-start.2 = (bf16[2,4,3,1152]{3,1,2,0:T(4,128)(2,1)S(1)}, bf16[2,4,3,1152]{3,1,2,0:T(4,128)(2,1)S(1)}, u32[]{:S(2)}, u32[]{:S(2)}) collective-permute-start(bf16[2,4,3,1152]{3,1,2,0:T(4,128)(2,1)S(1)} %get-tuple-element.56), channel_id=1, source_target_pairs={{0,510},{1,511},{2,496},{3,497},{4,498},{5,499},{6,500},{7,501},{8... | collective-permute-start | bytes 165896 | tf_op jit(solution)/shard_map/ppermute | solution.py:437
  15.2 2.3 %collective-permute-start.1 = (bf16[2,4,3,1152]{3,1,2,0:T(4,128)(2,1)S(1)}, bf16[2,4,3,1152]{3,1,2,0:T(4,128)(2,1)S(1)}, u32[]{:S(2)}, u32[]{:S(2)}) collective-permute-start(bf16[2,4,3,1152]{3,1,2,0:T(4,128)(2,1)S(1)} %get-tuple-element.57), channel_id=1, source_target_pairs={{0,14},{1,15},{2,0},{3,1},{4,2},{5,3},{6,4},{7,5},{8,6},{9,7},{10,... | collective-permute-start | bytes 165896 | tf_op jit(solution)/shard_map/ppermute | solution.py:439
  17.5 2.6 %collective-permute-start = (bf16[2,4,3,1152]{3,1,2,0:T(4,128)(2,1)S(1)}, bf16[2,4,3,1152]{3,1,2,0:T(4,128)(2,1)S(1)}, u32[]{:S(2)}, u32[]{:S(2)}) collective-permute-start(bf16[2,4,3,1152]{3,1,2,0:T(4,128)(2,1)S(1)} %get-tuple-element.58), channel_id=1, source_target_pairs={{0,496},{1,497},{2,498},{3,499},{4,500},{5,501},{6,502},{7,503},{8... | collective-permute-start | bytes 165896 | tf_op jit(solution)/shard_map/ppermute | solution.py:438
  20.2 2.6 %find_bias.1 = (f32[6,144,144]{2,1,0:T(8,128)S(1)}, f32[2,192]{1,0:T(2,128)S(1)}, s32[4,6]{1,0:T(4,128)S(1)}, bf16[192,576]{1,0:T(8,128)(2,1)S(1)}, bf16[192,192...) custom-call(s32[144,144]{1,0:T(8,128)S(1)} %copy-done, f32[6,1,3312]{2,1,0:T(1,128)S(1)} %bitcast.8, ...), custom_call_target="tpu_custom_call" | custom-call | flops 20000000 | bytes 1000000 | tf_op jit(solution)/shard_map/find_bias/pallas_call | solution.py:355
  22.9 0.1 maximum_maximum_fusion
  23.0 0.4 reshape.24.cells_ref
  23.4 6.1 %block_grads.1 = (bf16[288,192]{1,0:T(8,128)(2,1)S(1)}, bf16[1792,128]{1,0:T(8,128)(2,1)S(1)}, bf16[1792,128]{1,0:T(8,128)(2,1)S(1)}, f32[6,144,144]{2,1,0:T(8,128)S(1)}) custom-call(s32[4,6]{1,0:T(4,128)S(1)} %get-tuple-element.24.region_ref, s32[1]{0:T(128)} %bitcast.3.core_ref.refs_0_, bf16[2,288,192]{2,1,0:T(8,128)(2,1)S(1)} %reshape.24.cells_ref, ...), custom_call_target="tpu_custom_call" | custom-call | flops 1000000000 | bytes 4000000 | tf_op jit(solution)/shard_map/block_grads/pallas_call | solution.py:355
  29.5 3.5 %collective-permute-start.6 = (bf16[1792,128]{1,0:T(8,128)(2,1)S(1)}, bf16[1792,128]{1,0:T(8,128)(2,1)S(1)}, u32[]{:S(2)}, u32[]{:S(2)}) collective-permute-start(bf16[1792,128]{1,0:T(8,128)(2,1)S(1)} %get-tuple-element.33), channel_id=1, source_target_pairs={{0,2},{2,0},{1,3},{3,1},{4,6},{6,4},{5,7},{7,5},{8,10},{10,8},{9,1... | collective-permute-start | bytes 1376264 | tf_op jit(solution)/shard_map/ppermute | solution.py:473
  33.0 2.4 %spread_bias.1.table_ref = f32[192,128]{1,0:T(8,128)S(1)} custom-call(s32[144,144]{1,0:T(8,128)S(1)} %copy-done, f32[6,144,144]{2,1,0:T(8,128)S(1)} %get-tuple-element.34.score_ref), custom_call_target="tpu_custom_call" | custom-call | flops 1000000000 | bytes 1000000 | tf_op jit(solution)/shard_map/spread_bias/pallas_call | solution.py:355
  35.5 0.2 first_sum.1
  35.7 16.1 %all_to_all.15.came_ref = bf16[32,64,128]{2,1,0:T(8,128)(2,1)S(1)} all-to-all(bf16[32,64,128]{2,1,0:T(8,128)(2,1)S(1)} %first_sum.1), channel_id=1, replica_groups=mesh['x'=2,'far'=8,'pair'=2,'y'=4,'c'=2,'m'=2] {'x','m','y','pair'}, dimensions={0} | all-to-all | bytes 1048576 | tf_op jit(solution)/shard_map/all_to_all | solution.py:478
  51.8 0.8 second_sum.1
  52.6 6.4 %all-to-all-start.1 = ((bf16[8,80,128]{2,1,0:T(8,128)(2,1)}), bf16[8,80,128]{2,1,0:T(8,128)(2,1)S(1)}, u32[]{:S(2)}, u32[]{:S(2)}) async-start(bf16[8,80,128]{2,1,0:T(8,128)(2,1)} %second_sum.1), calls=%async_computation.1 | async-start | bytes 327680 | tf_op jit(solution)/shard_map/all_to_all | solution.py:480
  59.0 0.2 reshape.25
  59.2 0.1 fusion.1
  59.3 3.7 %collective-permute-start.3 = (bf16[4,3,1152]{2,1,0:T(4,128)(2,1)S(1)}, bf16[4,3,1152]{2,1,0:T(4,128)(2,1)S(1)}, u32[]{:S(2)}, u32[]{:S(2)}) collective-permute-start(bf16[4,3,1152]{2,1,0:T(4,128)(2,1)S(1)} %get-tuple-element.59), channel_id=1, source_target_pairs={{0,18},{1,19},{2,20},{3,21},{4,22},{5,23},{6,24},{7,25},{8,26},{9,... | collective-permute-start | bytes 82952 | tf_op jit(solution)/shard_map/ppermute | solution.py:449
  63.0 4.5 %collective-permute-start.5 = (bf16[4,3,1152]{2,1,0:T(4,128)(2,1)S(1)}, bf16[4,3,1152]{2,1,0:T(4,128)(2,1)S(1)}, u32[]{:S(2)}, u32[]{:S(2)}) collective-permute-start(bf16[4,3,1152]{2,1,0:T(4,128)(2,1)S(1)} %get-tuple-element.61), channel_id=1, source_target_pairs={{0,16},{1,17},{2,18},{3,19},{4,20},{5,21},{6,22},{7,23},{8,24},{9,... | collective-permute-start | bytes 82952 | tf_op jit(solution)/shard_map/ppermute | solution.py:450
  67.5 0.0 collective-permute-start.4
  67.6 2.7 %collective-permute-done.3.refs_0_ = bf16[4,3,1152]{2,1,0:T(4,128)(2,1)S(1)} collective-permute-done((bf16[4,3,1152]{2,1,0:T(4,128)(2,1)S(1)}, bf16[4,3,1152]{2,1,0:T(4,128)(2,1)S(1)}, u32[]{:S(2)}, u32[]{:S(2)}) %collective-permute-start.3) | collective-permute-done | bytes 27680 | tf_op jit(solution)/shard_map/ppermute | solution.py:449
  70.3 0.6 collective-permute-done.5.refs_1_
  70.9 1.4 %all-to-all-done.1.came_ref = bf16[8,80,128]{2,1,0:T(8,128)(2,1)S(1)} async-done(((bf16[8,80,128]{2,1,0:T(8,128)(2,1)}), bf16[8,80,128]{2,1,0:T(8,128)(2,1)S(1)}, u32[]{:S(2)}, u32[]{:S(2)}) %all-to-all-start.1) | async-done | bytes 163872 | tf_op jit(solution)/shard_map/all_to_all | solution.py:480
  72.3 0.1 fan.1
  72.4 14.0 %all_to_all.16.refs_1_ = bf16[32,64,128]{2,1,0:T(8,128)(2,1)S(1)} all-to-all(bf16[32,64,128]{2,1,0:T(8,128)(2,1)S(1)} %fan.1), channel_id=1, replica_groups=mesh['x'=2,'far'=8,'pair'=2,'y'=4,'c'=2,'m'=2] {'x','m','y','pair'}, dimensions={0} | all-to-all | bytes 1048576 | tf_op jit(solution)/shard_map/all_to_all | solution.py:482
  86.4 7.1 %collective-permute-start.7 = (bf16[32,64,128]{2,1,0:T(8,128)(2,1)S(1)}, bf16[32,64,128]{2,1,0:T(8,128)(2,1)S(1)}, u32[]{:S(2)}, u32[]{:S(2)}) collective-permute-start(bf16[32,64,128]{2,1,0:T(8,128)(2,1)S(1)} %all_to_all.16.refs_1_), channel_id=1, source_target_pairs={{0,2},{2,0},{1,3},{3,1},{4,6},{6,4},{5,7},{7,5},{8,10},{10,8},{9,1... | collective-permute-start | bytes 1572872 | tf_op jit(solution)/shard_map/ppermute | solution.py:483
  93.5 0.1 maximum_bitcast_fusion
  93.6 0.7 copy.20
  94.3 0.7 collective-permute-done.7.refs_2_
  95.0 1.5 %finish.1 = (f32[192,576]{1,0:T(8,128)}, f32[192,192]{1,0:T(8,128)}, f32[192,768]{1,0:T(8,128)}, f32[192,768]{1,0:T(8,128)}, f32[2,192]{1,0:T(2,128)}, /*index=5*/f32[6,1,3312]{2,1,0:T(1,128)}) custom-call(s32[1]{0:T(128)} %bitcast.3.core_ref.refs_0_, bf16[32,64,128]{2,1,0:T(8,128)(2,1)S(1)} %all_to_all.16.refs_1_, ...), custom_call_target="tpu_custom_call" | custom-call | flops 1000000 | bytes 1000000 | tf_op jit(solution)/shard_map/finish/pallas_call | solution.py:355
  (11 shorter events, 0.1 us)
Async XLA Ops:
  0.6 1.0 %copy-start.2 = (bf16[1,4,6,2304]{3,1,2,0:T(4,128)(2,1)S(1)}, bf16[1,4,6,2304]{3,1,2,0:T(4,128)(2,1)}, u32[]{:S(2)}) copy-start(bf16[1,4,6,2304]{3,1,2,0:T(4,128)(2,1)} %param.11) | copy-start | bytes 331780
  1.7 18.5 %copy-start = (s32[144,144]{1,0:T(8,128)S(1)}, s32[144,144]{1,0:T(8,128)}, u32[]{:S(2)}) copy-start(s32[144,144]{1,0:T(8,128)} %pos_ref.3) | copy-start | bytes 248836
  1.7 18.5 %copy-start.1 = (f32[1,6,3312]{2,0,1:T(1,128)S(1)}, f32[1,6,3312]{2,0,1:T(1,128)}, u32[]{:S(2)}) copy-start(f32[1,6,3312]{2,0,1:T(1,128)} %param.19) | copy-start | bytes 238468
  1.8 21.0 %collective-permute-start.2 = (bf16[2,4,3,1152]{3,1,2,0:T(4,128)(2,1)S(1)}, bf16[2,4,3,1152]{3,1,2,0:T(4,128)(2,1)S(1)}, u32[]{:S(2)}, u32[]{:S(2)}) collective-permute-start(bf16[2,4,3,1152]{3,1,2,0:T(4,128)(2,1)S(1)} %get-tuple-element.56), channel_id=1, source_target_pairs={{0,510},{1,511},{2,496},{3,497},{4,498},{5,499},{6,500},{7,501},{8... | collective-permute-start | bytes 165896 | tf_op jit(solution)/shard_map/ppermute | solution.py:437
  15.2 7.6 %collective-permute-start.1 = (bf16[2,4,3,1152]{3,1,2,0:T(4,128)(2,1)S(1)}, bf16[2,4,3,1152]{3,1,2,0:T(4,128)(2,1)S(1)}, u32[]{:S(2)}, u32[]{:S(2)}) collective-permute-start(bf16[2,4,3,1152]{3,1,2,0:T(4,128)(2,1)S(1)} %get-tuple-element.57), channel_id=1, source_target_pairs={{0,14},{1,15},{2,0},{3,1},{4,2},{5,3},{6,4},{7,5},{8,6},{9,7},{10,... | collective-permute-start | bytes 165896 | tf_op jit(solution)/shard_map/ppermute | solution.py:439
  17.5 5.3 %collective-permute-start = (bf16[2,4,3,1152]{3,1,2,0:T(4,128)(2,1)S(1)}, bf16[2,4,3,1152]{3,1,2,0:T(4,128)(2,1)S(1)}, u32[]{:S(2)}, u32[]{:S(2)}) collective-permute-start(bf16[2,4,3,1152]{3,1,2,0:T(4,128)(2,1)S(1)} %get-tuple-element.58), channel_id=1, source_target_pairs={{0,496},{1,497},{2,498},{3,499},{4,500},{5,501},{6,502},{7,503},{8... | collective-permute-start | bytes 165896 | tf_op jit(solution)/shard_map/ppermute | solution.py:438
  29.5 5.9 %collective-permute-start.6 = (bf16[1792,128]{1,0:T(8,128)(2,1)S(1)}, bf16[1792,128]{1,0:T(8,128)(2,1)S(1)}, u32[]{:S(2)}, u32[]{:S(2)}) collective-permute-start(bf16[1792,128]{1,0:T(8,128)(2,1)S(1)} %get-tuple-element.33), channel_id=1, source_target_pairs={{0,2},{2,0},{1,3},{3,1},{4,6},{6,4},{5,7},{7,5},{8,10},{10,8},{9,1... | collective-permute-start | bytes 1376264 | tf_op jit(solution)/shard_map/ppermute | solution.py:473
  52.6 19.7 %all-to-all-start.1 = ((bf16[8,80,128]{2,1,0:T(8,128)(2,1)}), bf16[8,80,128]{2,1,0:T(8,128)(2,1)S(1)}, u32[]{:S(2)}, u32[]{:S(2)}) async-start(bf16[8,80,128]{2,1,0:T(8,128)(2,1)} %second_sum.1), calls=%async_computation.1 | async-start | bytes 327680 | tf_op jit(solution)/shard_map/all_to_all | solution.py:480
  59.3 11.0 %collective-permute-start.3 = (bf16[4,3,1152]{2,1,0:T(4,128)(2,1)S(1)}, bf16[4,3,1152]{2,1,0:T(4,128)(2,1)S(1)}, u32[]{:S(2)}, u32[]{:S(2)}) collective-permute-start(bf16[4,3,1152]{2,1,0:T(4,128)(2,1)S(1)} %get-tuple-element.59), channel_id=1, source_target_pairs={{0,18},{1,19},{2,20},{3,21},{4,22},{5,23},{6,24},{7,25},{8,26},{9,... | collective-permute-start | bytes 82952 | tf_op jit(solution)/shard_map/ppermute | solution.py:449
  63.0 7.9 %collective-permute-start.5 = (bf16[4,3,1152]{2,1,0:T(4,128)(2,1)S(1)}, bf16[4,3,1152]{2,1,0:T(4,128)(2,1)S(1)}, u32[]{:S(2)}, u32[]{:S(2)}) collective-permute-start(bf16[4,3,1152]{2,1,0:T(4,128)(2,1)S(1)} %get-tuple-element.61), channel_id=1, source_target_pairs={{0,16},{1,17},{2,18},{3,19},{4,20},{5,21},{6,22},{7,23},{8,24},{9,... | collective-permute-start | bytes 82952 | tf_op jit(solution)/shard_map/ppermute | solution.py:450
  67.5 3.3 %collective-permute-start.4 = (bf16[4,3,1152]{2,1,0:T(4,128)(2,1)S(1)}, bf16[4,3,1152]{2,1,0:T(4,128)(2,1)S(1)}, u32[]{:S(2)}, u32[]{:S(2)}) collective-permute-start(bf16[4,3,1152]{2,1,0:T(4,128)(2,1)S(1)} %get-tuple-element.62), channel_id=1, source_target_pairs={{0,2},{1,3},{2,4},{3,5},{4,6},{5,7},{6,8},{7,9},{8,10},{9,11},{10,... | collective-permute-start | bytes 82952 | tf_op jit(solution)/shard_map/ppermute | solution.py:451
  86.4 8.6 %collective-permute-start.7 = (bf16[32,64,128]{2,1,0:T(8,128)(2,1)S(1)}, bf16[32,64,128]{2,1,0:T(8,128)(2,1)S(1)}, u32[]{:S(2)}, u32[]{:S(2)}) collective-permute-start(bf16[32,64,128]{2,1,0:T(8,128)(2,1)S(1)} %all_to_all.16.refs_1_), channel_id=1, source_target_pairs={{0,2},{2,0},{1,3},{3,1},{4,6},{6,4},{5,7},{7,5},{8,10},{10,8},{9,1... | collective-permute-start | bytes 1572872 | tf_op jit(solution)/shard_map/ppermute | solution.py:483

commit v7 on v6

--- a/solution.py
+++ b/solution.py
@@ -63,6 +63,18 @@
     cumulative = 0.5 * (1.0 + lax.erf(upward * 0.7071067811865476))
     density = jnp.exp(-0.5 * upward * upward) * 0.3989422804014327
     return (upward * cumulative, cumulative + upward * density)
+
+
+def cut_kernel(states_far, cot_far, own_ref, east_ref, south_ref, corner_ref, arrived):
+    copies = []
+    for n, far in enumerate((states_far, cot_far)):
+        rows, cols = far.shape[0] // 2, far.shape[2] // 2
+        for k, ref in enumerate((corner_ref, south_ref, east_ref, own_ref)):
+            at = pl.ds(k // 2 * rows, rows), slice(None), pl.ds(k % 2 * cols, cols)
+            copies.append(pltpu.make_async_copy(far.at[at], ref.at[n], arrived.at[4 * n + k]))
+            copies[-1].start()
+    for copy in copies:
+        copy.wait()
 
 
 def bias_kernel(pos_ref, table_ref, *refs):
@@ -366,6 +378,8 @@
     return call
 
 
+QUARTER = ((2, WIN_LAT // 2, 4, WIN_LON * WIDTH // 2), BF)
+cut = kernel(cut_kernel, "cut", [QUARTER] * 4, copies=8, later=2)
 REST = [((WIN - LANES, 2 * LANES), jnp.int32), ((HEADS, WIN - LANES, 2 * LANES), F32)]
 find_bias = kernel(
     bias_kernel,
@@ -430,16 +444,13 @@
     ]
 
 
-def shifted(pair):
-    half_rows, half_cols = pair.shape[2] // 2, pair.shape[3] // 2
-    own, east = pair[:, :, half_rows:, half_cols:], pair[:, :, half_rows:, :half_cols]
-    south, corner = pair[:, :, :half_rows, half_cols:], pair[:, :, :half_rows, :half_cols]
+def shifted(own, east, south, corner):
     corner = lax.ppermute(corner, ALL, routes(-1, -1))
     east = lax.ppermute(east, ALL, routes(-1, 0))
     south = lax.ppermute(south, ALL, routes(0, -1))
     top = jnp.concatenate([own, east], axis=3)
     bottom = jnp.concatenate([south, corner], axis=3)
-    return jnp.concatenate([top, bottom], axis=2)
+    return jnp.concatenate([top, bottom], axis=1).transpose(0, 2, 1, 3).reshape(2, CELLS, WIDTH)
 
 
 def sent_back(grad):
@@ -461,11 +472,12 @@
 
 def body(states, cotangent, region, pos_index, w_qkv, w_proj, w_up, w_down, gains, earth_bias):
     levels, rows, merged = states.shape[1:]
+    turned = [array[0].transpose(1, 0, 2) for array in (states, cotangent)]
+    quarters = cut(*[pltpu.with_memory_space_constraint(array, pltpu.HBM) for array in turned])
     far = (gains, region.T, w_qkv, w_proj, w_up, w_down.T)
     far = [pltpu.with_memory_space_constraint(array, pltpu.HBM) for array in far]
     earth, gains, region, *weights = find_bias(pos_index, earth_bias.transpose(1, 0, 2), *far)
-    pair = shifted(jnp.concatenate([states, cotangent], axis=0))
-    cells = pair.reshape(2, CELLS, WIDTH)
+    cells = shifted(*quarters)
     core = lax.axis_index("c").astype(jnp.int32).reshape(1)
     grad, send, keep, score = block_grads(
         region, core, cells, earth, gains, *weights

time: 97 us -> 97.3 us (level)
  local copies, waits for them, and re-layouts: 2.48 us -> 1.37 us
  Pallas kernels: 13.7 us -> 14.7 us
    ppermute x1, starting transfers between devices: 2.62 us -> 12.9 us  [shifted(): east = lax.ppermute(east, ALL, routes(-1, 0))]
    ppermute x1, starting transfers between devices: 13.4 us -> 4.68 us  [shifted(): corner = lax.ppermute(corner, ALL, routes(-1, -1))]
    ppermute x1, starting transfers between devices: 2.3 us -> 0.97 us  [shifted(): south = lax.ppermute(south, ALL, routes(0, -1))]
    unnamed x8 -> x5, local copies, waits for them, and re-layouts: 1.68 us -> 0.7 us
    pallas_call x7 -> x8, Pallas kernels: 13.7 us -> 14.7 us  [call(): pl.pallas_call(function, out_shape=shapes, in_specs=[SMEM] * scalars + [V...]
where the time goes in v7:
time: 97.3 us; the launch traced here: 96.8 us
  starting transfers between devices  43.8 us (45%)
  blocking collectives  30 us (31%)
  Pallas kernels  14.7 us (15%)
  waiting for transfers between devices  5.92 us (6%)
  local copies, waits for them, and re-layouts  1.37 us (1%)
    all_to_all x2, blocking collectives, body(): plane = lax.all_to_all(plane, PLANE, 0, 0)  30 us
    pallas_call x8, Pallas kernels, call(): pl.pallas_call(function, out_shape=shapes, in_specs=[SMEM] * scalars + [V...  14.7 us
    ppermute x1, starting transfers between devices, shifted(): east = lax.ppermute(east, ALL, routes(-1, 0))  12.9 us
    ppermute x1, starting transfers between devices, body(): came = lax.ppermute(plane, 'c', SWAP)  7.27 us
    all_to_all x1, starting transfers between devices, body(): line = lax.all_to_all(line, 'far', 0, 0)  6.47 us
    ppermute x1, starting transfers between devices, shifted(): corner = lax.ppermute(corner, ALL, routes(-1, -1))  4.68 us
    ppermute x1, starting transfers between devices, sent_back(): east = lax.ppermute(east, ALL, routes(1, 0))  4.52 us
    ppermute x1, starting transfers between devices, sent_back(): corner = lax.ppermute(corner, ALL, routes(1, 1))  4.28 us
  transfers between devices with their start and end apart: 9, of which 4 were waited for; matrix products, arithmetic and copies ran while one was open for 1% of the time, Pallas kernels for 5%

profile of v7, /device:TPU:1, one launch (start us, length us, event | category | flops | bytes accessed | tf_op | source)
XLA Modules:
  0.0 96.8 jit_solution(12256327992544687194)
XLA Ops:
  0.7 1.0 cut.1
  1.6 12.9 %collective-permute-start = (bf16[2,3,4,1152]{3,2,1,0:T(4,128)(2,1)S(1)}, bf16[2,3,4,1152]{3,2,1,0:T(4,128)(2,1)S(1)}, u32[]{:S(2)}, u32[]{:S(2)}) collective-permute-start(bf16[2,3,4,1152]{3,2,1,0:T(4,128)(2,1)S(1)} %get-tuple-element.30), channel_id=1, source_target_pairs={{0,496},{1,497},{2,498},{3,499},{4,500},{5,501},{6,502},{7,503},{8... | collective-permute-start | bytes 165896 | tf_op jit(solution)/shard_map/ppermute | solution.py:449
  14.5 1.0 collective-permute-start.1
  15.5 4.7 %collective-permute-start.2 = (bf16[2,3,4,1152]{3,2,1,0:T(4,128)(2,1)S(1)}, bf16[2,3,4,1152]{3,2,1,0:T(4,128)(2,1)S(1)}, u32[]{:S(2)}, u32[]{:S(2)}) collective-permute-start(bf16[2,3,4,1152]{3,2,1,0:T(4,128)(2,1)S(1)} %get-tuple-element.32), channel_id=1, source_target_pairs={{0,510},{1,511},{2,496},{3,497},{4,498},{5,499},{6,500},{7,501},{8... | collective-permute-start | bytes 165896 | tf_op jit(solution)/shard_map/ppermute | solution.py:448
  20.2 2.6 %find_bias.1 = (f32[6,144,144]{2,1,0:T(8,128)S(1)}, f32[2,192]{1,0:T(2,128)S(1)}, s32[4,6]{1,0:T(4,128)S(1)}, bf16[192,576]{1,0:T(8,128)(2,1)S(1)}, bf16[192,192...) custom-call(s32[144,144]{1,0:T(8,128)S(1)} %copy-done, f32[6,1,3312]{2,1,0:T(1,128)S(1)} %bitcast.16, ...), custom_call_target="tpu_custom_call" | custom-call | flops 20000000 | bytes 1000000 | tf_op jit(solution)/shard_map/find_bias/pallas_call | solution.py:367
  22.8 0.0 collective-permute-done
  22.9 0.0 collective-permute-done.2
  22.9 0.1 maximum_bitcast_fusion
  23.0 0.4 reshape.24.cells_ref
  23.4 6.1 %block_grads.1 = (bf16[288,192]{1,0:T(8,128)(2,1)S(1)}, bf16[1792,128]{1,0:T(8,128)(2,1)S(1)}, bf16[1792,128]{1,0:T(8,128)(2,1)S(1)}, f32[6,144,144]{2,1,0:T(8,128)S(1)}) custom-call(s32[4,6]{1,0:T(4,128)S(1)} %get-tuple-element.28.region_ref, s32[1]{0:T(128)} %bitcast.3.core_ref.refs_0_, bf16[2,288,192]{2,1,0:T(8,128)(2,1)S(1)} %reshape.24.cells_ref, ...), custom_call_target="tpu_custom_call" | custom-call | flops 1000000000 | bytes 4000000 | tf_op jit(solution)/shard_map/block_grads/pallas_call | solution.py:367
  29.5 2.7 %collective-permute-start.6 = (bf16[1792,128]{1,0:T(8,128)(2,1)S(1)}, bf16[1792,128]{1,0:T(8,128)(2,1)S(1)}, u32[]{:S(2)}, u32[]{:S(2)}) collective-permute-start(bf16[1792,128]{1,0:T(8,128)(2,1)S(1)} %get-tuple-element.41), channel_id=1, source_target_pairs={{0,2},{2,0},{1,3},{3,1},{4,6},{6,4},{5,7},{7,5},{8,10},{10,8},{9,1... | collective-permute-start | bytes 1376264 | tf_op jit(solution)/shard_map/ppermute | solution.py:485
  32.2 2.4 %spread_bias.1.table_ref = f32[192,128]{1,0:T(8,128)S(1)} custom-call(s32[144,144]{1,0:T(8,128)S(1)} %copy-done, f32[6,144,144]{2,1,0:T(8,128)S(1)} %get-tuple-element.42.score_ref), custom_call_target="tpu_custom_call" | custom-call | flops 1000000000 | bytes 1000000 | tf_op jit(solution)/shard_map/spread_bias/pallas_call | solution.py:367
  34.7 0.0 collective-permute-done.6.came_ref
  34.7 0.2 first_sum.1
  34.9 17.2 %all_to_all.15.came_ref = bf16[32,64,128]{2,1,0:T(8,128)(2,1)S(1)} all-to-all(bf16[32,64,128]{2,1,0:T(8,128)(2,1)S(1)} %first_sum.1), channel_id=1, replica_groups=mesh['x'=2,'far'=8,'pair'=2,'y'=4,'c'=2,'m'=2] {'x','m','y','pair'}, dimensions={0} | all-to-all | bytes 1048576 | tf_op jit(solution)/shard_map/all_to_all | solution.py:490
  52.1 0.8 second_sum.1
  52.9 6.5 %all-to-all-start.1 = ((bf16[8,80,128]{2,1,0:T(8,128)(2,1)}), bf16[8,80,128]{2,1,0:T(8,128)(2,1)S(1)}, u32[]{:S(2)}, u32[]{:S(2)}) async-start(bf16[8,80,128]{2,1,0:T(8,128)(2,1)} %second_sum.1), calls=%async_computation.1 | async-start | bytes 327680 | tf_op jit(solution)/shard_map/all_to_all | solution.py:492
  59.4 0.2 reshape.25
  59.6 0.1 fusion
  59.6 4.3 %collective-permute-start.3 = (bf16[4,3,1152]{2,1,0:T(4,128)(2,1)S(1)}, bf16[4,3,1152]{2,1,0:T(4,128)(2,1)S(1)}, u32[]{:S(2)}, u32[]{:S(2)}) collective-permute-start(bf16[4,3,1152]{2,1,0:T(4,128)(2,1)S(1)} %get-tuple-element.63), channel_id=1, source_target_pairs={{0,18},{1,19},{2,20},{3,21},{4,22},{5,23},{6,24},{7,25},{8,26},{9,... | collective-permute-start | bytes 82952 | tf_op jit(solution)/shard_map/ppermute | solution.py:460
  63.9 4.5 %collective-permute-start.5 = (bf16[4,3,1152]{2,1,0:T(4,128)(2,1)S(1)}, bf16[4,3,1152]{2,1,0:T(4,128)(2,1)S(1)}, u32[]{:S(2)}, u32[]{:S(2)}) collective-permute-start(bf16[4,3,1152]{2,1,0:T(4,128)(2,1)S(1)} %get-tuple-element.65), channel_id=1, source_target_pairs={{0,16},{1,17},{2,18},{3,19},{4,20},{5,21},{6,22},{7,23},{8,24},{9,... | collective-permute-start | bytes 82952 | tf_op jit(solution)/shard_map/ppermute | solution.py:461
  68.5 0.0 collective-permute-start.4
  68.5 1.8 %collective-permute-done.3.refs_0_ = bf16[4,3,1152]{2,1,0:T(4,128)(2,1)S(1)} collective-permute-done((bf16[4,3,1152]{2,1,0:T(4,128)(2,1)S(1)}, bf16[4,3,1152]{2,1,0:T(4,128)(2,1)S(1)}, u32[]{:S(2)}, u32[]{:S(2)}) %collective-permute-start.3) | collective-permute-done | bytes 27680 | tf_op jit(solution)/shard_map/ppermute | solution.py:460
  70.3 1.0 %collective-permute-done.5.refs_1_ = bf16[4,3,1152]{2,1,0:T(4,128)(2,1)S(1)} collective-permute-done((bf16[4,3,1152]{2,1,0:T(4,128)(2,1)S(1)}, bf16[4,3,1152]{2,1,0:T(4,128)(2,1)S(1)}, u32[]{:S(2)}, u32[]{:S(2)}) %collective-permute-start.5) | collective-permute-done | bytes 27680 | tf_op jit(solution)/shard_map/ppermute | solution.py:461
  71.4 2.3 %all-to-all-done.1.came_ref = bf16[8,80,128]{2,1,0:T(8,128)(2,1)S(1)} async-done(((bf16[8,80,128]{2,1,0:T(8,128)(2,1)}), bf16[8,80,128]{2,1,0:T(8,128)(2,1)S(1)}, u32[]{:S(2)}, u32[]{:S(2)}) %all-to-all-start.1) | async-done | bytes 163872 | tf_op jit(solution)/shard_map/all_to_all | solution.py:492
  73.7 0.1 fan.1
  73.7 12.8 %all_to_all.16.refs_1_ = bf16[32,64,128]{2,1,0:T(8,128)(2,1)S(1)} all-to-all(bf16[32,64,128]{2,1,0:T(8,128)(2,1)S(1)} %fan.1), channel_id=1, replica_groups=mesh['x'=2,'far'=8,'pair'=2,'y'=4,'c'=2,'m'=2] {'x','m','y','pair'}, dimensions={0} | all-to-all | bytes 1048576 | tf_op jit(solution)/shard_map/all_to_all | solution.py:494
  86.6 7.3 %collective-permute-start.7 = (bf16[32,64,128]{2,1,0:T(8,128)(2,1)S(1)}, bf16[32,64,128]{2,1,0:T(8,128)(2,1)S(1)}, u32[]{:S(2)}, u32[]{:S(2)}) collective-permute-start(bf16[32,64,128]{2,1,0:T(8,128)(2,1)S(1)} %all_to_all.16.refs_1_), channel_id=1, source_target_pairs={{0,2},{2,0},{1,3},{3,1},{4,6},{6,4},{5,7},{7,5},{8,10},{10,8},{9,1... | collective-permute-start | bytes 1572872 | tf_op jit(solution)/shard_map/ppermute | solution.py:495
  93.8 0.1 maximum_bitcast_fusion.1
  93.9 0.7 copy.20
  94.6 0.7 collective-permute-done.7.refs_2_
  95.4 1.5 %finish.1 = (f32[192,576]{1,0:T(8,128)}, f32[192,192]{1,0:T(8,128)}, f32[192,768]{1,0:T(8,128)}, f32[192,768]{1,0:T(8,128)}, f32[2,192]{1,0:T(2,128)}, /*index=5*/f32[6,1,3312]{2,1,0:T(1,128)}) custom-call(s32[1]{0:T(128)} %bitcast.3.core_ref.refs_0_, bf16[32,64,128]{2,1,0:T(8,128)(2,1)S(1)} %all_to_all.16.refs_1_, ...), custom_call_target="tpu_custom_call" | custom-call | flops 1000000 | bytes 1000000 | tf_op jit(solution)/shard_map/finish/pallas_call | solution.py:367
  (7 shorter events, 0.0 us)
Async XLA Ops:
  0.6 19.5 %copy-start = (s32[144,144]{1,0:T(8,128)S(1)}, s32[144,144]{1,0:T(8,128)}, u32[]{:S(2)}) copy-start(s32[144,144]{1,0:T(8,128)} %pos_ref.3) | copy-start | bytes 248836
  0.6 19.5 %copy-start.1 = (f32[1,6,3312]{2,0,1:T(1,128)S(1)}, f32[1,6,3312]{2,0,1:T(1,128)}, u32[]{:S(2)}) copy-start(f32[1,6,3312]{2,0,1:T(1,128)} %param.19) | copy-start | bytes 238468
  1.6 21.2 %collective-permute-start = (bf16[2,3,4,1152]{3,2,1,0:T(4,128)(2,1)S(1)}, bf16[2,3,4,1152]{3,2,1,0:T(4,128)(2,1)S(1)}, u32[]{:S(2)}, u32[]{:S(2)}) collective-permute-start(bf16[2,3,4,1152]{3,2,1,0:T(4,128)(2,1)S(1)} %get-tuple-element.30), channel_id=1, source_target_pairs={{0,496},{1,497},{2,498},{3,499},{4,500},{5,501},{6,502},{7,503},{8... | collective-permute-start | bytes 165896 | tf_op jit(solution)/shard_map/ppermute | solution.py:449
  14.5 8.3 %collective-permute-start.1 = (bf16[2,3,4,1152]{3,2,1,0:T(4,128)(2,1)S(1)}, bf16[2,3,4,1152]{3,2,1,0:T(4,128)(2,1)S(1)}, u32[]{:S(2)}, u32[]{:S(2)}) collective-permute-start(bf16[2,3,4,1152]{3,2,1,0:T(4,128)(2,1)S(1)} %get-tuple-element.31), channel_id=1, source_target_pairs={{0,14},{1,15},{2,0},{3,1},{4,2},{5,3},{6,4},{7,5},{8,6},{9,7},{10,... | collective-permute-start | bytes 165896 | tf_op jit(solution)/shard_map/ppermute | solution.py:450
  15.5 7.4 %collective-permute-start.2 = (bf16[2,3,4,1152]{3,2,1,0:T(4,128)(2,1)S(1)}, bf16[2,3,4,1152]{3,2,1,0:T(4,128)(2,1)S(1)}, u32[]{:S(2)}, u32[]{:S(2)}) collective-permute-start(bf16[2,3,4,1152]{3,2,1,0:T(4,128)(2,1)S(1)} %get-tuple-element.32), channel_id=1, source_target_pairs={{0,510},{1,511},{2,496},{3,497},{4,498},{5,499},{6,500},{7,501},{8... | collective-permute-start | bytes 165896 | tf_op jit(solution)/shard_map/ppermute | solution.py:448
  29.5 5.1 %collective-permute-start.6 = (bf16[1792,128]{1,0:T(8,128)(2,1)S(1)}, bf16[1792,128]{1,0:T(8,128)(2,1)S(1)}, u32[]{:S(2)}, u32[]{:S(2)}) collective-permute-start(bf16[1792,128]{1,0:T(8,128)(2,1)S(1)} %get-tuple-element.41), channel_id=1, source_target_pairs={{0,2},{2,0},{1,3},{3,1},{4,6},{6,4},{5,7},{7,5},{8,10},{10,8},{9,1... | collective-permute-start | bytes 1376264 | tf_op jit(solution)/shard_map/ppermute | solution.py:485
  52.9 20.7 %all-to-all-start.1 = ((bf16[8,80,128]{2,1,0:T(8,128)(2,1)}), bf16[8,80,128]{2,1,0:T(8,128)(2,1)S(1)}, u32[]{:S(2)}, u32[]{:S(2)}) async-start(bf16[8,80,128]{2,1,0:T(8,128)(2,1)} %second_sum.1), calls=%async_computation.1 | async-start | bytes 327680 | tf_op jit(solution)/shard_map/all_to_all | solution.py:492
  59.6 10.7 %collective-permute-start.3 = (bf16[4,3,1152]{2,1,0:T(4,128)(2,1)S(1)}, bf16[4,3,1152]{2,1,0:T(4,128)(2,1)S(1)}, u32[]{:S(2)}, u32[]{:S(2)}) collective-permute-start(bf16[4,3,1152]{2,1,0:T(4,128)(2,1)S(1)} %get-tuple-element.63), channel_id=1, source_target_pairs={{0,18},{1,19},{2,20},{3,21},{4,22},{5,23},{6,24},{7,25},{8,26},{9,... | collective-permute-start | bytes 82952 | tf_op jit(solution)/shard_map/ppermute | solution.py:460
  63.9 7.4 %collective-permute-start.5 = (bf16[4,3,1152]{2,1,0:T(4,128)(2,1)S(1)}, bf16[4,3,1152]{2,1,0:T(4,128)(2,1)S(1)}, u32[]{:S(2)}, u32[]{:S(2)}) collective-permute-start(bf16[4,3,1152]{2,1,0:T(4,128)(2,1)S(1)} %get-tuple-element.65), channel_id=1, source_target_pairs={{0,16},{1,17},{2,18},{3,19},{4,20},{5,21},{6,22},{7,23},{8,24},{9,... | collective-permute-start | bytes 82952 | tf_op jit(solution)/shard_map/ppermute | solution.py:461
  68.5 2.9 %collective-permute-start.4 = (bf16[4,3,1152]{2,1,0:T(4,128)(2,1)S(1)}, bf16[4,3,1152]{2,1,0:T(4,128)(2,1)S(1)}, u32[]{:S(2)}, u32[]{:S(2)}) collective-permute-start(bf16[4,3,1152]{2,1,0:T(4,128)(2,1)S(1)} %get-tuple-element.66), channel_id=1, source_target_pairs={{0,2},{1,3},{2,4},{3,5},{4,6},{5,7},{6,8},{7,9},{8,10},{9,11},{10,... | collective-permute-start | bytes 82952 | tf_op jit(solution)/shard_map/ppermute | solution.py:462
  86.6 8.8 %collective-permute-start.7 = (bf16[32,64,128]{2,1,0:T(8,128)(2,1)S(1)}, bf16[32,64,128]{2,1,0:T(8,128)(2,1)S(1)}, u32[]{:S(2)}, u32[]{:S(2)}) collective-permute-start(bf16[32,64,128]{2,1,0:T(8,128)(2,1)S(1)} %all_to_all.16.refs_1_), channel_id=1, source_target_pairs={{0,2},{2,0},{1,3},{3,1},{4,6},{6,4},{5,7},{7,5},{8,10},{10,8},{9,1... | collective-permute-start | bytes 1572872 | tf_op jit(solution)/shard_map/ppermute | solution.py:495
